TPU v7x, 32 devices: a whole 2x2x4 slice. The times are simulated.
32 devices in a mesh: section: 2 (over core), dp: 8 (over z, x), tensor: 2 (over y).
Axes of the slice: x: 2, y: 2, z: 4, core: 2. Of those that a mesh axis runs over, the one named last changes fastest.
Arguments:
- x_input: bfloat16 [2, 8192, 768], P(None, ('dp', 'tensor')), may hold values from -6 to 6
- teacher: float32 [2, 8192, 768], P(None, ('dp', 'tensor')), may hold values from -6 to 6
- segment_ids: int32 [2, 8, 1024], P(None, 'dp'), may hold values from 0 to 2, as said below
- valid_len: int32 [2, 8], replicated, may hold values from 256 to 1024
- norm_gain: bfloat16 [2, 768], P('section', 'dp'), may hold values from 0.5 to 1.5
- w_zx: bfloat16 [2, 768, 2, 1536], P('section', 'dp', None, 'tensor'), may hold values from -0.21875 to 0.21875
- w_bc: bfloat16 [2, 768, 256], P('section', 'dp'), may hold values from -0.21875 to 0.21875
- w_dt: bfloat16 [2, 768, 24], P('section', 'dp', 'tensor'), may hold values from -0.21875 to 0.21875
- conv_x: bfloat16 [2, 5, 1536], P('section', None, 'tensor'), may hold values from -3 to 3
- conv_bc: bfloat16 [2, 5, 256], P('section'), may hold values from -3 to 3
- dt_bias: float32 [2, 24], P('section'), may hold values from -4.5 to -1.5
- a_log: float32 [2, 24], P('section'), may hold values from -4 to 2.5
- d_skip: float32 [2, 24], P('section'), may hold values from 0.5 to 1.5
- gnorm_gain: bfloat16 [2, 1536], P('section', 'tensor'), may hold values from 0.5 to 1.5
- w_out: bfloat16 [2, 1536, 768], P('section', 'tensor', 'dp'), may hold values from -0.15625 to 0.15625
Outputs:
- layer_outputs: bfloat16 [2, 2, 8192, 768], P('section', None, ('dp', 'tensor'))
- boundary_grads: float32 [2, 2, 8192, 768], P('section', None, ('dp', 'tensor'))
- grad_norm_gain: float32 [2, 768], P('section', 'dp')
- grad_w_zx: float32 [2, 768, 2, 1536], P('section', 'dp', None, 'tensor')
- grad_w_bc: float32 [2, 768, 256], P('section', 'dp')
- grad_w_dt: float32 [2, 768, 24], P('section', 'dp', 'tensor')
- grad_conv_x: float32 [2, 5, 1536], P('section', None, 'tensor')
- grad_conv_bc: float32 [2, 5, 256], P('section')
- grad_dt_bias: float32 [2, 24], P('section', 'tensor')
- grad_a_log: float32 [2, 24], P('section', 'tensor')
- grad_d_skip: float32 [2, 24], P('section', 'tensor')
- grad_gnorm_gain: float32 [2, 1536], P('section', 'tensor')
- grad_w_out: float32 [2, 1536, 768], P('section', 'tensor', 'dp')
Inputs may be any that keep to these rules, and one draw needn't show every extreme that they name: `segment_ids`: within each sequence the ids start at 0 at the first token, never fall, and rise by at most one from a token to the next; the last document is cut at the sequence's end.
All inputs are finite; a program needn't handle non-finite values.
Results may differ from a plain program's by a relative error of at most 0.019.
Values may be sent and summed in bfloat16 or wider, within the bound.
No kernel may reach another device: no remote copies, remote signals or barrier semaphores. Data moves between devices by JAX's collectives and lax.ppermute only.
A program may use at most 256 MiB of HBM per device.

v0:
```python
import functools

import jax
import jax.numpy as jnp
import numpy as np
from jax import lax
from jax.experimental import pallas as pl
from jax.experimental.pallas import tpu as pltpu
from jax.sharding import PartitionSpec as P

HEAD_DIM = 64
STATE = 128
SPAN = 256
LANES = 128

epsilon = 1e-05
f32 = jnp.float32
bf16 = jnp.bfloat16


def nn(left, right):
    return lax.dot_general(left, right, (((1,), (0,)), ((), ())), preferred_element_type=f32)


def nt(left, right):
    return lax.dot_general(left, right, (((1,), (1,)), ((), ())), preferred_element_type=f32)


def tn(left, right):
    return lax.dot_general(left, right, (((0,), (0,)), ((), ())), preferred_element_type=f32)


def high_low(value):
    high = value.astype(bf16)
    return high, (value - high.astype(f32)).astype(bf16)


def spread(per_head, spreader):
    return nn(jnp.concatenate(high_low(per_head), axis=1), spreader)


def gathered_heads(units, spreader):
    high, low = high_low(units)
    once = spreader[:LANES]
    return nt(high, once) + nt(low, once)


def running_sum(triangle, value):
    high = value.astype(bf16)
    rest = value - high.astype(f32)
    middle = rest.astype(bf16)
    low = (rest - middle.astype(f32)).astype(bf16)
    sums = nn(triangle, jnp.concatenate([high, middle, low], axis=1))
    return sums[:, :LANES] + sums[:, LANES : 2 * LANES] + sums[:, 2 * LANES :]


def softplus(value):
    return jnp.maximum(value, 0.0) + jnp.log1p(jnp.exp(-jnp.abs(value)))


def moved_down(block, edge, lag):
    return jnp.concatenate([edge, block], axis=0)[8 - lag : 8 - lag + block.shape[0]]


def moved_up(block, edge, lag):
    return jnp.concatenate([block, edge], axis=0)[lag : lag + block.shape[0]]


def decay_parts(steps_in, head_rows, marks, heads):
    lane = lax.broadcasted_iota(jnp.int32, (1, LANES), 1)
    live = lane < heads
    shifted = steps_in + head_rows[0:1, :LANES]
    steps = jnp.where(live, softplus(shifted), 0.0)
    rates = head_rows[1:2, :LANES]
    log_steps = -steps * rates
    row = lax.broadcasted_iota(jnp.int32, (SPAN, SPAN), 0)
    column = lax.broadcasted_iota(jnp.int32, (SPAN, SPAN), 1)
    lower = (row >= column).astype(bf16)
    logs = running_sum(lower, log_steps)
    last = logs[SPAN - 1 : SPAN]
    entry = jnp.exp(logs) * marks[:, 3:4]
    tail = jnp.exp(last - logs) * marks[:, 4:5]
    through = jnp.exp(last) * marks[SPAN - 1 : SPAN, 3:4]
    entry = jnp.where(live, entry, 0.0)
    tail = jnp.where(live, tail, 0.0)
    through = jnp.where(live, through, 0.0)
    return shifted, steps, log_steps, logs, entry, tail, through, row, column


def linked_mask(row, column, marks, segment_row):
    linked = (row >= column) & (marks[:, 5:6] == segment_row)
    return jnp.where(linked, 0.0, -1e30)


def branch_of(own_ref, other_ref, units):
    width = own_ref.shape[1] - LANES
    own = own_ref[...].astype(f32)
    other = other_ref[...].astype(f32)
    total = own[:, :width] + other[:, :width]
    own_squares = own[:, width : width + 1] + own[:, width + 1 : width + 2]
    other_squares = other[:, width : width + 1] + other[:, width + 1 : width + 2]
    inverse = lax.rsqrt((own_squares + other_squares) / (2 * units) + epsilon)
    return total * inverse, total, inverse


def pieces_of(rows, places):
    half = places // 2
    return ((False, False, 0, places), (True, False, 0, places), (False, True, 0, places), (True, True, 0, half), (True, True, half, places - half))


def load_weights(weights, start, refs, columns, rows, place_ref):
    first, last = columns
    places = weights.shape[0] // (2 * rows)
    mine = place_ref[0]
    size = refs[0].shape[1] // 4
    for index, (moved, turned, base, count) in enumerate(pieces_of(rows, places)):
        if len(refs) == 1:
            if index == 4:
                break
            ref, offset, base, count = refs[0], index * size, 0, places
        else:
            ref, offset = refs[index], 0
        place = 1 - mine if moved else mine
        target = start + (last - first if turned else 0)
        for step in range(count):
            row = pl.multiple_of((2 * (base + step) + place) * rows, 32)
            weights[pl.ds(row, rows), target : target + last - first] = ref[step * rows : (step + 1) * rows, offset + first : offset + last]


def store_grads(refs, columns, acc, start, rows, place_ref):
    first, last = columns
    mine = place_ref[0]
    for ref, (moved, turned, base, count) in zip(refs, pieces_of(rows, acc.shape[0] // (2 * rows))):
        place = 1 - mine if moved else mine
        source = start + (last - first if turned else 0)
        for step in range(count):
            row = pl.multiple_of((2 * (base + step) + place) * rows, 32)
            ref[step * rows : (step + 1) * rows, first:last] = acc[pl.ds(row, rows), source : source + last - first].astype(bf16)


def scan_forward_kernel(second, heads, rows, pieces, *refs):
    place_ref, refs = refs[0], refs[1:]
    if second:
        (h_ref, own_ref, other_ref), refs = refs[:3], refs[3:]
    else:
        (h_ref,), refs = refs[:1], refs[1:]
    parts, refs = refs[:pieces], refs[pieces:]
    (marks_ref, segment_ref, small_ref, states_small_ref, head_ref, spread_ref), refs = refs[:6], refs[6:]
    if second:
        h_out, refs = refs[0], refs[1:]
    gain_ref, refs = refs[0], refs[1:]
    normed_ref, raw_ref, conv_ref, y_ref, raw_states_ref, conv_states_ref, steps_ref, entry_state_ref = refs[:8]
    state, raw_edge, states_edge, gain, weights = refs[8:]
    units = raw_ref.shape[1]

    @pl.when(pl.program_id(0) == 0)
    def _():
        state[...] = jnp.zeros_like(state)
        raw_edge[...] = jnp.zeros_like(raw_edge)
        states_edge[...] = jnp.zeros_like(states_edge)
        load_weights(weights, 0, parts, (0, units // 2), rows, place_ref)
        load_weights(weights, units, parts, (units // 2, units // 2 + 2 * STATE), rows, place_ref)
        steps_columns = weights[:, units + STATE : units + STATE + LANES].astype(f32)
        gain[...] = jnp.broadcast_to(jnp.transpose(steps_columns)[LANES // 2 : LANES // 2 + 1, :], gain.shape)
        gain_ref[...] = gain[...]

    hidden = h_ref[...].astype(f32)
    if second:
        rounded = (hidden + branch_of(own_ref, other_ref, units)[0]).astype(bf16)
        h_out[...] = rounded
        hidden = rounded.astype(f32)
    scale = lax.rsqrt(jnp.mean(hidden * hidden, axis=1, keepdims=True) + epsilon)
    normed = (hidden * scale * gain[0:1, :]).astype(bf16)
    normed_ref[...] = normed
    projected = nn(normed, weights[...])
    raw = projected[:, :units]
    first, second_part = projected[:, units : units + 2 * STATE], projected[:, units + 2 * STATE :]
    marks = marks_ref[...]
    turned = marks[0:1, 10:11] > 0.5
    raw_states = jnp.concatenate(
        [
            jnp.where(turned, second_part[:, :STATE], first[:, :STATE]),
            jnp.where(turned, first[:, :STATE], second_part[:, :STATE]),
        ],
        axis=1,
    )
    lane = lax.broadcasted_iota(jnp.int32, (1, LANES), 1)
    steps_in = jnp.where(lane < heads // 2, first[:, STATE:], pltpu.roll(second_part[:, STATE:], heads // 2, 1))
    raw_ref[...] = raw
    raw_states_ref[...] = raw_states
    steps_ref[...] = steps_in

    def conv(block, edge, taps):
        total = taps[4:5] + taps[3:4] * block
        for lag in (1, 2, 3):
            total = total + taps[3 - lag : 4 - lag] * (moved_down(block, edge, lag) * marks[:, lag - 1 : lag])
        return total

    taps = small_ref[...]
    conved = conv(raw, raw_edge[...], taps)
    conv_ref[...] = conved
    conved_states = conv(raw_states, states_edge[...], states_small_ref[...])
    conv_states_ref[...] = conved_states
    raw_edge[...] = raw[SPAN - 8 :]
    states_edge[...] = raw_states[SPAN - 8 :]
    values = conved * jax.nn.sigmoid(conved)
    states_in = conved_states * jax.nn.sigmoid(conved_states)
    b_rows = states_in[:, :STATE].astype(bf16)
    c_rows = states_in[:, STATE:].astype(bf16)
    _, steps, _, logs, entry, tail, through, row, column = decay_parts(steps_in, head_ref[...], marks, heads)
    spreader = spread_ref[...]
    scaled = values * spread(steps, spreader)
    mask = linked_mask(row, column, marks, segment_ref[...])
    scores = nt(c_rows, b_rows)
    logs_across = jnp.transpose(logs)
    pieces = []
    for pair in range(heads // 2):
        mixes = []
        for head in (2 * pair, 2 * pair + 1):
            factor = jnp.exp(logs[:, head : head + 1] - logs_across[head : head + 1, :] + mask)
            mixes.append((factor * scores).astype(bf16))
        block = scaled[:, pair * LANES : (pair + 1) * LANES]
        left = jnp.where(lane < HEAD_DIM, block, 0.0).astype(bf16)
        right = jnp.where(lane < HEAD_DIM, 0.0, block).astype(bf16)
        pieces.append(nn(jnp.concatenate(mixes, axis=1), jnp.concatenate([left, right], axis=0)))
    inside = jnp.concatenate(pieces, axis=1)
    held = state[...]
    entry_state_ref[0] = held
    across = nn(c_rows, held.astype(bf16)) * spread(entry, spreader)
    through_row = spread(jnp.broadcast_to(through, (8, LANES)), spreader)[0:1]
    state[...] = through_row * held + tn(b_rows, (spread(tail, spreader) * scaled).astype(bf16))
    y_ref[...] = inside + across + taps[6:7] * values


def gate_forward_kernel(rows, pieces, place_ref, normed_ref, y_ref, *refs):
    parts, refs = refs[:pieces], refs[pieces:]
    small_ref, gate_ref, part_ref, weights, out_weights = refs

    @pl.when(pl.program_id(0) == 0)
    def _():
        half = weights.shape[1] // 2
        load_weights(weights, 0, parts, (0, half), rows, place_ref)
        load_weights(out_weights, 0, parts, (half, 2 * half), rows, place_ref)

    gate = nn(normed_ref[...], weights[...])
    gate_ref[...] = gate
    gated = y_ref[...] * (gate * jax.nn.sigmoid(gate))
    squares = jnp.sum(gated * gated, axis=1, keepdims=True)
    part = nt((gated * small_ref[5:6]).astype(bf16), out_weights[...])
    width = part.shape[1]
    part_ref[:, :width] = part.astype(bf16)
    high, low = high_low(squares)
    lane = lax.broadcasted_iota(jnp.int32, (1, LANES), 1)
    part_ref[:, width:] = jnp.where(lane == 0, high, jnp.where(lane == 1, low, jnp.zeros_like(low)))


def gate_backward_kernel(second, rows, pieces, *refs):
    place_ref, refs = refs[0], refs[1:]
    if second:
        (h_ref, own_ref, other_ref, target_ref), refs = refs[:4], refs[4:]
    else:
        (own_ref, other_ref, next_h_ref, next_out_ref, grad_own_ref, grad_other_ref, next_gain_ref), refs = refs[:7], refs[7:]
    (normed_ref, gate_ref, y_ref), parts, refs = refs[:3], refs[3 : 3 + pieces], refs[3 + pieces :]
    (marks_ref, small_ref), refs = refs[:2], refs[2:]
    if second:
        out_ref, refs = refs[0], refs[1:]
    (grad_out_ref, grad_y_ref, part_ref), grads, sums_ref, refs = refs[:3], refs[3:8], refs[8], refs[9:]
    weights, out_weights, acc_z, acc_o, sums = refs
    units = y_ref.shape[1]

    @pl.when(pl.program_id(0) == 0)
    def _():
        load_weights(weights, 0, parts, (0, units // 2), rows, place_ref)
        load_weights(out_weights, 0, parts, (units // 2, units), rows, place_ref)
        for ref in (acc_z, acc_o, sums):
            ref[...] = jnp.zeros_like(ref)

    branch, total, inverse = branch_of(own_ref, other_ref, units)
    if second:
        produced = h_ref[...].astype(f32) + branch
        out_ref[...] = jnp.where(place_ref[3] == 0, h_ref[...].astype(f32), produced).astype(bf16)
        grad_out = marks_ref[:, 9:10] * (produced - target_ref[...])
    else:
        grad_normed = grad_own_ref[...].astype(f32) + grad_other_ref[...].astype(f32)
        grad_out, gain_term = norm_backward(grad_normed, next_h_ref[...].astype(f32), next_out_ref[...], next_gain_ref[0:1, :])
        sums[7:8, :] += jnp.sum(gain_term, axis=0, keepdims=True)
    grad_out_ref[...] = grad_out
    grad = grad_out.astype(bf16)
    inner = jnp.sum(grad.astype(f32) * total, axis=1, keepdims=True) * (inverse * inverse * inverse) / (2 * units)
    gain = small_ref[5:6]
    gate = gate_ref[...]
    y = y_ref[...]
    gate_sig = jax.nn.sigmoid(gate)
    gate_silu = gate * gate_sig
    gated = y * gate_silu
    gated_unit = gated * inverse
    grad_mixed = nn(grad, out_weights[...])
    acc_o[...] += tn(grad, (gated_unit * gain).astype(bf16))
    sums[5:6, :] += jnp.sum(grad_mixed * gated_unit, axis=0, keepdims=True)
    grad_gated = grad_mixed * gain * inverse - gated * inner
    grad_gate = (grad_gated * y * (gate_sig * (1.0 + gate * (1.0 - gate_sig)))).astype(bf16)
    grad_y_ref[...] = (grad_gated * gate_silu).astype(bf16)
    acc_z[...] += tn(normed_ref[...], grad_gate)
    part_ref[...] = nt(grad_gate, weights[...])

    @pl.when(pl.program_id(0) == pl.num_programs(0) - 1)
    def _():
        store_grads(grads, (0, units // 2), acc_z, 0, rows, place_ref)
        store_grads(grads, (units // 2, units), acc_o, 0, rows, place_ref)
        sums_ref[...] = sums[...]


def scan_backward_kernel(heads, rows, pieces, *refs):
    (place_ref, grad_y_ref, gate_part_ref), parts, refs = refs[:3], refs[3 : 3 + pieces], refs[3 + pieces :]
    (marks_ref, segment_ref, small_ref, states_small_ref, head_ref, spread_ref), refs = refs[:6], refs[6:]
    (raw_ref, conv_ref, y_ref, raw_states_ref, conv_states_ref, steps_ref, entry_state_ref), refs = refs[:7], refs[7:]
    (grads_ref, part_ref, sums_ref, states_sums_ref), refs = refs[:4], refs[4:]
    weights, dstate, next_state, conv_edge, states_edge, sums, states_sums = refs
    step = pl.program_id(0)
    units = raw_ref.shape[1]

    @pl.when(step == 0)
    def _():
        for ref in (dstate, next_state, conv_edge, states_edge, sums, states_sums):
            ref[...] = jnp.zeros_like(ref)
        load_weights(weights, 0, parts, (0, units // 2), rows, place_ref)
        load_weights(weights, units, parts, (units // 2, units // 2 + 2 * STATE), rows, place_ref)

    marks = marks_ref[...]
    taps = small_ref[...]
    y = y_ref[...]
    grad_y_low = grad_y_ref[...]
    grad_y = grad_y_low.astype(f32)
    conved = conv_ref[...]
    value_sig = jax.nn.sigmoid(conved)
    values = conved * value_sig
    conved_states = conv_states_ref[...]
    states_sig = jax.nn.sigmoid(conved_states)
    states_in = conved_states * states_sig
    b_rows = states_in[:, :STATE].astype(bf16)
    c_rows = states_in[:, STATE:].astype(bf16)
    shifted, steps, log_steps, logs, entry, tail, through, row, column = decay_parts(steps_ref[...], head_ref[...], marks, heads)
    spreader = spread_ref[...]
    spread_steps = spread(steps, spreader)
    spread_entry = spread(entry, spreader)
    spread_tail = spread(tail, spreader)
    through_row = spread(jnp.broadcast_to(through, (8, LANES)), spreader)[0:1]
    scaled_low = (values * spread_steps).astype(bf16)
    scaled = scaled_low.astype(f32)
    mask = linked_mask(row, column, marks, segment_ref[...])
    scores = nt(c_rows, b_rows)
    logs_across = jnp.transpose(logs)
    lane = lax.broadcasted_iota(jnp.int32, (1, LANES), 1)
    is_left = lane < HEAD_DIM
    zero = jnp.zeros((), bf16)
    grad_scores = jnp.zeros((SPAN, SPAN), f32)
    pieces = []
    for pair in range(heads // 2):
        columns = slice(pair * LANES, (pair + 1) * LANES)
        block, grad = scaled_low[:, columns], grad_y_low[:, columns]
        grad_left = jnp.where(is_left, grad, zero)
        grad_right = jnp.where(is_left, zero, grad)
        mixes = []
        for head, grad_one in ((2 * pair, grad_left), (2 * pair + 1, grad_right)):
            factor = jnp.exp(logs[:, head : head + 1] - logs_across[head : head + 1, :] + mask)
            mixes.append((factor * scores).astype(bf16))
            grad_scores = grad_scores + nt(grad_one, block) * factor
        pieces.append(tn(jnp.concatenate(mixes, axis=0), jnp.concatenate([grad_left, grad_right], axis=0)))
    held = entry_state_ref[0]
    held_low = held.astype(bf16)
    gradient = dstate[...]
    gradient_low = gradient.astype(bf16)
    grad_scaled = jnp.concatenate(pieces, axis=1) + spread_tail * nn(b_rows, gradient_low)
    grad_entry = (spread_entry * grad_y).astype(bf16)
    grad_scores_low = grad_scores.astype(bf16)
    grad_c = nn(grad_scores_low, b_rows) + nt(grad_entry, held_low)
    grad_b = tn(grad_scores_low, c_rows) + nt((spread_tail * scaled).astype(bf16), gradient_low)
    state_term = jnp.sum(gradient * next_state[...], axis=0, keepdims=True)
    dstate[...] = through_row * gradient + tn(c_rows, grad_entry)
    next_state[...] = held
    skip = taps[6:7]
    sums[6:7, :] += jnp.sum(grad_y * values, axis=0, keepdims=True)
    grad_logs = gathered_heads(grad_y * (y - skip * values) - scaled * grad_scaled, spreader)
    state_heads = gathered_heads(jnp.broadcast_to(state_term, (8, units)), spreader)[0:1]
    last_row = lax.broadcasted_iota(jnp.int32, (SPAN, 1), 0) == SPAN - 1
    grad_logs = grad_logs + jnp.where(last_row, state_heads, 0.0)
    grad_log_steps = running_sum((row <= column).astype(bf16), grad_logs)
    grad_steps = gathered_heads(grad_scaled * values, spreader) - head_ref[1:2, :LANES] * grad_log_steps
    grad_steps_in = jnp.where(lane < heads, grad_steps * jax.nn.sigmoid(shifted), 0.0)
    states_sums[5:6, :] += jnp.concatenate(
        [
            jnp.sum(grad_steps_in, axis=0, keepdims=True),
            jnp.sum(grad_log_steps * log_steps, axis=0, keepdims=True),
        ],
        axis=1,
    )
    grad_values = grad_scaled * spread_steps + skip * grad_y
    grad_conved = grad_values * (value_sig * (1.0 + conved * (1.0 - value_sig)))
    grad_states = jnp.concatenate([grad_b, grad_c], axis=1)
    grad_conved_states = grad_states * (states_sig * (1.0 + conved_states * (1.0 - states_sig)))

    def conv_backward(block, edge, tap_rows, raw, total_ref):
        result = tap_rows[3:4] * block
        total_ref[3:4, :] += jnp.sum(block * raw, axis=0, keepdims=True)
        total_ref[4:5, :] += jnp.sum(block, axis=0, keepdims=True)
        for lag in (1, 2, 3):
            term = moved_up(block, edge, lag) * marks[:, 5 + lag : 6 + lag]
            result = result + tap_rows[3 - lag : 4 - lag] * term
            total_ref[3 - lag : 4 - lag, :] += jnp.sum(term * raw, axis=0, keepdims=True)
        return result

    grad_raw = conv_backward(grad_conved, conv_edge[...], taps, raw_ref[...], sums)
    grad_raw_states = conv_backward(
        grad_conved_states, states_edge[...], states_small_ref[...], raw_states_ref[...], states_sums
    )
    conv_edge[...] = grad_conved[:8]
    states_edge[...] = grad_conved_states[:8]
    turned = marks[0:1, 10:11] > 0.5
    first_states = jnp.where(turned, grad_raw_states[:, STATE:], grad_raw_states[:, :STATE])
    second_states = jnp.where(turned, grad_raw_states[:, :STATE], grad_raw_states[:, STATE:])
    own_steps = jnp.where(lane < heads // 2, grad_steps_in, 0.0)
    other_steps = jnp.where(lane < heads // 2, pltpu.roll(grad_steps_in, LANES - heads // 2, 1), 0.0)
    grads = jnp.concatenate([grad_raw, first_states, own_steps, second_states, other_steps], axis=1).astype(bf16)
    grads_ref[...] = grads
    part_ref[...] = (nt(grads, weights[...]) + gate_part_ref[...]).astype(bf16)

    @pl.when(step == pl.num_programs(0) - 1)
    def _():
        skips = gathered_heads(sums[...], spreader)[6:7]
        states_sums[6:7, :] = jnp.concatenate([skips, jnp.zeros_like(skips)], axis=1)
        sums_ref[...] = sums[...]
        states_sums_ref[...] = states_sums[...]


def weight_grads_kernel(rows, place_ref, normed_ref, grads_ref, *refs):
    outs, acc = refs[-6:-1], refs[-1]
    units = acc.shape[1] - 4 * STATE

    @pl.when(pl.program_id(0) == 0)
    def _():
        acc[...] = jnp.zeros_like(acc)

    acc[...] += tn(normed_ref[...], grads_ref[...])

    @pl.when(pl.program_id(0) == pl.num_programs(0) - 1)
    def _():
        store_grads(outs, (0, units // 2), acc, 0, rows, place_ref)
        store_grads(outs, (units // 2, units // 2 + 2 * STATE), acc, units, rows, place_ref)


def norm_backward(grad_normed, hidden, grad_out, gain):
    scale = lax.rsqrt(jnp.mean(hidden * hidden, axis=1, keepdims=True) + epsilon)
    weighted = grad_normed * gain
    shared = jnp.mean(weighted * hidden, axis=1, keepdims=True) * (scale * scale * scale)
    return grad_out + scale * weighted - hidden * shared, grad_normed * hidden * scale


VMEM_LIMIT = 60 * 1024 * 1024


def spreader_of(units):
    one = (np.arange(LANES)[:, None] == np.arange(units)[None, :] // HEAD_DIM).astype(np.float32)
    return jnp.asarray(np.concatenate([one, one], axis=0), bf16)


def rows_spec(width, last=None):
    if last is None:
        return pl.BlockSpec((SPAN, width), lambda i: (i, 0))
    return pl.BlockSpec((SPAN, width), lambda i: (last - i, 0))


def whole_spec(array):
    return pl.BlockSpec(array.shape, lambda i: (0,) * array.ndim)


def call(kernel, inputs, outputs, scratch, chunks, flops):
    return pl.pallas_call(
        kernel,
        grid=(chunks,),
        in_specs=[spec for _, spec in inputs],
        out_specs=[spec for _, _, spec in outputs],
        out_shape=[jax.ShapeDtypeStruct(shape, dtype) for shape, dtype, _ in outputs],
        scratch_shapes=[pltpu.VMEM(shape, dtype) for shape, dtype in scratch],
        compiler_params=pltpu.CompilerParams(vmem_limit_bytes=VMEM_LIMIT, dimension_semantics=("arbitrary",)),
        cost_estimate=pl.CostEstimate(flops=flops, bytes_accessed=500_000, transcendentals=0),
    )(*[array for array, _ in inputs])


def fixed(array):
    return array, whole_spec(array)


def scalars(array):
    return array, pl.BlockSpec(memory_space=pltpu.SMEM)


def grad_outputs(width, rows, columns):
    outputs = []
    for _, _, _, count in pieces_of(rows, width // (2 * rows)):
        shape = (count * rows, columns)
        outputs.append((shape, bf16, pl.BlockSpec(shape, lambda i: (0, 0))))
    return outputs


def awaited(arrays):
    return [(array, pl.BlockSpec(memory_space=pl.ANY)) for array in arrays]


def scan_forward(place, rows, h, parts, weights, marks, segment_row, params):
    length, width = h.shape
    units = params[0].shape[1]
    chunks = length // SPAN
    second = parts is not None
    inputs = [scalars(place), (h, rows_spec(width))]
    outputs = []
    if second:
        inputs += [(part, rows_spec(width + LANES)) for part in parts]
        outputs.append(((length, width), bf16, rows_spec(width)))
    inputs += [fixed(w) for w in weights]
    inputs += [(marks, rows_spec(LANES)), (segment_row, pl.BlockSpec((1, SPAN), lambda i: (0, i)))]
    inputs += [fixed(p) for p in params] + [fixed(spreader_of(units))]
    outputs.append(((8, width), f32, pl.BlockSpec((8, width), lambda i: (0, 0))))
    outputs.append(((length, width), bf16, rows_spec(width)))
    for columns in (units, units, units, 2 * STATE, 2 * STATE, LANES):
        outputs.append(((length, columns), f32, rows_spec(columns)))
    outputs.append(((chunks, STATE, units), f32, pl.BlockSpec((1, STATE, units), lambda i: (i, 0, 0))))
    scratch = [
        ((STATE, units), f32),
        ((8, units), f32),
        ((8, 2 * STATE), f32),
        ((8, width), f32),
        ((width, units + 4 * STATE), bf16),
    ]
    kernel = functools.partial(scan_forward_kernel, second, units // HEAD_DIM, rows, len(weights))
    results = call(kernel, inputs, outputs, scratch, chunks, 2_000_000_000)
    if not second:
        results = [h] + list(results)
    return results[0], results[1], results[2], results[3:]


def gate_forward(place, rows, normed, y, weights, params):
    length, width = normed.shape
    units = params[0].shape[1]
    inputs = [scalars(place), (normed, rows_spec(width)), (y, rows_spec(units))] + [fixed(w) for w in weights] + [fixed(params[0])]
    outputs = [((length, units), f32, rows_spec(units)), ((length, width + LANES), bf16, rows_spec(width + LANES))]
    scratch = [((width, units), bf16)] * 2
    return call(functools.partial(gate_forward_kernel, rows, len(weights)), inputs, outputs, scratch, length // SPAN, 1_000_000_000)


def gate_backward(place, rows, h, parts, extra, normed, gate, y, weights, marks, params):
    length, width = normed.shape
    units = params[0].shape[1]
    second = len(extra) == 1
    inputs = [scalars(place)] + ([(h, rows_spec(width))] if second else [])
    inputs += [(part, rows_spec(width + LANES)) for part in parts]
    inputs += [(array, rows_spec(width)) for array in extra[:4]] + [fixed(gain) for gain in extra[4:]]
    inputs += [(normed, rows_spec(width)), (gate, rows_spec(units)), (y, rows_spec(units))]
    inputs += [fixed(w) for w in weights] + [(marks, rows_spec(LANES)), fixed(params[0])]
    outputs = [((length, width), bf16, rows_spec(width))] if second else []
    outputs += [((length, width), f32, rows_spec(width)), ((length, units), bf16, rows_spec(units)), ((length, width), f32, rows_spec(width))]
    outputs += grad_outputs(width, rows, units)
    outputs.append(((8, units), f32, pl.BlockSpec((8, units), lambda i: (0, 0))))
    scratch = [((width, units), bf16)] * 2 + [((width, units), f32)] * 2 + [((8, units), f32)]
    results = call(functools.partial(gate_backward_kernel, second, rows, len(weights)), inputs, outputs, scratch, length // SPAN, 2_000_000_000)
    if not second:
        results = [None] + list(results)
    return results


def scan_backward(place, rows, grad_y, gate_part, weights, marks, segment_row, params, saved):
    length, width = gate_part.shape
    units = params[0].shape[1]
    chunks = length // SPAN
    last = chunks - 1
    inputs = [scalars(place), (grad_y, rows_spec(units, last)), (gate_part, rows_spec(width, last))]
    inputs += [fixed(w) for w in weights]
    inputs += [(marks, rows_spec(LANES, last)), (segment_row, pl.BlockSpec((1, SPAN), lambda i: (0, last - i)))]
    inputs += [fixed(p) for p in params] + [fixed(spreader_of(units))]
    inputs += [(s, rows_spec(s.shape[1], last)) for s in saved[:6]]
    inputs.append((saved[6], pl.BlockSpec((1, STATE, units), lambda i: (last - i, 0, 0))))
    columns = units + 4 * STATE
    outputs = [((length, columns), bf16, rows_spec(columns, last)), ((length, width), bf16, rows_spec(width, last))]
    for columns in (units, 2 * STATE):
        outputs.append(((8, columns), f32, pl.BlockSpec((8, columns), lambda i: (0, 0))))
    scratch = [
        ((width, units + 4 * STATE), bf16),
        ((STATE, units), f32),
        ((STATE, units), f32),
        ((8, units), f32),
        ((8, 2 * STATE), f32),
        ((8, units), f32),
        ((8, 2 * STATE), f32),
    ]
    kernel = functools.partial(scan_backward_kernel, units // HEAD_DIM, rows, len(weights))
    return call(kernel, inputs, outputs, scratch, chunks, 3_000_000_000)


def weight_grads(place, rows, normed, grads, ready):
    length, width = normed.shape
    columns = grads.shape[1]
    inputs = [scalars(place), (normed, rows_spec(width)), (grads, rows_spec(columns))] + awaited(ready)
    outputs = grad_outputs(width, rows, columns // 2)
    scratch = [((width, columns), f32)]
    return call(functools.partial(weight_grads_kernel, rows), inputs, outputs, scratch, length // SPAN, 500_000_000)


def finish_kernel(place_ref, own_ref, other_ref, h_ref, grad_out_ref, gain_ref, *refs):
    grad_ref, low_ref, sums_ref, sums = refs[-4:]

    @pl.when(pl.program_id(0) == 0)
    def _():
        sums[...] = jnp.zeros_like(sums)

    grad_normed = own_ref[...].astype(f32) + other_ref[...].astype(f32)
    next_grad = grad_out_ref[...]
    grad, gain_term = norm_backward(grad_normed, h_ref[...].astype(f32), next_grad.astype(bf16).astype(f32), gain_ref[0:1, :])
    rows = jnp.where(place_ref[3] == 0, grad, next_grad)
    grad_ref[...] = rows
    low_ref[...] = rows.astype(bf16)
    sums[0:1, :] += jnp.sum(gain_term, axis=0, keepdims=True)
    sums_ref[...] = sums[...]


def finish(place, own, other, h, grad_out, gain, ready):
    length, width = h.shape
    inputs = [scalars(place)] + [(rows, rows_spec(width)) for rows in (own, other, h, grad_out)] + [fixed(gain)]
    inputs += awaited(ready)
    outputs = [((length, width), f32, rows_spec(width)), ((length, width), bf16, rows_spec(width))]
    outputs.append(((8, width), f32, pl.BlockSpec((8, width), lambda i: (0, 0))))
    return call(finish_kernel, inputs, outputs, [((8, width), f32)], length // SPAN, 30_000_000)


def placed_kernel(place_ref, own_ref, away_ref, *refs):
    out_ref = refs[-1]
    own = pl.program_id(0) == place_ref[1]
    out_ref[0] = jnp.where(own, own_ref[...].astype(f32), away_ref[...].astype(f32)).astype(out_ref.dtype)


def placed_rows(place, rows, away, ready=()):
    half, width = away.shape
    return pl.pallas_call(
        placed_kernel,
        grid_spec=pltpu.PrefetchScalarGridSpec(
            num_scalar_prefetch=1,
            grid=(2,),
            in_specs=[
                pl.BlockSpec((half, width), lambda m, place: (place[1], 0)),
                pl.BlockSpec((half, width), lambda m, place: (0, 0)),
            ]
            + [pl.BlockSpec(memory_space=pl.ANY)] * len(ready),
            out_specs=pl.BlockSpec((1, half, width), lambda m, place: (m, 0, 0)),
        ),
        out_shape=jax.ShapeDtypeStruct((2, half, width), rows.dtype),
        compiler_params=pltpu.CompilerParams(vmem_limit_bytes=VMEM_LIMIT, dimension_semantics=("arbitrary",)),
        cost_estimate=pl.CostEstimate(flops=0, bytes_accessed=500_000, transcendentals=0),
    )(place, rows, away, *ready)


def marks_kernel(place_ref, lengths_ref, segments_ref, marks_ref, row_ref):
    turn, rank = place_ref[1], place_ref[2]
    micro, sequences = lengths_ref.shape
    length = segments_ref.shape[1]
    total = jnp.int32(0)
    for batch in range(micro):
        total = lax.fori_loop(0, sequences, lambda i, t: t + lengths_ref[batch, i], total)
    weight = 2.0 * (micro * sequences * length) / jnp.full((1, length), total, jnp.int32).astype(f32)
    position = lax.broadcasted_iota(jnp.int32, (1, length), 1)
    segment = jnp.where(turn == 0, segments_ref[0:1, :], segments_ref[1:2, :])
    wide = jnp.broadcast_to(segment, (8, length))

    def same(lag):
        moved = pltpu.roll(wide, lag % length, 1)[0:1]
        inside = (position >= lag) & (position < length + lag)
        return jnp.where(inside & (moved == segment), 1.0, 0.0)

    before = jnp.full((1, length), -1, jnp.int32)
    end = before
    for block in range(length // SPAN):
        here = (position >= block * SPAN) & (position < (block + 1) * SPAN)
        end = jnp.where(here, segment[:, (block + 1) * SPAN - 1 : (block + 1) * SPAN], end)
        if block:
            before = jnp.where(here, segment[:, block * SPAN - 1 : block * SPAN], before)
    as_float = segment.astype(f32)
    rows = [same(1), same(2), same(3)]
    rows += [jnp.where(segment == before, 1.0, 0.0), jnp.where(segment == end, 1.0, 0.0), as_float]
    rows += [same(-1), same(-2), same(-3)]
    rows += [jnp.where(position < lengths_ref[turn, rank], weight, 0.0), jnp.full((1, length), turn, jnp.int32).astype(f32)]
    rows.append(jnp.zeros((LANES - len(rows), length), f32))
    marks_ref[...] = jnp.transpose(jnp.concatenate(rows, axis=0))
    row_ref[...] = as_float


def token_marks(place, lengths, segments):
    length = segments.shape[1]
    return pl.pallas_call(
        marks_kernel,
        in_specs=[pl.BlockSpec(memory_space=pltpu.SMEM)] * 2 + [pl.BlockSpec(memory_space=pltpu.VMEM)],
        out_shape=[jax.ShapeDtypeStruct((length, LANES), f32), jax.ShapeDtypeStruct((1, length), f32)],
        compiler_params=pltpu.CompilerParams(vmem_limit_bytes=VMEM_LIMIT),
        cost_estimate=pl.CostEstimate(flops=0, bytes_accessed=500_000, transcendentals=0),
    )(place, lengths, segments)


def three_parts(value):
    high = value.astype(bf16)
    rest = value - high.astype(f32)
    middle = rest.astype(bf16)
    return high, middle, (rest - middle.astype(f32)).astype(bf16)


PARAM_ROWS = 16


def pack_kernel(
    place_ref, zx_ref, bc_ref, dt_ref, gain_ref, out_ref, conv_ref, gate_gain_ref, states_conv_ref, bias_ref, rate_ref, skip_ref, kept_ref, sent_ref
):
    turn, core = place_ref[1], place_ref[3]
    rows = zx_ref.shape[0]
    half = zx_ref.shape[2] // 2
    heads_half = dt_ref.shape[0] // 2
    lane = lax.broadcasted_iota(jnp.int32, (1, LANES), 1)
    bc = jnp.where(turn == 0, bc_ref[:, :STATE], bc_ref[:, STATE:])
    diagonal = lax.broadcasted_iota(jnp.int32, (rows, rows), 0) == lax.broadcasted_iota(jnp.int32, (rows, rows), 1)
    gain = jnp.sum(jnp.where(diagonal, gain_ref[...].astype(f32), 0.0), axis=1, keepdims=True)
    head = lax.broadcasted_iota(jnp.int32, (2 * heads_half, LANES), 0)
    column = lax.broadcasted_iota(jnp.int32, (2 * heads_half, LANES), 1)
    shared = jnp.concatenate([states_conv_ref[...], jnp.zeros((PARAM_ROWS - 5, 2 * STATE), bf16)], axis=0)
    split = [part.astype(f32) for ref in (bias_ref, rate_ref, skip_ref) for part in three_parts(ref[...])]
    heads = jnp.concatenate(split + [jnp.zeros((PARAM_ROWS - 9, split[0].shape[1]), f32)], axis=0)
    heads = jnp.concatenate([heads, jnp.zeros((PARAM_ROWS, LANES - heads.shape[1]), f32)], axis=1).astype(bf16)
    for ref, part in ((kept_ref, core), (sent_ref, 1 - core)):
        first = part == 0

        def chosen(array, start):
            return jnp.where(first, array[:, start : start + half], array[:, start + half : start + 2 * half])

        ref[:rows, :half] = chosen(zx_ref[:, 1, :], 0)
        ref[:rows, half : half + STATE] = bc
        taken = (head == column + part * heads_half) & (column < heads_half)
        own_steps = tn(dt_ref[...], jnp.where(taken, 1.0, 0.0).astype(bf16))
        ref[:rows, half + STATE : half + 2 * STATE] = jnp.where(lane == LANES // 2, gain, own_steps).astype(bf16)
        ref[:rows, half + 2 * STATE : 2 * half + 2 * STATE] = chosen(zx_ref[:, 0, :], 0)
        ref[:rows, 2 * half + 2 * STATE :] = chosen(out_ref, 0)
        ref[rows:, :] = jnp.zeros((PARAM_ROWS, ref.shape[1]), bf16)
        channels = jnp.concatenate([chosen(conv_ref, 0), chosen(gate_gain_ref, 0)], axis=0)
        ref[rows:, :half] = jnp.concatenate([channels, jnp.zeros((PARAM_ROWS - 6, half), bf16)], axis=0)
        ref[rows:, half : half + 2 * STATE] = shared
        ref[rows:, half + 2 * STATE : half + 2 * STATE + LANES] = heads


def plain_call(kernel, place, inputs, outputs, ready=()):
    count = len(ready)
    body = kernel if not count else lambda place_ref, *refs: kernel(place_ref, *refs[count:])
    return pl.pallas_call(
        body,
        in_specs=[pl.BlockSpec(memory_space=pltpu.SMEM)]
        + [pl.BlockSpec(memory_space=pl.ANY)] * count
        + [pl.BlockSpec(memory_space=pltpu.VMEM)] * len(inputs),
        out_shape=[jax.ShapeDtypeStruct(shape, dtype) for shape, dtype in outputs],
        compiler_params=pltpu.CompilerParams(vmem_limit_bytes=VMEM_LIMIT),
        cost_estimate=pl.CostEstimate(flops=0, bytes_accessed=500_000, transcendentals=0),
    )(place, *ready, *inputs)


def unpack_kernel(place_ref, kept_ref, received_ref, *refs):
    scan_ref, middle_ref, gate_ref, params_ref, channels_ref = refs
    kept_first = place_ref[3] == 0
    kept, received = kept_ref[...], received_ref[...]
    first = jnp.where(kept_first, kept, received)
    second = jnp.where(kept_first, received, kept)
    rows, scan = scan_ref.shape
    half = channels_ref.shape[1]
    scan_ref[...] = first[:rows, :scan]
    middle_ref[:, : 2 * half] = first[:rows, scan:]
    middle_ref[:, 2 * half :] = second[:rows, :scan]
    gate_ref[...] = second[:rows, scan:]
    params_ref[0] = first[rows:, : scan + LANES]
    params_ref[1] = second[rows:, : scan + LANES]
    channels_ref[:PARAM_ROWS] = first[rows:, :half]
    channels_ref[PARAM_ROWS:] = second[rows:, :half]


def params_kernel(heads_half, place_ref, params_ref, channels_ref, spread_ref, *refs):
    turn, core = place_ref[1], place_ref[3]
    half = channels_ref.shape[1]
    lane = lax.broadcasted_iota(jnp.int32, (1, LANES), 1)
    for layer in range(2):
        small_ref, states_ref, head_ref = refs[3 * layer : 3 * layer + 3]
        rows = params_ref[layer].astype(f32)
        split = rows[:, half + 2 * STATE :]
        heads = [split[3 * i : 3 * i + 1] + split[3 * i + 1 : 3 * i + 2] + split[3 * i + 2 : 3 * i + 3] for i in range(3)]
        heads = jnp.concatenate(heads + [jnp.zeros((5, LANES), f32)], axis=0)
        moved = [pltpu.roll(heads, (LANES - start * heads_half) % LANES, 1) for start in range(4)]

        def of(index):
            return jnp.where(index == 0, moved[0], jnp.where(index == 1, moved[1], jnp.where(index == 2, moved[2], moved[3])))

        own, other = of(2 * turn + core), pltpu.roll(of(2 * (1 - turn) + core), heads_half, 1)
        heads = jnp.where(lane < heads_half, own, jnp.where(lane < 2 * heads_half, other, 0.0))
        head_ref[...] = jnp.concatenate([heads[0:1], jnp.exp(heads[1:2]), jnp.zeros((6, LANES), f32)], axis=0)
        high, middle, low = three_parts(jnp.broadcast_to(heads[2:3], (8, LANES)))
        once = spread_ref[:LANES]
        skips = (nn(high, once) + nn(middle, once) + nn(low, once))[0:1]
        own_rows = rows[0:6, :half]
        other_rows = channels_ref[PARAM_ROWS * layer : PARAM_ROWS * layer + 6].astype(f32)
        channels = jnp.concatenate([own_rows, other_rows], axis=1)
        small_ref[...] = jnp.concatenate([channels, skips, jnp.zeros_like(skips)], axis=0)
        states_ref[...] = jnp.concatenate([rows[0:5, half : half + 2 * STATE], jnp.zeros((3, 2 * STATE), f32)], axis=0)


def beside_kernel(place_ref, *refs):
    out = refs[-1]
    start = 0
    for ref in refs[:-1]:
        out[:, start : start + ref.shape[1]] = ref[...]
        start += ref.shape[1]


def split_kernel(place_ref, whole_ref, *outs):
    start = 0
    for out in outs:
        out[...] = whole_ref[:, start : start + out.shape[1]]
        start += out.shape[1]


def cross_kernel(place_ref, *refs):
    over_x, over_tensor = refs[-2:]
    start = 0
    for group in range(len(refs[:-2]) // 4):
        x_ref, y_ref, first_ref, second_ref = refs[4 * group : 4 * group + 4]
        columns = slice(start, start + x_ref.shape[1])
        start += x_ref.shape[1]
        half = first_ref.shape[0]
        over_x[:half, columns] = (x_ref[:half].astype(f32) + first_ref[...].astype(f32)).astype(bf16)
        over_x[half:, columns] = x_ref[half:]
        over_tensor[:half, columns] = y_ref[:half]
        over_tensor[half:, columns] = (y_ref[half:].astype(f32) + second_ref[...].astype(f32)).astype(bf16)


def join_kernel(groups, place_ref, *refs):
    out = refs[-1]
    start = 0
    for own, over_x, over_tensor, offset in groups:
        width = refs[own].shape[1]
        there = slice(offset, offset + width)
        total = refs[own][...].astype(f32) + refs[over_x][:, there].astype(f32) + refs[over_tensor][:, there].astype(f32)
        out[:, start : start + width] = total.astype(bf16)
        start += width


def owned_kernel(place_ref, first_ref, second_ref, beside_ref, across_ref, both_ref, zx_ref, bc_ref, dt_ref, out_ref):
    first = place_ref[3] == 0
    half = out_ref.shape[1] // 2
    heads_half = dt_ref.shape[1] // 2
    mine = jnp.where(first, first_ref[...], second_ref[...]).astype(f32)
    beside = beside_ref[...].astype(f32)
    lower, upper = jnp.where(first, mine, beside), jnp.where(first, beside, mine)
    gate = half + 2 * STATE
    for index, part in enumerate((lower, upper)):
        columns = slice(index * half, (index + 1) * half)
        zx_ref[:, 0, columns] = part[:, gate : gate + half]
        zx_ref[:, 1, columns] = part[:, :half]
        out_ref[:, columns] = part[:, gate + half :]
    own = mine[:, half : half + STATE] + beside[:, half : half + STATE]
    other = across_ref[...].astype(f32) + both_ref[...].astype(f32)
    straight = place_ref[1] == 0
    bc_ref[:, :STATE] = jnp.where(straight, own, other)
    bc_ref[:, STATE:] = jnp.where(straight, other, own)
    lane = lax.broadcasted_iota(jnp.int32, (1, LANES), 1)
    steps = slice(half + STATE, half + 2 * STATE)
    both = jnp.where(lane < heads_half, lower[:, steps], pltpu.roll(upper[:, steps], heads_half, 1))
    dt_ref[...] = both[:, : 2 * heads_half]


def small_kernel(gate0, scan0, states0, gate1, scan1, states1, gain_ref, out_ref):
    for layer, (gate, scan, states, gain) in enumerate(
        ((gate0, scan0, states0, gain_ref[0:1, :]), (gate1, scan1, states1, gate0[7:8, :]))
    ):
        start = 16 * layer
        out_ref[start : start + 5, :] = scan[0:5, :]
        out_ref[start + 5 : start + 6, :] = gate[5:6, :]
        out_ref[start + 6 : start + 7, :] = gain
        out_ref[start + 7 : start + 16, :] = jnp.zeros((9, out_ref.shape[1]), f32)
        out_ref[start + 8 : start + 15, : 2 * STATE] = states[0:7, :]


def fold_kernel(heads_half, place_ref, own_ref, away_ref, mine_ref, others_ref):
    first = place_ref[3] == 0
    half = mine_ref.shape[1]
    folded = []
    for layer in range(2):
        own, away = own_ref[16 * layer : 16 * layer + 16], away_ref[16 * layer : 16 * layer + 16]
        units = own[0:6, :half] + away[0:6, half:]
        gain = own[6:7] + away[6:7]
        total = own[8:16, :half] + away[8:16, :half]
        own_heads = jnp.concatenate([own[14:15, :LANES], own[13:14, : 2 * LANES]], axis=1)
        away_heads = jnp.concatenate([away[14:15, :LANES], away[13:14, : 2 * LANES]], axis=1)
        moved = pltpu.roll(jnp.broadcast_to(away_heads, (8, 3 * LANES)), 3 * LANES - heads_half, 1)[0:1]
        heads = jnp.concatenate([own_heads + moved, jnp.zeros((1, half - 3 * LANES), f32)], axis=1) if half > 3 * LANES else own_heads + moved
        zeros = jnp.zeros((2, half), f32)
        folded.append(jnp.concatenate([units, gain[:, :half], gain[:, half:], total[0:5], heads, zeros], axis=0))
    mine_ref[...] = jnp.where(first, folded[0], folded[1])
    others_ref[...] = jnp.where(first, folded[1], folded[0])


def small_outputs_kernel(heads_half, place_ref, total_ref, conv_ref, states_conv_ref, gate_gain_ref, heads_ref, gain_ref):
    first = place_ref[3] == 0
    half = total_ref.shape[1]
    here, there = total_ref[0:16], total_ref[16:32]
    lower, upper = jnp.where(first, here, there), jnp.where(first, there, here)
    conv_ref[:, :half] = lower[0:5]
    conv_ref[:, half:] = upper[0:5]
    gate_gain_ref[:, :half] = lower[5:6]
    gate_gain_ref[:, half:] = upper[5:6]
    states_conv_ref[...] = here[8:13, : 2 * STATE] + there[8:13, : 2 * STATE]
    lane = lax.broadcasted_iota(jnp.int32, (1, LANES), 1)
    for row in range(3):
        own = lower[13:14, row * LANES : (row + 1) * LANES]
        other = pltpu.roll(jnp.broadcast_to(upper[13:14, row * LANES : (row + 1) * LANES], (8, LANES)), heads_half, 1)[0:1]
        heads_ref[row : row + 1, :] = jnp.where(lane < heads_half, own, other)[:, : 2 * heads_half]
    gain_ref[:, :half] = here[6:7]
    gain_ref[:, half:] = here[7:8]


def tied(*values):
    return lax.optimization_barrier(values)


def swapped(block, axis):
    return lax.ppermute(block, axis, [(0, 1), (1, 0)])


def far_swapped(block):
    size = lax.axis_size("tensor")
    return lax.ppermute(block, ("section", "tensor"), [(i, 2 * size - 1 - i) for i in range(2 * size)])


def body(
    x_input,
    teacher,
    segment_ids,
    valid_len,
    norm_gain,
    w_zx,
    w_bc,
    w_dt,
    conv_x,
    conv_bc,
    dt_bias,
    a_log,
    d_skip,
    gnorm_gain,
    w_out,
):
    local_rows, width = x_input.shape[1:]
    ranks = lax.axis_size("dp")
    places = ranks // 2
    core = lax.axis_index("section")
    turn = lax.axis_index("tensor")
    rank = lax.axis_index("dp")
    place = jnp.stack([rank % 2, turn, rank, core]).astype(jnp.int32)
    on_first = core == 0
    block_rows = w_zx.shape[1]
    half = w_zx.shape[3] // 2
    units = 2 * half
    heads_half = w_dt.shape[2] // 2
    scan_columns = half + 2 * STATE
    line_groups = [[2 * index + start for index in range(places)] for start in range(2)]

    def by_layer(kept, received):
        return jnp.where(on_first, kept, received), jnp.where(on_first, received, kept)

    def x_swapped(block):
        return lax.ppermute(block, "dp", [(i, i ^ 1) for i in range(ranks)])

    def y_swapped(block):
        return swapped(block, "tensor")

    def line_gather(block):
        return lax.all_gather(block, "dp", axis_index_groups=line_groups, axis=0, tiled=True)

    def line_reduce(block):
        return lax.psum_scatter(block, "dp", axis_index_groups=line_groups, scatter_dimension=0, tiled=True)

    def line_total(block):
        if places != 4:
            return lax.psum(block, "dp", axis_index_groups=line_groups)

        def send(rows, moves):
            return lax.ppermute(rows, "dp", [(2 * a + start, 2 * b + start) for a, b in moves for start in range(2)])

        up, down = send(block, [(0, 1), (1, 2), (2, 3)]), send(block, [(1, 0), (2, 1), (3, 2)])
        up2, down2 = send(up, [(1, 2), (2, 3)]), send(down, [(2, 1), (1, 0)])
        far = send(jnp.where(rank // 2 == 1, up, down), [(1, 3), (2, 0)])
        return block + up + down + up2 + down2 + far

    pack_shape = (block_rows + PARAM_ROWS, scan_columns + units)
    kept, sent = plain_call(
        pack_kernel,
        place,
        (w_zx[0], w_bc[0], w_dt[0].T, norm_gain, w_out[0].T, conv_x[0], gnorm_gain, conv_bc[0], dt_bias, a_log, d_skip),
        [(pack_shape, bf16)] * 2,
    )
    received = swapped(sent, "section")
    scan_block, middle_block, gate_block, params_both, channels = plain_call(
        unpack_kernel,
        place,
        (kept, received),
        [
            ((block_rows, scan_columns), bf16),
            ((block_rows, units + scan_columns), bf16),
            ((block_rows, units), bf16),
            ((2, PARAM_ROWS, scan_columns + LANES), bf16),
            ((2 * PARAM_ROWS, half), bf16),
        ],
    )

    def plane_end(block, over_x, over_tensor):
        cut = places // 2 * block_rows
        return block, over_x, over_tensor, y_swapped(over_x[:cut]), x_swapped(over_tensor[cut:])

    def quarter(rows):
        away = lax.dynamic_index_in_dim(rows, 1 - turn, 0, keepdims=False)
        return lax.dynamic_slice_in_dim(away, core * (local_rows // 2), local_rows // 2, 0)

    def whole_rows(rows, here, beside):
        own = lax.dynamic_index_in_dim(rows, turn, 0, keepdims=False)
        other = jnp.concatenate(by_layer(here, beside), axis=0)
        return jnp.where(turn == 0, jnp.concatenate([own, other]), jnp.concatenate([other, own]))

    scan_line, here, channels = tied(line_gather(scan_block), y_swapped(quarter(x_input)), y_swapped(channels))
    scan_line, middle_block = tied(scan_line, middle_block)
    middle_line = line_gather(middle_block)
    scan_half = scan_line, x_swapped(scan_line), y_swapped(scan_line)
    x_rows = whole_rows(x_input, here, swapped(here, "section"))
    params = plain_call(
        functools.partial(params_kernel, heads_half),
        place,
        (params_both, channels, spreader_of(units)),
        [((8, units), f32), ((8, 2 * STATE), f32), ((8, LANES), f32)] * 2,
    )
    params = [params[:3], params[3:]]
    marks, segment_row = token_marks(place, valid_len, segment_ids[:, 0])
    over_x = x_swapped(gate_block)
    side = (gate_block, over_x, y_swapped(gate_block), y_swapped(over_x))
    side = plain_call(beside_kernel, place, side, [((block_rows, 4 * units), bf16)], (x_rows, marks, params[0][0]))[0]
    scan_first, side = tied(plane_end(*scan_half), side)
    middle_line, side = tied(middle_line, side)
    gate_second = (line_gather(side),)
    gate_line, next_line = plain_call(
        split_kernel,
        place,
        (middle_line,),
        [((places * block_rows, units), bf16), ((places * block_rows, scan_columns), bf16)],
        (scan_first[4],),
    )

    gate_half = gate_line, x_swapped(gate_line), y_swapped(gate_line)
    next_half = next_line, x_swapped(next_line), y_swapped(next_line)
    results = scan_forward(place, block_rows, x_rows, None, scan_first, marks, segment_row, params[0])
    results, gate_half, next_half = tied(results, gate_half, next_half)
    _, gain_first, normed_first, saved_first = results
    gate_first = plane_end(*gate_half)
    gated_first, part = gate_forward(place, block_rows, normed_first, saved_first[2], gate_first, params[0])
    part, next_half = tied(part, next_half)
    scan_second = plane_end(*next_half)
    parts_first = (part, swapped(part, "section"))
    parts_first, teacher = tied(parts_first, teacher)
    results = scan_forward(place, block_rows, x_rows, parts_first, scan_second, marks, segment_row, params[1])
    results, here = tied(results, y_swapped(quarter(teacher)))
    hidden, gain_second, normed_second, saved_second = results
    results = gate_forward(place, block_rows, normed_second, saved_second[2], gate_second, params[1])
    (gated_second, part), here, beside = tied(results, here, swapped(here, "section"))
    parts_second = (part, swapped(part, "section"))
    target = whole_rows(teacher, here, beside)

    def plane_start(pieces):
        return tuple(pieces[:3]), (y_swapped(pieces[3]), x_swapped(pieces[4]))

    def crossed(*groups):
        arrays = [array for pieces, came in groups for array in pieces[1:] + came]
        columns = sum(pieces[0].shape[1] for pieces, _ in groups)
        over_x, over_tensor = plain_call(cross_kernel, place, arrays, [((places * block_rows, columns), bf16)] * 2)
        return [pieces[0] for pieces, _ in groups], x_swapped(over_x), y_swapped(over_tensor)

    def joined(*groups, ready=()):
        arrays, spans = [], []
        for owns, over_x, over_tensor in groups:
            base = len(arrays)
            arrays += list(owns) + [over_x, over_tensor]
            offset = 0
            for index, own in enumerate(owns):
                spans.append((base + index, base + len(owns), base + len(owns) + 1, offset))
                offset += own.shape[1]
        columns = sum(arrays[span[0]].shape[1] for span in spans)
        kernel = functools.partial(join_kernel, spans)
        return plain_call(kernel, place, arrays, [((places * block_rows, columns), bf16)], ready)[0]

    results = gate_backward(
        place,
        block_rows,
        hidden,
        parts_second,
        (target,),
        normed_second,
        gated_second,
        saved_second[2],
        gate_second,
        marks,
        params[1],
    )
    produced, grad_out, grad_y, gate_part = results[:4]
    gate_reduce = plane_start(results[4:9])
    gate_sums_second = results[9]

    def away_rows(rows):
        return y_swapped(lax.dynamic_slice_in_dim(rows, (1 - turn) * local_rows, local_rows, 0))

    results = scan_backward(
        place, block_rows, grad_y, gate_part, scan_second, marks, segment_row, params[1], saved_second
    )
    results, gate_reduce, produced_away = tied(results, gate_reduce, away_rows(produced))
    grads, part, sums, states_sums = results
    sums_second = (gate_sums_second, sums, states_sums)
    results = weight_grads(place, block_rows, normed_second, grads, ())
    results, grad_parts = tied(results, (part, swapped(part, "section")))
    scan_reduce = plane_start(results)
    results = gate_backward(
        place,
        block_rows,
        x_rows,
        parts_first,
        (hidden, grad_out) + grad_parts + (gain_second,),
        normed_first,
        gated_first,
        saved_first[2],
        gate_first,
        marks,
        params[0],
    )
    results, scan_reduce = tied(results[1:], scan_reduce)
    grad_hidden, grad_y, gate_part = results[:3]
    crossed_second = crossed(scan_reduce, gate_reduce)
    gate_reduce = plane_start(results[3:8])
    gate_sums_first = results[8]
    results = scan_backward(
        place, block_rows, grad_y, gate_part, scan_first, marks, segment_row, params[0], saved_first
    )
    results, crossed_second, gate_reduce = tied(results, crossed_second, gate_reduce)
    grads, part, sums, states_sums = results
    sums_first = (gate_sums_first, sums, states_sums)
    results = weight_grads(place, block_rows, normed_first, grads, ())
    results, grad_parts = tied(results, (part, swapped(part, "section")))
    scan_reduce = plane_start(results)
    owned_second = line_reduce(joined(crossed_second, ready=(results[0],)))
    crossed_gate = crossed(gate_reduce)
    results = finish(place, *grad_parts, x_rows, grad_hidden, gain_first, (crossed_gate[0][0],))
    (grad_rows, grad_low, gain_sums), scan_reduce = tied(results, scan_reduce)
    crossed_scan = crossed(scan_reduce)
    layer_outputs = placed_rows(place, produced, produced_away, (crossed_scan[0][0],))
    smalls = plain_call(
        lambda place_ref, *refs: small_kernel(*refs), place, sums_first + sums_second + (gain_sums,), [((32, units), f32)]
    )[0]
    smalls_away = y_swapped(smalls)
    mine, others = plain_call(
        functools.partial(fold_kernel, heads_half), place, (smalls, smalls_away), [((16, half), f32)] * 2
    )
    total = jnp.concatenate([mine, swapped(others, "section")])
    total = total + x_swapped(total)
    blocks = joined(crossed_scan, crossed_gate, ready=(total,))
    grad_low, blocks = tied(grad_low, blocks)
    owned_first = line_reduce(blocks)
    boundary = placed_rows(place, grad_rows, away_rows(grad_low))
    total = line_total(total)
    grad_conv, grad_states_conv, grad_gate_gain, grad_heads, gain_total = plain_call(
        functools.partial(small_outputs_kernel, heads_half),
        place,
        (total,),
        [((5, units), f32), ((5, 2 * STATE), f32), ((1, units), f32), ((3, 2 * heads_half), f32), ((1, width), f32)],
    )

    others = jnp.where(on_first, owned_second, owned_first)
    own_states, other_states = by_layer(owned_first[:, half : half + STATE], owned_second[:, half : half + STATE])
    grad_zx, grad_bc, grad_dt, grad_out_w = plain_call(
        owned_kernel,
        place,
        (owned_first, owned_second, swapped(others, "section"), y_swapped(own_states), far_swapped(other_states)),
        [((block_rows, 2, units), f32)] + [((block_rows, columns), f32) for columns in (2 * STATE, 2 * heads_half, units)],
        (boundary, layer_outputs, grad_conv),
    )
    return (
        layer_outputs[None],
        boundary[None],
        lax.dynamic_slice_in_dim(gain_total, rank * block_rows, block_rows, 1),
        grad_zx[None],
        grad_bc[None],
        grad_dt[None],
        grad_conv[None],
        grad_states_conv[None],
        grad_heads[1:2],
        grad_heads[2:3],
        grad_heads[0:1],
        grad_gate_gain,
        grad_out_w.T[None],
    )


def solution(mesh):
    placed = (
        P(None, ("dp", "tensor"), None),
        P(None, ("dp", "tensor"), None),
        P(None, "dp", None),
        P(),
        P("section", "dp"),
        P("section", "dp", None, "tensor"),
        P("section", "dp", None),
        P("section", "dp", "tensor"),
        P("section", None, "tensor"),
        P("section", None, None),
        P("section", None),
        P("section", None),
        P("section", None),
        P("section", "tensor"),
        P("section", "tensor", "dp"),
    )
    return jax.shard_map(
        body,
        mesh=mesh,
        in_specs=placed,
        out_specs=(
            P("section", None, ("dp", "tensor"), None),
            P("section", None, ("dp", "tensor"), None),
            P("section", "dp"),
            P("section", "dp", None, "tensor"),
            P("section", "dp", None),
            P("section", "dp", "tensor"),
            P("section", None, "tensor"),
            P("section", None, None),
            P("section", "tensor"),
            P("section", "tensor"),
            P("section", "tensor"),
            P("section", "tensor"),
            P("section", "tensor", "dp"),
        ),
        check_vma=False,
    )
```

profile of v0, /device:TPU:0, one launch (start us, length us, event | category | flops | bytes accessed | tf_op | source)
XLA Modules:
  0.0 406.3 jit_solution(1636119136971597073)
XLA Ops:
  7.9 3.1 shard_map.291
  12.6 2.6 collective-permute-start.1
  15.9 1.9 shard_map.292
  18.4 17.8 %all_gather.9.refs_2_.refs_3_ = bf16[384,640]{1,0:T(8,128)(2,1)} all-gather(bf16[96,640]{1,0:T(8,128)(2,1)} %get-tuple-element.223), channel_id=1, replica_groups={{0,4,8,12},{2,6,10,14},{1,5,9,13},{3,7,11,15},{16,20,24,28},{18,22,26,3..., dimensions={0}, use_global_device_ids=true | all-gather | bytes 614400 | tf_op jit(solution)/shard_map/all_gather | solution.py:980
  36.3 1.6 collective-permute-start.5
  40.5 1.9 shard_map.293
  44.2 2.1 shard_map.294
  46.3 5.7 %collective-permute-done.8.refs_4_ = bf16[96,768]{1,0:T(8,128)(2,1)} collective-permute-done((bf16[96,768]{1,0:T(8,128)(2,1)}, bf16[96,768]{1,0:T(8,128)(2,1)}, u32[]{:S(2)}, u32[]{:S(2)}) %collective-permute-start.8) | collective-permute-done | bytes 147488 | tf_op jit(solution)/shard_map/ppermute | solution.py:974
  52.3 1.7 slice.45
  55.5 1.7 slice.44
  57.2 1.7 collective-permute-start.6
  60.0 1.8 maximum_select_fusion.1.refs_0_.refs_1_.h_ref
  61.8 2.0 shard_map.295
  64.4 2.3 shard_map.297
  70.7 17.4 %shard_map.296 = (f32[8,768]{1,0:T(8,128)}, bf16[1024,768]{1,0:T(8,128)(2,1)}, f32[1024,768]{1,0:T(8,128)}, f32[1024,768]{1,0:T(8,128)}, f32[1024,768]{1,0:T(8,1...) custom-call(s32[4]{0:T(128)} %pad_add_fusion.place_ref.refs_0_, ...), custom_call_target="tpu_custom_call" | custom-call | flops 2000000000 | bytes 500000 | tf_op jit(solution)/shard_map/pallas_call | solution.py:477
  88.1 4.3 %collective-permute-done.14.refs_6_.refs_5_ = bf16[384,640]{1,0:T(8,128)(2,1)} collective-permute-done((bf16[384,640]{1,0:T(8,128)(2,1)}, bf16[384,640]{1,0:T(8,128)(2,1)}, u32[]{:S(2)}, u32[]{:S(2)}) %collective-permute-start.14) | collective-permute-done | bytes 491552 | tf_op jit(solution)/shard_map/ppermute | solution.py:930
  93.6 1.9 slice.35
  96.2 1.6 collective-permute-start.16
  98.5 5.3 %collective-permute-done.16.refs_4_.refs_15_ = bf16[192,768]{1,0:T(8,128)(2,1)S(1)} collective-permute-done((bf16[192,768]{1,0:T(8,128)(2,1)}, bf16[192,768]{1,0:T(8,128)(2,1)S(1)}, u32[]{:S(2)}, u32[]{:S(2)}) %collective-permute-start.16) | collective-permute-done | bytes 294944 | tf_op jit(solution)/shard_map/ppermute | solution.py:974
  105.3 7.5 %shard_map.298 = (f32[1024,768]{1,0:T(8,128)}, bf16[1024,896]{1,0:T(8,128)(2,1)}) custom-call(s32[4]{0:T(128)} %pad_add_fusion.place_ref.refs_0_, bf16[1024,768]{1,0:T(8,128)(2,1)} %get-tuple-element.256.normed_ref.refs_8_, f32[1024,768]{1,0:T(8,128)} %get-tuple-element.257.y_ref.refs_10_.refs_16_, bf16[384,768]{1,0:T(8,128)(2,1)} %get-tuple-element.258.refs_0_.refs_11_, ...), custom_call_target="tpu_custom_call" | custom-call | flops 1000000000 | bytes 500000 | tf_op jit(solution)/shard_map/pallas_call | solution.py:477
  112.8 4.1 %collective-permute-done.17.refs_3_.refs_2_ = bf16[1024,896]{1,0:T(8,128)(2,1)} collective-permute-done((bf16[1024,896]{1,0:T(8,128)(2,1)}, bf16[1024,896]{1,0:T(8,128)(2,1)}, u32[]{:S(2)}, u32[]{:S(2)}) %collective-permute-start.17) | collective-permute-done | bytes 1835040 | tf_op jit(solution)/shard_map/ppermute | solution.py:930
  122.8 5.4 %collective-permute-done.19.refs_8_.refs_7_ = bf16[192,640]{1,0:T(8,128)(2,1)S(1)} collective-permute-done((bf16[192,640]{1,0:T(8,128)(2,1)S(1)}, bf16[192,640]{1,0:T(8,128)(2,1)S(1)}, u32[]{:S(2)}, u32[]{:S(2)}) %collective-permute-start.19) | collective-permute-done | bytes 245792 | tf_op jit(solution)/shard_map/ppermute | solution.py:974
  128.2 14.7 %collective-permute-done.18.refs_7_.refs_6_ = bf16[192,640]{1,0:T(8,128)(2,1)S(1)} collective-permute-done((bf16[192,640]{1,0:T(8,128)(2,1)S(1)}, bf16[192,640]{1,0:T(8,128)(2,1)S(1)}, u32[]{:S(2)}, u32[]{:S(2)}) %collective-permute-start.18) | collective-permute-done | bytes 245792 | tf_op jit(solution)/shard_map/ppermute | solution.py:930
  143.6 19.0 %shard_map.299 = (bf16[1024,768]{1,0:T(8,128)(2,1)}, f32[8,768]{1,0:T(8,128)}, bf16[1024,768]{1,0:T(8,128)(2,1)}, f32[1024,768]{1,0:T(8,128)}, f32[1024,768]{1,0...) custom-call(s32[4]{0:T(128)} %pad_add_fusion.place_ref.refs_0_, ...), custom_call_target="tpu_custom_call" | custom-call | flops 2000000000 | bytes 500000 | tf_op jit(solution)/shard_map/pallas_call | solution.py:477
  162.8 7.4 %shard_map.300 = (f32[1024,768]{1,0:T(8,128)}, bf16[1024,896]{1,0:T(8,128)(2,1)}) custom-call(s32[4]{0:T(128)} %pad_add_fusion.place_ref.refs_0_, bf16[1024,768]{1,0:T(8,128)(2,1)} %get-tuple-element.286.normed_ref.refs_5_, f32[1024,768]{1,0:T(8,128)} %get-tuple-element.287.y_ref.refs_7_.refs_16_, ...), custom_call_target="tpu_custom_call" | custom-call | flops 1000000000 | bytes 500000 | tf_op jit(solution)/shard_map/pallas_call | solution.py:477
  172.3 1.9 maximum_select_fusion.refs_4_
  174.5 16.2 %shard_map.301 = (bf16[1024,768]{1,0:T(8,128)(2,1)}, f32[1024,768]{1,0:T(8,128)}, bf16[1024,768]{1,0:T(8,128)(2,1)}, f32[1024,768]{1,0:T(8,128)}, bf16[384,768]{...) custom-call(s32[4]{0:T(128)} %pad_add_fusion.place_ref.refs_0_, ...), custom_call_target="tpu_custom_call" | custom-call | flops 2000000000 | bytes 500000 | tf_op jit(solution)/shard_map/pallas_call | solution.py:477
  194.9 29.9 %shard_map.302 = (bf16[1024,1280]{1,0:T(8,128)(2,1)}, bf16[1024,768]{1,0:T(8,128)(2,1)}, f32[8,768]{1,0:T(8,128)}, f32[8,256]{1,0:T(8,128)}) custom-call(s32[4]{0:T(128)} %pad_add_fusion.place_ref.refs_0_, bf16[1024,768]{1,0:T(8,128)(2,1)} %get-tuple-element.297.refs_1_, f32[1024,768]{1,0:T(8,128)} %get-tuple-element.298.refs_2_, ...), custom_call_target="tpu_custom_call" | custom-call | flops 3000000000 | bytes 500000 | tf_op jit(solution)/shard_map/pallas_call | solution.py:477
  225.8 6.5 %shard_map.303 = (bf16[384,640]{1,0:T(8,128)(2,1)}, bf16[384,640]{1,0:T(8,128)(2,1)}, bf16[384,640]{1,0:T(8,128)(2,1)}, bf16[192,640]{1,0:T(8,128)(2,1)}, bf16[192,640]{1,0:T(8,128)(2,1)}) custom-call(s32[4]{0:T(128)} %pad_add_fusion.place_ref.refs_0_, bf16[1024,768]{1,0:T(8,128)(2,1)} %get-tuple-element.286.normed_ref.refs_5_, ...), custom_call_target="tpu_custom_call" | custom-call | flops 500000000 | bytes 500000 | tf_op jit(solution)/shard_map/pallas_call | solution.py:477
  234.1 17.0 %shard_map.304 = (f32[1024,768]{1,0:T(8,128)}, bf16[1024,768]{1,0:T(8,128)(2,1)}, f32[1024,768]{1,0:T(8,128)}, bf16[384,768]{1,0:T(8,128)(2,1)}, bf16[384,768]{1...) custom-call(s32[4]{0:T(128)} %pad_add_fusion.place_ref.refs_0_, ...), custom_call_target="tpu_custom_call" | custom-call | flops 2000000000 | bytes 500000 | tf_op jit(solution)/shard_map/pallas_call | solution.py:477
  251.9 3.5 shard_map.306
  259.5 29.9 %shard_map.305 = (bf16[1024,1280]{1,0:T(8,128)(2,1)}, bf16[1024,768]{1,0:T(8,128)(2,1)}, f32[8,768]{1,0:T(8,128)}, f32[8,256]{1,0:T(8,128)}) custom-call(s32[4]{0:T(128)} %pad_add_fusion.place_ref.refs_0_, bf16[1024,768]{1,0:T(8,128)(2,1)} %get-tuple-element.341.refs_1_, f32[1024,768]{1,0:T(8,128)} %get-tuple-element.342.refs_2_, ...), custom_call_target="tpu_custom_call" | custom-call | flops 3000000000 | bytes 500000 | tf_op jit(solution)/shard_map/pallas_call | solution.py:477
  290.6 6.5 %shard_map.307 = (bf16[384,640]{1,0:T(8,128)(2,1)}, bf16[384,640]{1,0:T(8,128)(2,1)}, bf16[384,640]{1,0:T(8,128)(2,1)}, bf16[192,640]{1,0:T(8,128)(2,1)}, bf16[192,640]{1,0:T(8,128)(2,1)}) custom-call(s32[4]{0:T(128)} %pad_add_fusion.place_ref.refs_0_, bf16[1024,768]{1,0:T(8,128)(2,1)} %get-tuple-element.256.normed_ref.refs_8_, ...), custom_call_target="tpu_custom_call" | custom-call | flops 500000000 | bytes 500000 | tf_op jit(solution)/shard_map/pallas_call | solution.py:477
  297.1 3.9 shard_map.317
  303.4 2.5 shard_map.313
  307.7 6.6 %shard_map.308 = (f32[1024,768]{1,0:T(8,128)}, bf16[1024,768]{1,0:T(8,128)(2,1)}, f32[8,768]{1,0:T(8,128)}) custom-call(s32[4]{0:T(128)} %pad_add_fusion.place_ref.refs_0_, bf16[1024,768]{1,0:T(8,128)(2,1)} %get-tuple-element.377.own_ref, bf16[1024,768]{1,0:T(8,128)(2,1)} %copy-done.3, bf16[1024,768]{1,0:T(8,128)(2,1)} %maximum_select_fusion.1.refs_0_.refs_1_.h_ref, ...), custom_call_target="tpu_custom_call" | custom-call | flops 30000000 | bytes 500000 | tf_op jit(solution)/shard_map/pallas_call | solution.py:477
  315.1 2.4 shard_map.312
  321.9 12.9 %collective-permute-done.36.away_ref = f32[32,768]{1,0:T(8,128)S(1)} collective-permute-done((f32[32,768]{1,0:T(8,128)}, f32[32,768]{1,0:T(8,128)S(1)}, u32[]{:S(2)}, u32[]{:S(2)}) %collective-permute-start.36) | collective-permute-done | bytes 98336 | tf_op jit(solution)/shard_map/ppermute | solution.py:930
  335.4 1.6 shard_map.311
  339.4 3.2 collective-permute-done.38
  345.2 3.2 shard_map.314
  349.8 4.5 %collective-permute-start.44 = (f32[32,384]{1,0:T(8,128)S(1)}, f32[32,384]{1,0:T(8,128)S(1)}, u32[]{:S(2)}, u32[]{:S(2)}) collective-permute-start(f32[32,384]{1,0:T(8,128)S(1)} %copy-done.15), channel_id=1, source_target_pairs={{0,4},{2,6},{4,8},{6,10},{8,12},{10,14},{1,5},{3,7},{5,9},{7,11},{... | collective-permute-start | bytes 147464 | tf_op jit(solution)/shard_map/ppermute | solution.py:990
  358.8 3.4 shard_map.309.refs_1_
  363.4 4.5 %collective-permute-done.48 = f32[32,384]{1,0:T(8,128)S(1)} collective-permute-done((f32[32,384]{1,0:T(8,128)S(1)}, f32[32,384]{1,0:T(8,128)S(1)}, u32[]{:S(2)}, u32[]{:S(2)}) %collective-permute-start.48) | collective-permute-done | bytes 49184 | tf_op jit(solution)/shard_map/ppermute | solution.py:990
  373.8 3.5 reduce-scatter.3.cloned.1.call-done.refs_3_
  383.8 6.1 %collective-permute-done.43.away_ref = bf16[512,768]{1,0:T(8,128)(2,1)} collective-permute-done((bf16[512,768]{1,0:T(8,128)(2,1)S(1)}, bf16[512,768]{1,0:T(8,128)(2,1)}, u32[]{:S(2)}, u32[]{:S(2)}) %collective-permute-start.43) | collective-permute-done | bytes 786464 | tf_op jit(solution)/shard_map/ppermute | solution.py:930
  389.9 4.3 %shard_map.315.refs_0_ = f32[2,512,768]{2,1,0:T(8,128)} custom-call(s32[4]{0:T(128)} %pad_add_fusion.place_ref.refs_0_, f32[1024,768]{1,0:T(8,128)} %get-tuple-element.391.own_ref, bf16[512,768]{1,0:T(8,128)(2,1)} %collective-permute-done.43.away_ref), custom_call_target="tpu_custom_call" | custom-call | bytes 500000 | tf_op jit(solution)/shard_map/pallas_call | solution.py:641
  395.5 2.3 shard_map.318
  (203 shorter events, 78.7 us)
Async XLA Ops:
  7.2 57.2 %all-gather.3.cloned.1.call-start = ((), (), s32[]{:S(2)}) async-start(), calls=%async_computation.2 | async-start | bytes 1351680 | tf_op jit(solution)/shard_map/all_gather | solution.py:980
  12.6 23.6 %collective-permute-start.1 = (bf16[256,768]{1,0:T(8,128)(2,1)S(1)}, bf16[256,768]{1,0:T(8,128)(2,1)}, u32[]{:S(2)}, u32[]{:S(2)}) collective-permute-start(bf16[256,768]{1,0:T(8,128)(2,1)S(1)} %dynamic-slice_bitcast_fusion.3), channel_id=1, source_target_pairs={{0,1},{1,0},{2,3},{3,2},{4,5},{5,4},{6,7},{7,6},{8,9},{9,8},{10,11... | collective-permute-start | bytes 1179656 | tf_op jit(solution)/shard_map/ppermute | solution.py:930
  17.8 18.4 %collective-permute-start.2 = (bf16[32,384]{1,0:T(8,128)(2,1)}, bf16[32,384]{1,0:T(8,128)(2,1)S(1)}, u32[]{:S(2)}, u32[]{:S(2)}) collective-permute-start(bf16[32,384]{1,0:T(8,128)(2,1)} %get-tuple-element.224), channel_id=1, source_target_pairs={{0,1},{1,0},{2,3},{3,2},{4,5},{5,4},{6,7},{7,6},{8,9},{9,8},{10,11... | collective-permute-start | bytes 73736 | tf_op jit(solution)/shard_map/ppermute | solution.py:930
  36.2 126.6 %all-gather.5.cloned.1.call-start = ((), (), s32[]{:S(2)}) async-start(), calls=%async_computation.3 | async-start | bytes 2949120 | tf_op jit(solution)/shard_map/all_gather | solution.py:980
  36.3 16.1 %collective-permute-start.5 = (bf16[384,640]{1,0:T(8,128)(2,1)}, bf16[384,640]{1,0:T(8,128)(2,1)}, u32[]{:S(2)}, u32[]{:S(2)}) collective-permute-start(bf16[384,640]{1,0:T(8,128)(2,1)} %all_gather.9.refs_2_.refs_3_), channel_id=1, source_target_pairs={{0,1},{1,0},{2,3},{3,2},{4,5},{5,4},{6,7},{7,6},{8,9},{9,8},{10,11... | collective-permute-start | bytes 1474568 | tf_op jit(solution)/shard_map/ppermute | solution.py:930
  37.9 17.6 %collective-permute-start.4 = (bf16[384,640]{1,0:T(8,128)(2,1)}, bf16[384,640]{1,0:T(8,128)(2,1)}, u32[]{:S(2)}, u32[]{:S(2)}) collective-permute-start(bf16[384,640]{1,0:T(8,128)(2,1)} %all_gather.9.refs_2_.refs_3_), channel_id=1, source_target_pairs={{0,2},{2,0},{4,6},{6,4},{8,10},{10,8},{12,14},{14,12},{1,3},{3,1},... | collective-permute-start | bytes 1474568 | tf_op jit(solution)/shard_map/ppermute | solution.py:974
  39.4 19.5 %collective-permute-start.3 = (bf16[256,768]{1,0:T(8,128)(2,1)}, bf16[256,768]{1,0:T(8,128)(2,1)}, u32[]{:S(2)}, u32[]{:S(2)}) collective-permute-start(bf16[256,768]{1,0:T(8,128)(2,1)} %collective-permute-done.1), channel_id=1, source_target_pairs={{0,16},{16,0},{1,17},{17,1},{2,18},{18,2},{3,19},{19,3},{4,20},{20... | collective-permute-start | bytes 1179656 | tf_op jit(solution)/shard_map/ppermute | solution.py:930
  39.4 12.6 %collective-permute-start.8 = (bf16[96,768]{1,0:T(8,128)(2,1)}, bf16[96,768]{1,0:T(8,128)(2,1)}, u32[]{:S(2)}, u32[]{:S(2)}) collective-permute-start(bf16[96,768]{1,0:T(8,128)(2,1)} %get-tuple-element.233.refs_3_), channel_id=1, source_target_pairs={{0,2},{2,0},{4,6},{6,4},{8,10},{10,8},{12,14},{14,12},{1,3},{3,1},... | collective-permute-start | bytes 442376 | tf_op jit(solution)/shard_map/ppermute | solution.py:974
  43.7 18.2 %collective-permute-start.9 = (bf16[96,768]{1,0:T(8,128)(2,1)S(1)}, bf16[96,768]{1,0:T(8,128)(2,1)}, u32[]{:S(2)}, u32[]{:S(2)}) collective-permute-start(bf16[96,768]{1,0:T(8,128)(2,1)S(1)} %copy-done.26), channel_id=1, source_target_pairs={{0,1},{1,0},{2,3},{3,2},{4,5},{5,4},{6,7},{7,6},{8,9},{9,8},{10,11... | collective-permute-start | bytes 442376 | tf_op jit(solution)/shard_map/ppermute | solution.py:930
  52.0 9.8 %collective-permute-start.10 = (bf16[96,768]{1,0:T(8,128)(2,1)}, bf16[96,768]{1,0:T(8,128)(2,1)}, u32[]{:S(2)}, u32[]{:S(2)}) collective-permute-start(bf16[96,768]{1,0:T(8,128)(2,1)} %collective-permute-done.8.refs_4_), channel_id=1, source_target_pairs={{0,1},{1,0},{2,3},{3,2},{4,5},{5,4},{6,7},{7,6},{8,9},{9,8},{10,11... | collective-permute-start | bytes 442376 | tf_op jit(solution)/shard_map/ppermute | solution.py:930
  54.0 9.8 %collective-permute-start.7 = (bf16[192,640]{1,0:T(8,128)(2,1)}, bf16[192,640]{1,0:T(8,128)(2,1)}, u32[]{:S(2)}, u32[]{:S(2)}) collective-permute-start(bf16[192,640]{1,0:T(8,128)(2,1)} %slice.45), channel_id=1, source_target_pairs={{0,2},{2,0},{4,6},{6,4},{8,10},{10,8},{12,14},{14,12},{1,3},{3,1},... | collective-permute-start | bytes 737288 | tf_op jit(solution)/shard_map/ppermute | solution.py:974
  57.2 6.7 %collective-permute-start.6 = (bf16[192,640]{1,0:T(8,128)(2,1)}, bf16[192,640]{1,0:T(8,128)(2,1)}, u32[]{:S(2)}, u32[]{:S(2)}) collective-permute-start(bf16[192,640]{1,0:T(8,128)(2,1)} %slice.44), channel_id=1, source_target_pairs={{0,1},{1,0},{2,3},{3,2},{4,5},{5,4},{6,7},{7,6},{8,9},{9,8},{10,11... | collective-permute-start | bytes 737288 | tf_op jit(solution)/shard_map/ppermute | solution.py:930
  66.6 26.9 %collective-permute-start.12 = (bf16[384,768]{1,0:T(8,128)(2,1)}, bf16[384,768]{1,0:T(8,128)(2,1)S(1)}, u32[]{:S(2)}, u32[]{:S(2)}) collective-permute-start(bf16[384,768]{1,0:T(8,128)(2,1)} %get-tuple-element.258.refs_0_.refs_11_), channel_id=1, source_target_pairs={{0,1},{1,0},{2,3},{3,2},{4,5},{5,4},{6,7},{7,6},{8,9},{9,8},{10,11... | collective-permute-start | bytes 1769480 | tf_op jit(solution)/shard_map/ppermute | solution.py:930
  68.1 25.4 %collective-permute-start.11 = (bf16[384,768]{1,0:T(8,128)(2,1)}, bf16[384,768]{1,0:T(8,128)(2,1)}, u32[]{:S(2)}, u32[]{:S(2)}) collective-permute-start(bf16[384,768]{1,0:T(8,128)(2,1)} %get-tuple-element.258.refs_0_.refs_11_), channel_id=1, source_target_pairs={{0,2},{2,0},{4,6},{6,4},{8,10},{10,8},{12,14},{14,12},{1,3},{3,1},... | collective-permute-start | bytes 1769480 | tf_op jit(solution)/shard_map/ppermute | solution.py:974
  69.7 22.7 %collective-permute-start.14 = (bf16[384,640]{1,0:T(8,128)(2,1)}, bf16[384,640]{1,0:T(8,128)(2,1)}, u32[]{:S(2)}, u32[]{:S(2)}) collective-permute-start(bf16[384,640]{1,0:T(8,128)(2,1)} %get-tuple-element.268.refs_4_.refs_3_), channel_id=1, source_target_pairs={{0,1},{1,0},{2,3},{3,2},{4,5},{5,4},{6,7},{7,6},{8,9},{9,8},{10,11... | collective-permute-start | bytes 1474568 | tf_op jit(solution)/shard_map/ppermute | solution.py:930
  70.1 23.4 %collective-permute-start.13 = (bf16[384,640]{1,0:T(8,128)(2,1)}, bf16[384,640]{1,0:T(8,128)(2,1)}, u32[]{:S(2)}, u32[]{:S(2)}) collective-permute-start(bf16[384,640]{1,0:T(8,128)(2,1)} %get-tuple-element.268.refs_4_.refs_3_), channel_id=1, source_target_pairs={{0,2},{2,0},{4,6},{6,4},{8,10},{10,8},{12,14},{14,12},{1,3},{3,1},... | collective-permute-start | bytes 1474568 | tf_op jit(solution)/shard_map/ppermute | solution.py:974
  96.2 7.6 %collective-permute-start.16 = (bf16[192,768]{1,0:T(8,128)(2,1)}, bf16[192,768]{1,0:T(8,128)(2,1)S(1)}, u32[]{:S(2)}, u32[]{:S(2)}) collective-permute-start(bf16[192,768]{1,0:T(8,128)(2,1)} %slice.36), channel_id=1, source_target_pairs={{0,2},{2,0},{4,6},{6,4},{8,10},{10,8},{12,14},{14,12},{1,3},{3,1},... | collective-permute-start | bytes 884744 | tf_op jit(solution)/shard_map/ppermute | solution.py:974
  97.8 7.4 %collective-permute-start.15 = (bf16[192,768]{1,0:T(8,128)(2,1)}, bf16[192,768]{1,0:T(8,128)(2,1)}, u32[]{:S(2)}, u32[]{:S(2)}) collective-permute-start(bf16[192,768]{1,0:T(8,128)(2,1)} %slice.35), channel_id=1, source_target_pairs={{0,1},{1,0},{2,3},{3,2},{4,5},{5,4},{6,7},{7,6},{8,9},{9,8},{10,11... | collective-permute-start | bytes 884744 | tf_op jit(solution)/shard_map/ppermute | solution.py:930
  98.2 275.6 %reduce-scatter.5.cloned.1.call-start = ((), (), s32[]{:S(2)}) async-start(), calls=%async_computation.5 | async-start | bytes 1351680 | tf_op jit(solution)/shard_map/reduce_scatter | solution.py:983
  117.9 44.8 %collective-permute-start.20 = (f32[256,768]{1,0:T(8,128)}, f32[256,768]{1,0:T(8,128)}, u32[]{:S(2)}, u32[]{:S(2)}) collective-permute-start(f32[256,768]{1,0:T(8,128)} %dynamic-slice_bitcast_fusion.1), channel_id=1, source_target_pairs={{0,1},{1,0},{2,3},{3,2},{4,5},{5,4},{6,7},{7,6},{8,9},{9,8},{10,11... | collective-permute-start | bytes 2359304 | tf_op jit(solution)/shard_map/ppermute | solution.py:930
  120.5 7.8 %collective-permute-start.19 = (bf16[192,640]{1,0:T(8,128)(2,1)S(1)}, bf16[192,640]{1,0:T(8,128)(2,1)S(1)}, u32[]{:S(2)}, u32[]{:S(2)}) collective-permute-start(bf16[192,640]{1,0:T(8,128)(2,1)S(1)} %slice.38), channel_id=1, source_target_pairs={{0,2},{2,0},{4,6},{6,4},{8,10},{10,8},{12,14},{14,12},{1,3},{3,1},... | collective-permute-start | bytes 737288 | tf_op jit(solution)/shard_map/ppermute | solution.py:974
  121.5 21.5 %collective-permute-start.18 = (bf16[192,640]{1,0:T(8,128)(2,1)S(1)}, bf16[192,640]{1,0:T(8,128)(2,1)S(1)}, u32[]{:S(2)}, u32[]{:S(2)}) collective-permute-start(bf16[192,640]{1,0:T(8,128)(2,1)S(1)} %slice.37), channel_id=1, source_target_pairs={{0,1},{1,0},{2,3},{3,2},{4,5},{5,4},{6,7},{7,6},{8,9},{9,8},{10,11... | collective-permute-start | bytes 737288 | tf_op jit(solution)/shard_map/ppermute | solution.py:930
  162.7 7.5 %collective-permute-start.21 = (f32[256,768]{1,0:T(8,128)}, f32[256,768]{1,0:T(8,128)}, u32[]{:S(2)}, u32[]{:S(2)}) collective-permute-start(f32[256,768]{1,0:T(8,128)} %collective-permute-done.20), channel_id=1, source_target_pairs={{0,16},{16,0},{1,17},{17,1},{2,18},{18,2},{3,19},{19,3},{4,20},{20... | collective-permute-start | bytes 2359304 | tf_op jit(solution)/shard_map/ppermute | solution.py:930
  191.9 32.9 %collective-permute-start.25 = (bf16[512,768]{1,0:T(8,128)(2,1)S(1)}, bf16[512,768]{1,0:T(8,128)(2,1)S(1)}, u32[]{:S(2)}, u32[]{:S(2)}) collective-permute-start(bf16[512,768]{1,0:T(8,128)(2,1)S(1)} %constant_dynamic-slice_fusion.2), channel_id=1, source_target_pairs={{0,1},{1,0},{2,3},{3,2},{4,5},{5,4},{6,7},{7,6},{8,9},{9,8},{10,11... | collective-permute-start | bytes 2359304 | tf_op jit(solution)/shard_map/ppermute | solution.py:930
  192.6 32.2 %collective-permute-start.23 = (bf16[192,768]{1,0:T(8,128)(2,1)}, bf16[192,768]{1,0:T(8,128)(2,1)S(1)}, u32[]{:S(2)}, u32[]{:S(2)}) collective-permute-start(bf16[192,768]{1,0:T(8,128)(2,1)} %get-tuple-element.312), channel_id=1, source_target_pairs={{0,1},{1,0},{2,3},{3,2},{4,5},{5,4},{6,7},{7,6},{8,9},{9,8},{10,11... | collective-permute-start | bytes 884744 | tf_op jit(solution)/shard_map/ppermute | solution.py:930
  194.0 30.8 %collective-permute-start.24 = (bf16[192,768]{1,0:T(8,128)(2,1)}, bf16[192,768]{1,0:T(8,128)(2,1)S(1)}, u32[]{:S(2)}, u32[]{:S(2)}) collective-permute-start(bf16[192,768]{1,0:T(8,128)(2,1)} %get-tuple-element.313), channel_id=1, source_target_pairs={{0,2},{2,0},{4,6},{6,4},{8,10},{10,8},{12,14},{14,12},{1,3},{3,1},... | collective-permute-start | bytes 884744 | tf_op jit(solution)/shard_map/ppermute | solution.py:974
  232.3 18.8 %collective-permute-start.27 = (bf16[192,640]{1,0:T(8,128)(2,1)}, bf16[192,640]{1,0:T(8,128)(2,1)S(1)}, u32[]{:S(2)}, u32[]{:S(2)}) collective-permute-start(bf16[192,640]{1,0:T(8,128)(2,1)} %get-tuple-element.339), channel_id=1, source_target_pairs={{0,1},{1,0},{2,3},{3,2},{4,5},{5,4},{6,7},{7,6},{8,9},{9,8},{10,11... | collective-permute-start | bytes 737288 | tf_op jit(solution)/shard_map/ppermute | solution.py:930
  233.1 18.1 %collective-permute-start.28 = (bf16[192,640]{1,0:T(8,128)(2,1)}, bf16[192,640]{1,0:T(8,128)(2,1)S(1)}, u32[]{:S(2)}, u32[]{:S(2)}) collective-permute-start(bf16[192,640]{1,0:T(8,128)(2,1)} %get-tuple-element.340), channel_id=1, source_target_pairs={{0,2},{2,0},{4,6},{6,4},{8,10},{10,8},{12,14},{14,12},{1,3},{3,1},... | collective-permute-start | bytes 737288 | tf_op jit(solution)/shard_map/ppermute | solution.py:974
  255.4 34.0 %collective-permute-start.29 = (bf16[384,1408]{1,0:T(8,128)(2,1)}, bf16[384,1408]{1,0:T(8,128)(2,1)S(1)}, u32[]{:S(2)}, u32[]{:S(2)}) collective-permute-start(bf16[384,1408]{1,0:T(8,128)(2,1)} %get-tuple-element.363), channel_id=1, source_target_pairs={{0,2},{2,0},{4,6},{6,4},{8,10},{10,8},{12,14},{14,12},{1,3},{3,1},... | collective-permute-start | bytes 3244040 | tf_op jit(solution)/shard_map/ppermute | solution.py:974
  256.4 33.1 %collective-permute-start.30 = (bf16[384,1408]{1,0:T(8,128)(2,1)}, bf16[384,1408]{1,0:T(8,128)(2,1)S(1)}, u32[]{:S(2)}, u32[]{:S(2)}) collective-permute-start(bf16[384,1408]{1,0:T(8,128)(2,1)} %get-tuple-element.364), channel_id=1, source_target_pairs={{0,1},{1,0},{2,3},{3,2},{4,5},{5,4},{6,7},{7,6},{8,9},{9,8},{10,11... | collective-permute-start | bytes 3244040 | tf_op jit(solution)/shard_map/ppermute | solution.py:930
  257.8 31.7 %collective-permute-start.31 = (bf16[192,768]{1,0:T(8,128)(2,1)S(1)}, bf16[192,768]{1,0:T(8,128)(2,1)S(1)}, u32[]{:S(2)}, u32[]{:S(2)}) collective-permute-start(bf16[192,768]{1,0:T(8,128)(2,1)S(1)} %copy-done.35), channel_id=1, source_target_pairs={{0,1},{1,0},{2,3},{3,2},{4,5},{5,4},{6,7},{7,6},{8,9},{9,8},{10,11... | collective-permute-start | bytes 884744 | tf_op jit(solution)/shard_map/ppermute | solution.py:930
  258.4 31.0 %collective-permute-start.32 = (bf16[192,768]{1,0:T(8,128)(2,1)S(1)}, bf16[192,768]{1,0:T(8,128)(2,1)S(1)}, u32[]{:S(2)}, u32[]{:S(2)}) collective-permute-start(bf16[192,768]{1,0:T(8,128)(2,1)S(1)} %copy-done.34), channel_id=1, source_target_pairs={{0,2},{2,0},{4,6},{6,4},{8,10},{10,8},{12,14},{14,12},{1,3},{3,1},... | collective-permute-start | bytes 884744 | tf_op jit(solution)/shard_map/ppermute | solution.py:974
  301.0 76.4 %reduce-scatter.3.cloned.1.call-start = ((), (), s32[]{:S(2)}) async-start(), calls=%async_computation.4 | async-start | bytes 1351680 | tf_op jit(solution)/shard_map/reduce_scatter | solution.py:983
  301.0 13.2 %collective-permute-start.34 = (bf16[192,640]{1,0:T(8,128)(2,1)S(1)}, bf16[192,640]{1,0:T(8,128)(2,1)S(1)}, u32[]{:S(2)}, u32[]{:S(2)}) collective-permute-start(bf16[192,640]{1,0:T(8,128)(2,1)S(1)} %copy-done.37), channel_id=1, source_target_pairs={{0,1},{1,0},{2,3},{3,2},{4,5},{5,4},{6,7},{7,6},{8,9},{9,8},{10,11... | collective-permute-start | bytes 737288 | tf_op jit(solution)/shard_map/ppermute | solution.py:930
  302.5 11.8 %collective-permute-start.35 = (bf16[192,640]{1,0:T(8,128)(2,1)S(1)}, bf16[192,640]{1,0:T(8,128)(2,1)S(1)}, u32[]{:S(2)}, u32[]{:S(2)}) collective-permute-start(bf16[192,640]{1,0:T(8,128)(2,1)S(1)} %copy-done.36), channel_id=1, source_target_pairs={{0,2},{2,0},{4,6},{6,4},{8,10},{10,8},{12,14},{14,12},{1,3},{3,1},... | collective-permute-start | bytes 737288 | tf_op jit(solution)/shard_map/ppermute | solution.py:974
  305.9 37.3 %collective-permute-start.41 = (bf16[384,768]{1,0:T(8,128)(2,1)}, bf16[384,768]{1,0:T(8,128)(2,1)S(1)}, u32[]{:S(2)}, u32[]{:S(2)}) collective-permute-start(bf16[384,768]{1,0:T(8,128)(2,1)} %get-tuple-element.412), channel_id=1, source_target_pairs={{0,2},{2,0},{4,6},{6,4},{8,10},{10,8},{12,14},{14,12},{1,3},{3,1},... | collective-permute-start | bytes 1769480 | tf_op jit(solution)/shard_map/ppermute | solution.py:974
  307.0 36.2 %collective-permute-start.42 = (bf16[384,768]{1,0:T(8,128)(2,1)}, bf16[384,768]{1,0:T(8,128)(2,1)S(1)}, u32[]{:S(2)}, u32[]{:S(2)}) collective-permute-start(bf16[384,768]{1,0:T(8,128)(2,1)} %get-tuple-element.413), channel_id=1, source_target_pairs={{0,1},{1,0},{2,3},{3,2},{4,5},{5,4},{6,7},{7,6},{8,9},{9,8},{10,11... | collective-permute-start | bytes 1769480 | tf_op jit(solution)/shard_map/ppermute | solution.py:930
  317.4 25.8 %collective-permute-start.39 = (bf16[384,640]{1,0:T(8,128)(2,1)}, bf16[384,640]{1,0:T(8,128)(2,1)S(1)}, u32[]{:S(2)}, u32[]{:S(2)}) collective-permute-start(bf16[384,640]{1,0:T(8,128)(2,1)} %get-tuple-element.406), channel_id=1, source_target_pairs={{0,2},{2,0},{4,6},{6,4},{8,10},{10,8},{12,14},{14,12},{1,3},{3,1},... | collective-permute-start | bytes 1474568 | tf_op jit(solution)/shard_map/ppermute | solution.py:974
  318.3 24.9 %collective-permute-start.40 = (bf16[384,640]{1,0:T(8,128)(2,1)}, bf16[384,640]{1,0:T(8,128)(2,1)S(1)}, u32[]{:S(2)}, u32[]{:S(2)}) collective-permute-start(bf16[384,640]{1,0:T(8,128)(2,1)} %get-tuple-element.407), channel_id=1, source_target_pairs={{0,1},{1,0},{2,3},{3,2},{4,5},{5,4},{6,7},{7,6},{8,9},{9,8},{10,11... | collective-permute-start | bytes 1474568 | tf_op jit(solution)/shard_map/ppermute | solution.py:930
  321.2 13.6 %collective-permute-start.36 = (f32[32,768]{1,0:T(8,128)}, f32[32,768]{1,0:T(8,128)S(1)}, u32[]{:S(2)}, u32[]{:S(2)}) collective-permute-start(f32[32,768]{1,0:T(8,128)} %shard_map.310.own_ref), channel_id=1, source_target_pairs={{0,1},{1,0},{2,3},{3,2},{4,5},{5,4},{6,7},{7,6},{8,9},{9,8},{10,11... | collective-permute-start | bytes 294920 | tf_op jit(solution)/shard_map/ppermute | solution.py:930
  349.8 7.1 %collective-permute-start.44 = (f32[32,384]{1,0:T(8,128)S(1)}, f32[32,384]{1,0:T(8,128)S(1)}, u32[]{:S(2)}, u32[]{:S(2)}) collective-permute-start(f32[32,384]{1,0:T(8,128)S(1)} %copy-done.15), channel_id=1, source_target_pairs={{0,4},{2,6},{4,8},{6,10},{8,12},{10,14},{1,5},{3,7},{5,9},{7,11},{... | collective-permute-start | bytes 147464 | tf_op jit(solution)/shard_map/ppermute | solution.py:990
  354.4 8.9 %collective-permute-start.47 = (f32[32,384]{1,0:T(8,128)S(1)}, f32[32,384]{1,0:T(8,128)S(1)}, u32[]{:S(2)}, u32[]{:S(2)}) collective-permute-start(f32[32,384]{1,0:T(8,128)S(1)} %collective-permute-done.45), channel_id=1, source_target_pairs={{8,4},{10,6},{4,0},{6,2},{9,5},{11,7},{5,1},{7,3},{24,20},{26,22},... | collective-permute-start | bytes 147464 | tf_op jit(solution)/shard_map/ppermute | solution.py:990
  356.8 11.0 %collective-permute-start.48 = (f32[32,384]{1,0:T(8,128)S(1)}, f32[32,384]{1,0:T(8,128)S(1)}, u32[]{:S(2)}, u32[]{:S(2)}) collective-permute-start(f32[32,384]{1,0:T(8,128)S(1)} %broadcast_select_fusion.7), channel_id=1, source_target_pairs={{4,12},{6,14},{8,0},{10,2},{5,13},{7,15},{9,1},{11,3},{20,28},{22,... | collective-permute-start | bytes 147464 | tf_op jit(solution)/shard_map/ppermute | solution.py:990
  358.1 9.8 %collective-permute-start.46 = (f32[32,384]{1,0:T(8,128)S(1)}, f32[32,384]{1,0:T(8,128)S(1)}, u32[]{:S(2)}, u32[]{:S(2)}) collective-permute-start(f32[32,384]{1,0:T(8,128)S(1)} %collective-permute-done.44), channel_id=1, source_target_pairs={{4,8},{6,10},{8,12},{10,14},{5,9},{7,11},{9,13},{11,15},{20,24},{2... | collective-permute-start | bytes 147464 | tf_op jit(solution)/shard_map/ppermute | solution.py:990
  372.5 17.4 %collective-permute-start.43 = (bf16[512,768]{1,0:T(8,128)(2,1)S(1)}, bf16[512,768]{1,0:T(8,128)(2,1)}, u32[]{:S(2)}, u32[]{:S(2)}) collective-permute-start(bf16[512,768]{1,0:T(8,128)(2,1)S(1)} %constant_dynamic-slice_fusion.1), channel_id=1, source_target_pairs={{0,1},{1,0},{2,3},{3,2},{4,5},{5,4},{6,7},{7,6},{8,9},{9,8},{10,11... | collective-permute-start | bytes 2359304 | tf_op jit(solution)/shard_map/ppermute | solution.py:930
  378.3 15.9 %collective-permute-start.49 = (bf16[96,1408]{1,0:T(8,128)(2,1)S(1)}, bf16[96,1408]{1,0:T(8,128)(2,1)S(1)}, u32[]{:S(2)}, u32[]{:S(2)}) collective-permute-start(bf16[96,1408]{1,0:T(8,128)(2,1)S(1)} %broadcast_select_fusion.4), channel_id=1, source_target_pairs={{0,16},{16,0},{1,17},{17,1},{2,18},{18,2},{3,19},{19,3},{4,20},{20... | collective-permute-start | bytes 811016 | tf_op jit(solution)/shard_map/ppermute | solution.py:930
  379.2 15.0 %collective-permute-start.51 = (bf16[96,128]{1,0:T(8,128)(2,1)S(1)}, bf16[96,128]{1,0:T(8,128)(2,1)S(1)}, u32[]{:S(2)}, u32[]{:S(2)}) collective-permute-start(bf16[96,128]{1,0:T(8,128)(2,1)S(1)} %get-tuple-element.446), channel_id=1, source_target_pairs={{0,17},{1,16},{16,1},{17,0},{2,19},{3,18},{18,3},{19,2},{4,21},{5,... | collective-permute-start | bytes 73736 | tf_op jit(solution)/shard_map/ppermute | solution.py:935
  380.8 13.5 %collective-permute-start.50 = (bf16[96,128]{1,0:T(8,128)(2,1)S(1)}, bf16[96,128]{1,0:T(8,128)(2,1)S(1)}, u32[]{:S(2)}, u32[]{:S(2)}) collective-permute-start(bf16[96,128]{1,0:T(8,128)(2,1)S(1)} %get-tuple-element.447), channel_id=1, source_target_pairs={{0,1},{1,0},{2,3},{3,2},{4,5},{5,4},{6,7},{7,6},{8,9},{9,8},{10,11... | collective-permute-start | bytes 73736 | tf_op jit(solution)/shard_map/ppermute | solution.py:930
  (46 other events, 401.6 us)
Sparse Core Ops, SparseCore 0:
  36.4 27.9 all-gather.2
  98.4 49.4 all-gather.4
  301.1 27.2 reduce-scatter.4
  348.6 28.7 reduce-scatter.2
where the time goes:
time: 414 us; the launch traced here: 406 us
  Pallas kernels  207 us (50%)
  waiting for transfers between devices  76.4 us (18%)
  starting transfers between devices  50.8 us (12%)
  local copies, waits for them, and re-layouts  29.1 us (7%)
  blocking collectives  17.8 us (4%)
  between operations  14.8 us (4%)
  other arithmetic  10.1 us (2%)
    pallas_call x11, Pallas kernels, call(): pl.pallas_call(kernel, grid=(chunks,), in_specs=[spec for _, spec in inpu...  164 us
    ppermute x31, waiting for transfers between devices, swapped(): return lax.ppermute(block, axis, [(0, 1), (1, 0)])  44.6 us
    pallas_call x14, Pallas kernels, plain_call(): pl.pallas_call(body, in_specs=[pl.BlockSpec(memory_space=pltpu.SMEM)] + [...  33.7 us
    ppermute x31, starting transfers between devices, swapped(): return lax.ppermute(block, axis, [(0, 1), (1, 0)])  23.7 us
    ppermute x15, waiting for transfers between devices, x_swapped(): return lax.ppermute(block, 'dp', [(i, i ^ 1) for i in range(ranks)])  20.8 us
    all_gather x1, blocking collectives, line_gather(): lax.all_gather(block, 'dp', axis_index_groups=line_groups, axis=0, tiled=...  17.8 us
    ppermute x15, starting transfers between devices, x_swapped(): return lax.ppermute(block, 'dp', [(i, i ^ 1) for i in range(ranks)])  16.1 us
    unnamed x81, local copies, waits for them, and re-layouts  12.9 us
  transfers between devices with their start and end apart: 56, of which 19 were waited for; matrix products, arithmetic and copies ran while one was open for 6% of the time, Pallas kernels for 43%

commit v1 on v0

--- a/solution.py
+++ b/solution.py
@@ -1061,11 +1061,10 @@
     results, gate_half, next_half = tied(results, gate_half, next_half)
     _, gain_first, normed_first, saved_first = results
     gate_first = plane_end(*gate_half)
-    gated_first, part = gate_forward(place, block_rows, normed_first, saved_first[2], gate_first, params[0])
-    part, next_half = tied(part, next_half)
-    scan_second = plane_end(*next_half)
+    results = gate_forward(place, block_rows, normed_first, saved_first[2], gate_first, params[0])
+    (gated_first, part), scan_second = tied(results, plane_end(*next_half))
     parts_first = (part, swapped(part, "section"))
-    parts_first, teacher = tied(parts_first, teacher)
+    parts_first, teacher, gate_second = tied(parts_first, teacher, gate_second)
     results = scan_forward(place, block_rows, x_rows, parts_first, scan_second, marks, segment_row, params[1])
     results, here = tied(results, y_swapped(quarter(teacher)))
     hidden, gain_second, normed_second, saved_second = results
@@ -1152,25 +1151,31 @@
     results = weight_grads(place, block_rows, normed_first, grads, ())
     results, grad_parts = tied(results, (part, swapped(part, "section")))
     scan_reduce = plane_start(results)
-    owned_second = line_reduce(joined(crossed_second, ready=(results[0],)))
+    blocks_second = joined(crossed_second, ready=(results[0],))
+    owned_second = line_reduce(blocks_second)
+    gate_reduce, blocks_second = tied(gate_reduce, blocks_second)
     crossed_gate = crossed(gate_reduce)
     results = finish(place, *grad_parts, x_rows, grad_hidden, gain_first, (crossed_gate[0][0],))
     (grad_rows, grad_low, gain_sums), scan_reduce = tied(results, scan_reduce)
     crossed_scan = crossed(scan_reduce)
     layer_outputs = placed_rows(place, produced, produced_away, (crossed_scan[0][0],))
+    blocks = joined(crossed_scan, crossed_gate, ready=(layer_outputs, owned_second))
+    owned_first = line_reduce(blocks)
     smalls = plain_call(
-        lambda place_ref, *refs: small_kernel(*refs), place, sums_first + sums_second + (gain_sums,), [((32, units), f32)]
+        lambda place_ref, *refs: small_kernel(*refs),
+        place,
+        sums_first + sums_second + (gain_sums,),
+        [((32, units), f32)],
+        (blocks,),
     )[0]
     smalls_away = y_swapped(smalls)
+    grad_low, smalls = tied(grad_low, smalls)
     mine, others = plain_call(
         functools.partial(fold_kernel, heads_half), place, (smalls, smalls_away), [((16, half), f32)] * 2
     )
     total = jnp.concatenate([mine, swapped(others, "section")])
     total = total + x_swapped(total)
-    blocks = joined(crossed_scan, crossed_gate, ready=(total,))
-    grad_low, blocks = tied(grad_low, blocks)
-    owned_first = line_reduce(blocks)
-    boundary = placed_rows(place, grad_rows, away_rows(grad_low))
+    owned_first, boundary = tied(owned_first, placed_rows(place, grad_rows, away_rows(grad_low)))
     total = line_total(total)
     grad_conv, grad_states_conv, grad_gate_gain, grad_heads, gain_total = plain_call(
         functools.partial(small_outputs_kernel, heads_half),

time: 414 us -> 376 us (0.908)
  waiting for transfers between devices: 76.4 us -> 43.7 us
    ppermute x31, waiting for transfers between devices: 44.6 us -> 16.1 us  [swapped(): return lax.ppermute(block, axis, [(0, 1), (1, 0)])]
    unnamed x81 -> x79, local copies, waits for them, and re-layouts: 12.9 us -> 12.2 us
  transfers between devices with their start and end apart: 56 -> 56, of which waited for: 19 -> 18; matrix products, arithmetic and copies ran while one was open for 6% -> 7% of each run, Pallas kernels for 43% -> 47%
where the time goes in v1:
time: 376 us; the launch traced here: 370 us
  Pallas kernels  207 us (55%)
  starting transfers between devices  51.1 us (14%)
  waiting for transfers between devices  43.7 us (12%)
  local copies, waits for them, and re-layouts  27.4 us (7%)
  blocking collectives  17.8 us (5%)
  between operations  14.6 us (4%)
  other arithmetic  8.36 us (2%)
    pallas_call x11, Pallas kernels, call(): pl.pallas_call(kernel, grid=(chunks,), in_specs=[spec for _, spec in inpu...  164 us
    pallas_call x14, Pallas kernels, plain_call(): pl.pallas_call(body, in_specs=[pl.BlockSpec(memory_space=pltpu.SMEM)] + [...  33.6 us
    ppermute x31, starting transfers between devices, swapped(): return lax.ppermute(block, axis, [(0, 1), (1, 0)])  24.5 us
    ppermute x15, waiting for transfers between devices, x_swapped(): return lax.ppermute(block, 'dp', [(i, i ^ 1) for i in range(ranks)])  19.2 us
    all_gather x1, blocking collectives, line_gather(): lax.all_gather(block, 'dp', axis_index_groups=line_groups, axis=0, tiled=...  17.8 us
    ppermute x31, waiting for transfers between devices, swapped(): return lax.ppermute(block, axis, [(0, 1), (1, 0)])  16.1 us
    ppermute x15, starting transfers between devices, x_swapped(): return lax.ppermute(block, 'dp', [(i, i ^ 1) for i in range(ranks)])  15.5 us
    unnamed x79, local copies, waits for them, and re-layouts  12.2 us
  transfers between devices with their start and end apart: 56, of which 18 were waited for; matrix products, arithmetic and copies ran while one was open for 7% of the time, Pallas kernels for 47%

profile of v1, /device:TPU:0, one launch (start us, length us, event | category | flops | bytes accessed | tf_op | source)
XLA Modules:
  0.0 370.3 jit_solution(13909654299361883477)
XLA Ops:
  7.8 3.0 shard_map.291
  12.4 2.6 collective-permute-start.1
  15.7 1.9 shard_map.292
  18.3 17.8 %all_gather.9.refs_2_.refs_3_ = bf16[384,640]{1,0:T(8,128)(2,1)} all-gather(bf16[96,640]{1,0:T(8,128)(2,1)} %get-tuple-element.234), channel_id=1, replica_groups={{0,4,8,12},{2,6,10,14},{1,5,9,13},{3,7,11,15},{16,20,24,28},{18,22,26,3..., dimensions={0}, use_global_device_ids=true | all-gather | bytes 614400 | tf_op jit(solution)/shard_map/all_gather | solution.py:980
  40.3 1.9 shard_map.293
  44.1 2.1 shard_map.294
  46.2 5.6 %collective-permute-done.8.refs_4_ = bf16[96,768]{1,0:T(8,128)(2,1)} collective-permute-done((bf16[96,768]{1,0:T(8,128)(2,1)}, bf16[96,768]{1,0:T(8,128)(2,1)}, u32[]{:S(2)}, u32[]{:S(2)}) %collective-permute-start.8) | collective-permute-done | bytes 147488 | tf_op jit(solution)/shard_map/ppermute | solution.py:974
  52.2 1.7 slice.45
  55.4 1.7 slice.44
  57.0 1.7 collective-permute-start.6
  59.8 1.8 maximum_select_fusion.1.refs_0_.refs_1_.h_ref
  61.7 2.0 shard_map.295
  64.5 2.3 shard_map.297
  70.9 17.6 %shard_map.296 = (f32[8,768]{1,0:T(8,128)}, bf16[1024,768]{1,0:T(8,128)(2,1)}, f32[1024,768]{1,0:T(8,128)}, f32[1024,768]{1,0:T(8,128)}, f32[1024,768]{1,0:T(8,1...) custom-call(s32[4]{0:T(128)} %pad_add_fusion.place_ref.refs_0_, ...), custom_call_target="tpu_custom_call" | custom-call | flops 2000000000 | bytes 500000 | tf_op jit(solution)/shard_map/pallas_call | solution.py:477
  88.5 4.1 %collective-permute-done.14.refs_6_.refs_5_ = bf16[384,640]{1,0:T(8,128)(2,1)} collective-permute-done((bf16[384,640]{1,0:T(8,128)(2,1)}, bf16[384,640]{1,0:T(8,128)(2,1)}, u32[]{:S(2)}, u32[]{:S(2)}) %collective-permute-start.14) | collective-permute-done | bytes 491552 | tf_op jit(solution)/shard_map/ppermute | solution.py:930
  97.0 1.7 slice.37
  98.7 1.6 slice.38
  103.6 2.2 collective-permute-done.15.refs_3_.refs_14_
  105.8 7.4 %shard_map.298 = (f32[1024,768]{1,0:T(8,128)}, bf16[1024,896]{1,0:T(8,128)(2,1)}) custom-call(s32[4]{0:T(128)} %pad_add_fusion.place_ref.refs_0_, bf16[1024,768]{1,0:T(8,128)(2,1)} %get-tuple-element.267.normed_ref.refs_8_, f32[1024,768]{1,0:T(8,128)} %get-tuple-element.268.y_ref.refs_10_.refs_16_, bf16[384,768]{1,0:T(8,128)(2,1)} %get-tuple-element.269.refs_0_.refs_11_, ...), custom_call_target="tpu_custom_call" | custom-call | flops 1000000000 | bytes 500000 | tf_op jit(solution)/shard_map/pallas_call | solution.py:477
  113.3 4.1 %collective-permute-done.19.refs_3_.refs_2_ = bf16[1024,896]{1,0:T(8,128)(2,1)} collective-permute-done((bf16[1024,896]{1,0:T(8,128)(2,1)}, bf16[1024,896]{1,0:T(8,128)(2,1)}, u32[]{:S(2)}, u32[]{:S(2)}) %collective-permute-start.19) | collective-permute-done | bytes 1835040 | tf_op jit(solution)/shard_map/ppermute | solution.py:930
  117.6 19.1 %shard_map.299 = (bf16[1024,768]{1,0:T(8,128)(2,1)}, f32[8,768]{1,0:T(8,128)}, bf16[1024,768]{1,0:T(8,128)(2,1)}, f32[1024,768]{1,0:T(8,128)}, f32[1024,768]{1,0...) custom-call(s32[4]{0:T(128)} %pad_add_fusion.place_ref.refs_0_, ...), custom_call_target="tpu_custom_call" | custom-call | flops 2000000000 | bytes 500000 | tf_op jit(solution)/shard_map/pallas_call | solution.py:477
  137.2 7.4 %shard_map.300 = (f32[1024,768]{1,0:T(8,128)}, bf16[1024,896]{1,0:T(8,128)(2,1)}) custom-call(s32[4]{0:T(128)} %pad_add_fusion.place_ref.refs_0_, bf16[1024,768]{1,0:T(8,128)(2,1)} %get-tuple-element.301.normed_ref.refs_5_, f32[1024,768]{1,0:T(8,128)} %get-tuple-element.302.y_ref.refs_7_.refs_16_, ...), custom_call_target="tpu_custom_call" | custom-call | flops 1000000000 | bytes 500000 | tf_op jit(solution)/shard_map/pallas_call | solution.py:477
  146.8 1.9 maximum_select_fusion.refs_4_
  149.0 16.4 %shard_map.301 = (bf16[1024,768]{1,0:T(8,128)(2,1)}, f32[1024,768]{1,0:T(8,128)}, bf16[1024,768]{1,0:T(8,128)(2,1)}, f32[1024,768]{1,0:T(8,128)}, bf16[384,768]{...) custom-call(s32[4]{0:T(128)} %pad_add_fusion.place_ref.refs_0_, ...), custom_call_target="tpu_custom_call" | custom-call | flops 2000000000 | bytes 500000 | tf_op jit(solution)/shard_map/pallas_call | solution.py:477
  166.5 1.6 collective-permute-start.25
  169.5 29.7 %shard_map.302 = (bf16[1024,1280]{1,0:T(8,128)(2,1)}, bf16[1024,768]{1,0:T(8,128)(2,1)}, f32[8,768]{1,0:T(8,128)}, f32[8,256]{1,0:T(8,128)}) custom-call(s32[4]{0:T(128)} %pad_add_fusion.place_ref.refs_0_, bf16[1024,768]{1,0:T(8,128)(2,1)} %get-tuple-element.312.refs_1_, f32[1024,768]{1,0:T(8,128)} %get-tuple-element.313.refs_2_, ...), custom_call_target="tpu_custom_call" | custom-call | flops 3000000000 | bytes 500000 | tf_op jit(solution)/shard_map/pallas_call | solution.py:477
  200.3 6.5 %shard_map.303 = (bf16[384,640]{1,0:T(8,128)(2,1)}, bf16[384,640]{1,0:T(8,128)(2,1)}, bf16[384,640]{1,0:T(8,128)(2,1)}, bf16[192,640]{1,0:T(8,128)(2,1)}, bf16[192,640]{1,0:T(8,128)(2,1)}) custom-call(s32[4]{0:T(128)} %pad_add_fusion.place_ref.refs_0_, bf16[1024,768]{1,0:T(8,128)(2,1)} %get-tuple-element.301.normed_ref.refs_5_, ...), custom_call_target="tpu_custom_call" | custom-call | flops 500000000 | bytes 500000 | tf_op jit(solution)/shard_map/pallas_call | solution.py:477
  206.8 1.6 collective-permute-start.27
  209.5 17.4 %shard_map.304 = (f32[1024,768]{1,0:T(8,128)}, bf16[1024,768]{1,0:T(8,128)(2,1)}, f32[1024,768]{1,0:T(8,128)}, bf16[384,768]{1,0:T(8,128)(2,1)}, bf16[384,768]{1...) custom-call(s32[4]{0:T(128)} %pad_add_fusion.place_ref.refs_0_, ...), custom_call_target="tpu_custom_call" | custom-call | flops 2000000000 | bytes 500000 | tf_op jit(solution)/shard_map/pallas_call | solution.py:477
  227.7 3.5 shard_map.306
  235.2 29.7 %shard_map.305 = (bf16[1024,1280]{1,0:T(8,128)(2,1)}, bf16[1024,768]{1,0:T(8,128)(2,1)}, f32[8,768]{1,0:T(8,128)}, f32[8,256]{1,0:T(8,128)}) custom-call(s32[4]{0:T(128)} %pad_add_fusion.place_ref.refs_0_, bf16[1024,768]{1,0:T(8,128)(2,1)} %get-tuple-element.356.refs_1_, f32[1024,768]{1,0:T(8,128)} %get-tuple-element.357.refs_2_, ...), custom_call_target="tpu_custom_call" | custom-call | flops 3000000000 | bytes 500000 | tf_op jit(solution)/shard_map/pallas_call | solution.py:477
  266.1 6.5 %shard_map.307 = (bf16[384,640]{1,0:T(8,128)(2,1)}, bf16[384,640]{1,0:T(8,128)(2,1)}, bf16[384,640]{1,0:T(8,128)(2,1)}, bf16[192,640]{1,0:T(8,128)(2,1)}, bf16[192,640]{1,0:T(8,128)(2,1)}) custom-call(s32[4]{0:T(128)} %pad_add_fusion.place_ref.refs_0_, bf16[1024,768]{1,0:T(8,128)(2,1)} %get-tuple-element.267.normed_ref.refs_8_, ...), custom_call_target="tpu_custom_call" | custom-call | flops 500000000 | bytes 500000 | tf_op jit(solution)/shard_map/pallas_call | solution.py:477
  272.6 3.9 %shard_map.308 = bf16[384,1408]{1,0:T(8,128)(2,1)} custom-call(s32[4]{0:T(128)} %pad_add_fusion.place_ref.refs_0_, bf16[384,640]{1,0:T(8,128)(2,1)} %get-tuple-element.414.refs_0_.refs_2_, bf16[384,640]{1,0:T(8,128)(2,1)} %get-tuple-element.402.refs_1_, bf16[384,768]{1,0:T(8,128)(2,1)} %get-tuple-element.403.refs_2_, bf16[384,1408]{1,0:T(8,128)(2,1)} %copy-done.7, ...), custom_call_target="tpu_custom_call" | custom-call | bytes 500000 | tf_op jit(solution)/shard_map/pallas_call | solution.py:754
  278.2 2.5 shard_map.312
  283.4 6.6 %shard_map.309 = (f32[1024,768]{1,0:T(8,128)}, bf16[1024,768]{1,0:T(8,128)(2,1)}, f32[8,768]{1,0:T(8,128)}) custom-call(s32[4]{0:T(128)} %pad_add_fusion.place_ref.refs_0_, bf16[1024,768]{1,0:T(8,128)(2,1)} %get-tuple-element.392.own_ref, bf16[1024,768]{1,0:T(8,128)(2,1)} %copy-done.4, bf16[1024,768]{1,0:T(8,128)(2,1)} %maximum_select_fusion.1.refs_0_.refs_1_.h_ref, ...), custom_call_target="tpu_custom_call" | custom-call | flops 30000000 | bytes 500000 | tf_op jit(solution)/shard_map/pallas_call | solution.py:477
  290.8 2.4 shard_map.311
  294.6 3.4 shard_map.310.refs_0_.refs_1_
  298.8 9.8 %collective-permute-done.36.refs_3_ = bf16[384,640]{1,0:T(8,128)(2,1)S(1)} collective-permute-done((bf16[384,640]{1,0:T(8,128)(2,1)}, bf16[384,640]{1,0:T(8,128)(2,1)S(1)}, u32[]{:S(2)}, u32[]{:S(2)}) %collective-permute-start.36) | collective-permute-done | bytes 491552 | tf_op jit(solution)/shard_map/ppermute | solution.py:974
  309.6 3.2 shard_map.313.refs_0_
  315.9 3.3 collective-permute-done.41.away_ref
  319.8 1.6 shard_map.316
  328.3 4.5 %collective-permute-start.44 = (f32[32,384]{1,0:T(8,128)S(1)}, f32[32,384]{1,0:T(8,128)S(1)}, u32[]{:S(2)}, u32[]{:S(2)}) collective-permute-start(f32[32,384]{1,0:T(8,128)S(1)} %add.60), channel_id=1, source_target_pairs={{0,4},{2,6},{4,8},{6,10},{8,12},{10,14},{1,5},{3,7},{5,9},{7,11},{... | collective-permute-start | bytes 147464 | tf_op jit(solution)/shard_map/ppermute | solution.py:990
  332.9 2.7 collective-permute-done.45
  338.8 3.0 collective-permute-done.47
  341.8 1.9 collective-permute-done.48
  348.1 4.1 %shard_map.315.refs_0_ = f32[2,512,768]{2,1,0:T(8,128)} custom-call(s32[4]{0:T(128)} %pad_add_fusion.place_ref.refs_0_, f32[1024,768]{1,0:T(8,128)} %get-tuple-element.427.own_ref, bf16[512,768]{1,0:T(8,128)(2,1)} %copy-done.10), custom_call_target="tpu_custom_call" | custom-call | bytes 500000 | tf_op jit(solution)/shard_map/pallas_call | solution.py:641
  353.1 1.6 collective-permute-start.51
  359.8 2.3 shard_map.318
  (201 shorter events, 72.9 us)
Async XLA Ops:
  7.2 57.1 %all-gather.3.cloned.1.call-start = ((), (), s32[]{:S(2)}) async-start(), calls=%async_computation.2 | async-start | bytes 1351680 | tf_op jit(solution)/shard_map/all_gather | solution.py:980
  12.4 23.7 %collective-permute-start.1 = (bf16[256,768]{1,0:T(8,128)(2,1)S(1)}, bf16[256,768]{1,0:T(8,128)(2,1)}, u32[]{:S(2)}, u32[]{:S(2)}) collective-permute-start(bf16[256,768]{1,0:T(8,128)(2,1)S(1)} %dynamic-slice_bitcast_fusion.3), channel_id=1, source_target_pairs={{0,1},{1,0},{2,3},{3,2},{4,5},{5,4},{6,7},{7,6},{8,9},{9,8},{10,11... | collective-permute-start | bytes 1179656 | tf_op jit(solution)/shard_map/ppermute | solution.py:930
  17.6 18.5 %collective-permute-start.2 = (bf16[32,384]{1,0:T(8,128)(2,1)}, bf16[32,384]{1,0:T(8,128)(2,1)S(1)}, u32[]{:S(2)}, u32[]{:S(2)}) collective-permute-start(bf16[32,384]{1,0:T(8,128)(2,1)} %get-tuple-element.235), channel_id=1, source_target_pairs={{0,1},{1,0},{2,3},{3,2},{4,5},{5,4},{6,7},{7,6},{8,9},{9,8},{10,11... | collective-permute-start | bytes 73736 | tf_op jit(solution)/shard_map/ppermute | solution.py:930
  36.1 81.3 %all-gather.5.cloned.1.call-start = ((), (), s32[]{:S(2)}) async-start(), calls=%async_computation.3 | async-start | bytes 2949120 | tf_op jit(solution)/shard_map/all_gather | solution.py:980
  36.2 16.0 %collective-permute-start.5 = (bf16[384,640]{1,0:T(8,128)(2,1)}, bf16[384,640]{1,0:T(8,128)(2,1)}, u32[]{:S(2)}, u32[]{:S(2)}) collective-permute-start(bf16[384,640]{1,0:T(8,128)(2,1)} %all_gather.9.refs_2_.refs_3_), channel_id=1, source_target_pairs={{0,1},{1,0},{2,3},{3,2},{4,5},{5,4},{6,7},{7,6},{8,9},{9,8},{10,11... | collective-permute-start | bytes 1474568 | tf_op jit(solution)/shard_map/ppermute | solution.py:930
  37.7 17.6 %collective-permute-start.4 = (bf16[384,640]{1,0:T(8,128)(2,1)}, bf16[384,640]{1,0:T(8,128)(2,1)}, u32[]{:S(2)}, u32[]{:S(2)}) collective-permute-start(bf16[384,640]{1,0:T(8,128)(2,1)} %all_gather.9.refs_2_.refs_3_), channel_id=1, source_target_pairs={{0,2},{2,0},{4,6},{6,4},{8,10},{10,8},{12,14},{14,12},{1,3},{3,1},... | collective-permute-start | bytes 1474568 | tf_op jit(solution)/shard_map/ppermute | solution.py:974
  39.2 19.5 %collective-permute-start.3 = (bf16[256,768]{1,0:T(8,128)(2,1)}, bf16[256,768]{1,0:T(8,128)(2,1)}, u32[]{:S(2)}, u32[]{:S(2)}) collective-permute-start(bf16[256,768]{1,0:T(8,128)(2,1)} %collective-permute-done.1), channel_id=1, source_target_pairs={{0,16},{16,0},{1,17},{17,1},{2,18},{18,2},{3,19},{19,3},{4,20},{20... | collective-permute-start | bytes 1179656 | tf_op jit(solution)/shard_map/ppermute | solution.py:930
  39.2 12.6 %collective-permute-start.8 = (bf16[96,768]{1,0:T(8,128)(2,1)}, bf16[96,768]{1,0:T(8,128)(2,1)}, u32[]{:S(2)}, u32[]{:S(2)}) collective-permute-start(bf16[96,768]{1,0:T(8,128)(2,1)} %get-tuple-element.244.refs_3_), channel_id=1, source_target_pairs={{0,2},{2,0},{4,6},{6,4},{8,10},{10,8},{12,14},{14,12},{1,3},{3,1},... | collective-permute-start | bytes 442376 | tf_op jit(solution)/shard_map/ppermute | solution.py:974
  43.5 18.2 %collective-permute-start.9 = (bf16[96,768]{1,0:T(8,128)(2,1)S(1)}, bf16[96,768]{1,0:T(8,128)(2,1)}, u32[]{:S(2)}, u32[]{:S(2)}) collective-permute-start(bf16[96,768]{1,0:T(8,128)(2,1)S(1)} %copy-done.25), channel_id=1, source_target_pairs={{0,1},{1,0},{2,3},{3,2},{4,5},{5,4},{6,7},{7,6},{8,9},{9,8},{10,11... | collective-permute-start | bytes 442376 | tf_op jit(solution)/shard_map/ppermute | solution.py:930
  51.8 9.8 %collective-permute-start.10 = (bf16[96,768]{1,0:T(8,128)(2,1)}, bf16[96,768]{1,0:T(8,128)(2,1)}, u32[]{:S(2)}, u32[]{:S(2)}) collective-permute-start(bf16[96,768]{1,0:T(8,128)(2,1)} %collective-permute-done.8.refs_4_), channel_id=1, source_target_pairs={{0,1},{1,0},{2,3},{3,2},{4,5},{5,4},{6,7},{7,6},{8,9},{9,8},{10,11... | collective-permute-start | bytes 442376 | tf_op jit(solution)/shard_map/ppermute | solution.py:930
  53.9 9.8 %collective-permute-start.7 = (bf16[192,640]{1,0:T(8,128)(2,1)}, bf16[192,640]{1,0:T(8,128)(2,1)}, u32[]{:S(2)}, u32[]{:S(2)}) collective-permute-start(bf16[192,640]{1,0:T(8,128)(2,1)} %slice.45), channel_id=1, source_target_pairs={{0,2},{2,0},{4,6},{6,4},{8,10},{10,8},{12,14},{14,12},{1,3},{3,1},... | collective-permute-start | bytes 737288 | tf_op jit(solution)/shard_map/ppermute | solution.py:974
  57.0 6.6 %collective-permute-start.6 = (bf16[192,640]{1,0:T(8,128)(2,1)}, bf16[192,640]{1,0:T(8,128)(2,1)}, u32[]{:S(2)}, u32[]{:S(2)}) collective-permute-start(bf16[192,640]{1,0:T(8,128)(2,1)} %slice.44), channel_id=1, source_target_pairs={{0,1},{1,0},{2,3},{3,2},{4,5},{5,4},{6,7},{7,6},{8,9},{9,8},{10,11... | collective-permute-start | bytes 737288 | tf_op jit(solution)/shard_map/ppermute | solution.py:930
  64.3 244.3 %reduce-scatter.3.cloned.1.call-start = ((), (), s32[]{:S(2)}) async-start(), calls=%async_computation.4 | async-start | bytes 1351680 | tf_op jit(solution)/shard_map/reduce_scatter | solution.py:983
  66.8 26.9 %collective-permute-start.12 = (bf16[384,768]{1,0:T(8,128)(2,1)}, bf16[384,768]{1,0:T(8,128)(2,1)S(1)}, u32[]{:S(2)}, u32[]{:S(2)}) collective-permute-start(bf16[384,768]{1,0:T(8,128)(2,1)} %get-tuple-element.269.refs_0_.refs_11_), channel_id=1, source_target_pairs={{0,1},{1,0},{2,3},{3,2},{4,5},{5,4},{6,7},{7,6},{8,9},{9,8},{10,11... | collective-permute-start | bytes 1769480 | tf_op jit(solution)/shard_map/ppermute | solution.py:930
  68.3 25.5 %collective-permute-start.11 = (bf16[384,768]{1,0:T(8,128)(2,1)}, bf16[384,768]{1,0:T(8,128)(2,1)}, u32[]{:S(2)}, u32[]{:S(2)}) collective-permute-start(bf16[384,768]{1,0:T(8,128)(2,1)} %get-tuple-element.269.refs_0_.refs_11_), channel_id=1, source_target_pairs={{0,2},{2,0},{4,6},{6,4},{8,10},{10,8},{12,14},{14,12},{1,3},{3,1},... | collective-permute-start | bytes 1769480 | tf_op jit(solution)/shard_map/ppermute | solution.py:974
  69.8 22.8 %collective-permute-start.14 = (bf16[384,640]{1,0:T(8,128)(2,1)}, bf16[384,640]{1,0:T(8,128)(2,1)}, u32[]{:S(2)}, u32[]{:S(2)}) collective-permute-start(bf16[384,640]{1,0:T(8,128)(2,1)} %get-tuple-element.281.refs_4_.refs_3_), channel_id=1, source_target_pairs={{0,1},{1,0},{2,3},{3,2},{4,5},{5,4},{6,7},{7,6},{8,9},{9,8},{10,11... | collective-permute-start | bytes 1474568 | tf_op jit(solution)/shard_map/ppermute | solution.py:930
  70.3 23.4 %collective-permute-start.13 = (bf16[384,640]{1,0:T(8,128)(2,1)}, bf16[384,640]{1,0:T(8,128)(2,1)}, u32[]{:S(2)}, u32[]{:S(2)}) collective-permute-start(bf16[384,640]{1,0:T(8,128)(2,1)} %get-tuple-element.281.refs_4_.refs_3_), channel_id=1, source_target_pairs={{0,2},{2,0},{4,6},{6,4},{8,10},{10,8},{12,14},{14,12},{1,3},{3,1},... | collective-permute-start | bytes 1474568 | tf_op jit(solution)/shard_map/ppermute | solution.py:974
  95.0 8.7 %collective-permute-start.16 = (bf16[192,768]{1,0:T(8,128)(2,1)S(1)}, bf16[192,768]{1,0:T(8,128)(2,1)S(1)}, u32[]{:S(2)}, u32[]{:S(2)}) collective-permute-start(bf16[192,768]{1,0:T(8,128)(2,1)S(1)} %slice.36), channel_id=1, source_target_pairs={{0,2},{2,0},{4,6},{6,4},{8,10},{10,8},{12,14},{14,12},{1,3},{3,1},... | collective-permute-start | bytes 884744 | tf_op jit(solution)/shard_map/ppermute | solution.py:974
  96.5 9.3 %collective-permute-start.15 = (bf16[192,768]{1,0:T(8,128)(2,1)S(1)}, bf16[192,768]{1,0:T(8,128)(2,1)}, u32[]{:S(2)}, u32[]{:S(2)}) collective-permute-start(bf16[192,768]{1,0:T(8,128)(2,1)S(1)} %slice.35), channel_id=1, source_target_pairs={{0,1},{1,0},{2,3},{3,2},{4,5},{5,4},{6,7},{7,6},{8,9},{9,8},{10,11... | collective-permute-start | bytes 884744 | tf_op jit(solution)/shard_map/ppermute | solution.py:930
  100.3 12.9 %collective-permute-start.18 = (bf16[192,640]{1,0:T(8,128)(2,1)}, bf16[192,640]{1,0:T(8,128)(2,1)}, u32[]{:S(2)}, u32[]{:S(2)}) collective-permute-start(bf16[192,640]{1,0:T(8,128)(2,1)} %slice.38), channel_id=1, source_target_pairs={{0,2},{2,0},{4,6},{6,4},{8,10},{10,8},{12,14},{14,12},{1,3},{3,1},... | collective-permute-start | bytes 737288 | tf_op jit(solution)/shard_map/ppermute | solution.py:974
  100.9 12.3 %collective-permute-start.17 = (bf16[192,640]{1,0:T(8,128)(2,1)}, bf16[192,640]{1,0:T(8,128)(2,1)}, u32[]{:S(2)}, u32[]{:S(2)}) collective-permute-start(bf16[192,640]{1,0:T(8,128)(2,1)} %slice.37), channel_id=1, source_target_pairs={{0,1},{1,0},{2,3},{3,2},{4,5},{5,4},{6,7},{7,6},{8,9},{9,8},{10,11... | collective-permute-start | bytes 737288 | tf_op jit(solution)/shard_map/ppermute | solution.py:930
  117.5 19.8 %collective-permute-start.20 = (f32[256,768]{1,0:T(8,128)S(1)}, f32[256,768]{1,0:T(8,128)}, u32[]{:S(2)}, u32[]{:S(2)}) collective-permute-start(f32[256,768]{1,0:T(8,128)S(1)} %dynamic-slice_bitcast_fusion.1), channel_id=1, source_target_pairs={{0,1},{1,0},{2,3},{3,2},{4,5},{5,4},{6,7},{7,6},{8,9},{9,8},{10,11... | collective-permute-start | bytes 2359304 | tf_op jit(solution)/shard_map/ppermute | solution.py:930
  137.2 7.4 %collective-permute-start.21 = (f32[256,768]{1,0:T(8,128)}, f32[256,768]{1,0:T(8,128)}, u32[]{:S(2)}, u32[]{:S(2)}) collective-permute-start(f32[256,768]{1,0:T(8,128)} %collective-permute-done.20), channel_id=1, source_target_pairs={{0,16},{16,0},{1,17},{17,1},{2,18},{18,2},{3,19},{19,3},{4,20},{20... | collective-permute-start | bytes 2359304 | tf_op jit(solution)/shard_map/ppermute | solution.py:930
  166.5 32.7 %collective-permute-start.25 = (bf16[512,768]{1,0:T(8,128)(2,1)S(1)}, bf16[512,768]{1,0:T(8,128)(2,1)S(1)}, u32[]{:S(2)}, u32[]{:S(2)}) collective-permute-start(bf16[512,768]{1,0:T(8,128)(2,1)S(1)} %constant_dynamic-slice_fusion.2), channel_id=1, source_target_pairs={{0,1},{1,0},{2,3},{3,2},{4,5},{5,4},{6,7},{7,6},{8,9},{9,8},{10,11... | collective-permute-start | bytes 2359304 | tf_op jit(solution)/shard_map/ppermute | solution.py:930
  168.1 31.1 %collective-permute-start.23 = (bf16[192,768]{1,0:T(8,128)(2,1)}, bf16[192,768]{1,0:T(8,128)(2,1)S(1)}, u32[]{:S(2)}, u32[]{:S(2)}) collective-permute-start(bf16[192,768]{1,0:T(8,128)(2,1)} %get-tuple-element.327), channel_id=1, source_target_pairs={{0,1},{1,0},{2,3},{3,2},{4,5},{5,4},{6,7},{7,6},{8,9},{9,8},{10,11... | collective-permute-start | bytes 884744 | tf_op jit(solution)/shard_map/ppermute | solution.py:930
  168.6 30.6 %collective-permute-start.24 = (bf16[192,768]{1,0:T(8,128)(2,1)}, bf16[192,768]{1,0:T(8,128)(2,1)S(1)}, u32[]{:S(2)}, u32[]{:S(2)}) collective-permute-start(bf16[192,768]{1,0:T(8,128)(2,1)} %get-tuple-element.328), channel_id=1, source_target_pairs={{0,2},{2,0},{4,6},{6,4},{8,10},{10,8},{12,14},{14,12},{1,3},{3,1},... | collective-permute-start | bytes 884744 | tf_op jit(solution)/shard_map/ppermute | solution.py:974
  200.2 6.5 %collective-permute-start.26 = (bf16[1024,768]{1,0:T(8,128)(2,1)}, bf16[1024,768]{1,0:T(8,128)(2,1)S(1)}, u32[]{:S(2)}, u32[]{:S(2)}) collective-permute-start(bf16[1024,768]{1,0:T(8,128)(2,1)} %get-tuple-element.338.refs_5_), channel_id=1, source_target_pairs={{0,16},{16,0},{1,17},{17,1},{2,18},{18,2},{3,19},{19,3},{4,20},{20... | collective-permute-start | bytes 4718600 | tf_op jit(solution)/shard_map/ppermute | solution.py:930
  206.8 20.2 %collective-permute-start.27 = (bf16[192,640]{1,0:T(8,128)(2,1)}, bf16[192,640]{1,0:T(8,128)(2,1)S(1)}, u32[]{:S(2)}, u32[]{:S(2)}) collective-permute-start(bf16[192,640]{1,0:T(8,128)(2,1)} %get-tuple-element.354), channel_id=1, source_target_pairs={{0,1},{1,0},{2,3},{3,2},{4,5},{5,4},{6,7},{7,6},{8,9},{9,8},{10,11... | collective-permute-start | bytes 737288 | tf_op jit(solution)/shard_map/ppermute | solution.py:930
  208.3 18.6 %collective-permute-start.28 = (bf16[192,640]{1,0:T(8,128)(2,1)}, bf16[192,640]{1,0:T(8,128)(2,1)S(1)}, u32[]{:S(2)}, u32[]{:S(2)}) collective-permute-start(bf16[192,640]{1,0:T(8,128)(2,1)} %get-tuple-element.355), channel_id=1, source_target_pairs={{0,2},{2,0},{4,6},{6,4},{8,10},{10,8},{12,14},{14,12},{1,3},{3,1},... | collective-permute-start | bytes 737288 | tf_op jit(solution)/shard_map/ppermute | solution.py:974
  231.2 33.8 %collective-permute-start.29 = (bf16[384,1408]{1,0:T(8,128)(2,1)}, bf16[384,1408]{1,0:T(8,128)(2,1)S(1)}, u32[]{:S(2)}, u32[]{:S(2)}) collective-permute-start(bf16[384,1408]{1,0:T(8,128)(2,1)} %get-tuple-element.378), channel_id=1, source_target_pairs={{0,2},{2,0},{4,6},{6,4},{8,10},{10,8},{12,14},{14,12},{1,3},{3,1},... | collective-permute-start | bytes 3244040 | tf_op jit(solution)/shard_map/ppermute | solution.py:974
  232.0 33.0 %collective-permute-start.30 = (bf16[384,1408]{1,0:T(8,128)(2,1)}, bf16[384,1408]{1,0:T(8,128)(2,1)S(1)}, u32[]{:S(2)}, u32[]{:S(2)}) collective-permute-start(bf16[384,1408]{1,0:T(8,128)(2,1)} %get-tuple-element.379), channel_id=1, source_target_pairs={{0,1},{1,0},{2,3},{3,2},{4,5},{5,4},{6,7},{7,6},{8,9},{9,8},{10,11... | collective-permute-start | bytes 3244040 | tf_op jit(solution)/shard_map/ppermute | solution.py:930
  232.6 32.3 %collective-permute-start.31 = (bf16[192,768]{1,0:T(8,128)(2,1)S(1)}, bf16[192,768]{1,0:T(8,128)(2,1)S(1)}, u32[]{:S(2)}, u32[]{:S(2)}) collective-permute-start(bf16[192,768]{1,0:T(8,128)(2,1)S(1)} %copy-done.34), channel_id=1, source_target_pairs={{0,1},{1,0},{2,3},{3,2},{4,5},{5,4},{6,7},{7,6},{8,9},{9,8},{10,11... | collective-permute-start | bytes 884744 | tf_op jit(solution)/shard_map/ppermute | solution.py:930
  234.1 30.9 %collective-permute-start.32 = (bf16[192,768]{1,0:T(8,128)(2,1)S(1)}, bf16[192,768]{1,0:T(8,128)(2,1)S(1)}, u32[]{:S(2)}, u32[]{:S(2)}) collective-permute-start(bf16[192,768]{1,0:T(8,128)(2,1)S(1)} %copy-done.33), channel_id=1, source_target_pairs={{0,2},{2,0},{4,6},{6,4},{8,10},{10,8},{12,14},{14,12},{1,3},{3,1},... | collective-permute-start | bytes 884744 | tf_op jit(solution)/shard_map/ppermute | solution.py:974
  266.1 6.5 %collective-permute-start.33 = (bf16[1024,768]{1,0:T(8,128)(2,1)}, bf16[1024,768]{1,0:T(8,128)(2,1)S(1)}, u32[]{:S(2)}, u32[]{:S(2)}) collective-permute-start(bf16[1024,768]{1,0:T(8,128)(2,1)} %get-tuple-element.392.own_ref), channel_id=1, source_target_pairs={{0,16},{16,0},{1,17},{17,1},{2,18},{18,2},{3,19},{19,3},{4,20},{20... | collective-permute-start | bytes 4718600 | tf_op jit(solution)/shard_map/ppermute | solution.py:930
  276.5 75.7 %reduce-scatter.5.cloned.1.call-start = ((), (), s32[]{:S(2)}) async-start(), calls=%async_computation.5 | async-start | bytes 1351680 | tf_op jit(solution)/shard_map/reduce_scatter | solution.py:983
  276.7 13.3 %collective-permute-start.34 = (bf16[192,640]{1,0:T(8,128)(2,1)S(1)}, bf16[192,640]{1,0:T(8,128)(2,1)S(1)}, u32[]{:S(2)}, u32[]{:S(2)}) collective-permute-start(bf16[192,640]{1,0:T(8,128)(2,1)S(1)} %copy-done.36), channel_id=1, source_target_pairs={{0,1},{1,0},{2,3},{3,2},{4,5},{5,4},{6,7},{7,6},{8,9},{9,8},{10,11... | collective-permute-start | bytes 737288 | tf_op jit(solution)/shard_map/ppermute | solution.py:930
  277.3 12.7 %collective-permute-start.35 = (bf16[192,640]{1,0:T(8,128)(2,1)S(1)}, bf16[192,640]{1,0:T(8,128)(2,1)S(1)}, u32[]{:S(2)}, u32[]{:S(2)}) collective-permute-start(bf16[192,640]{1,0:T(8,128)(2,1)S(1)} %copy-done.35), channel_id=1, source_target_pairs={{0,2},{2,0},{4,6},{6,4},{8,10},{10,8},{12,14},{14,12},{1,3},{3,1},... | collective-permute-start | bytes 737288 | tf_op jit(solution)/shard_map/ppermute | solution.py:974
  280.7 18.0 %collective-permute-start.38 = (bf16[384,768]{1,0:T(8,128)(2,1)}, bf16[384,768]{1,0:T(8,128)(2,1)S(1)}, u32[]{:S(2)}, u32[]{:S(2)}) collective-permute-start(bf16[384,768]{1,0:T(8,128)(2,1)} %get-tuple-element.425), channel_id=1, source_target_pairs={{0,2},{2,0},{4,6},{6,4},{8,10},{10,8},{12,14},{14,12},{1,3},{3,1},... | collective-permute-start | bytes 1769480 | tf_op jit(solution)/shard_map/ppermute | solution.py:974
  281.9 16.9 %collective-permute-start.39 = (bf16[384,768]{1,0:T(8,128)(2,1)}, bf16[384,768]{1,0:T(8,128)(2,1)S(1)}, u32[]{:S(2)}, u32[]{:S(2)}) collective-permute-start(bf16[384,768]{1,0:T(8,128)(2,1)} %get-tuple-element.426), channel_id=1, source_target_pairs={{0,1},{1,0},{2,3},{3,2},{4,5},{5,4},{6,7},{7,6},{8,9},{9,8},{10,11... | collective-permute-start | bytes 1769480 | tf_op jit(solution)/shard_map/ppermute | solution.py:930
  293.2 15.4 %collective-permute-start.36 = (bf16[384,640]{1,0:T(8,128)(2,1)}, bf16[384,640]{1,0:T(8,128)(2,1)S(1)}, u32[]{:S(2)}, u32[]{:S(2)}) collective-permute-start(bf16[384,640]{1,0:T(8,128)(2,1)} %get-tuple-element.419), channel_id=1, source_target_pairs={{0,2},{2,0},{4,6},{6,4},{8,10},{10,8},{12,14},{14,12},{1,3},{3,1},... | collective-permute-start | bytes 1474568 | tf_op jit(solution)/shard_map/ppermute | solution.py:974
  294.0 14.6 %collective-permute-start.37 = (bf16[384,640]{1,0:T(8,128)(2,1)}, bf16[384,640]{1,0:T(8,128)(2,1)S(1)}, u32[]{:S(2)}, u32[]{:S(2)}) collective-permute-start(bf16[384,640]{1,0:T(8,128)(2,1)} %get-tuple-element.420), channel_id=1, source_target_pairs={{0,1},{1,0},{2,3},{3,2},{4,5},{5,4},{6,7},{7,6},{8,9},{9,8},{10,11... | collective-permute-start | bytes 1474568 | tf_op jit(solution)/shard_map/ppermute | solution.py:930
  325.0 22.2 %collective-permute-start.40 = (bf16[512,768]{1,0:T(8,128)(2,1)S(1)}, bf16[512,768]{1,0:T(8,128)(2,1)S(1)}, u32[]{:S(2)}, u32[]{:S(2)}) collective-permute-start(bf16[512,768]{1,0:T(8,128)(2,1)S(1)} %constant_dynamic-slice_fusion.1), channel_id=1, source_target_pairs={{0,1},{1,0},{2,3},{3,2},{4,5},{5,4},{6,7},{7,6},{8,9},{9,8},{10,11... | collective-permute-start | bytes 2359304 | tf_op jit(solution)/shard_map/ppermute | solution.py:930
  327.0 8.6 %collective-permute-start.45 = (f32[32,384]{1,0:T(8,128)S(1)}, f32[32,384]{1,0:T(8,128)S(1)}, u32[]{:S(2)}, u32[]{:S(2)}) collective-permute-start(f32[32,384]{1,0:T(8,128)S(1)} %add.60), channel_id=1, source_target_pairs={{4,0},{6,2},{8,4},{10,6},{12,8},{14,10},{5,1},{7,3},{9,5},{11,7},{... | collective-permute-start | bytes 147464 | tf_op jit(solution)/shard_map/ppermute | solution.py:990
  328.3 8.5 %collective-permute-start.44 = (f32[32,384]{1,0:T(8,128)S(1)}, f32[32,384]{1,0:T(8,128)S(1)}, u32[]{:S(2)}, u32[]{:S(2)}) collective-permute-start(f32[32,384]{1,0:T(8,128)S(1)} %add.60), channel_id=1, source_target_pairs={{0,4},{2,6},{4,8},{6,10},{8,12},{10,14},{1,5},{3,7},{5,9},{7,11},{... | collective-permute-start | bytes 147464 | tf_op jit(solution)/shard_map/ppermute | solution.py:990
  335.6 6.3 %collective-permute-start.47 = (f32[32,384]{1,0:T(8,128)S(1)}, f32[32,384]{1,0:T(8,128)S(1)}, u32[]{:S(2)}, u32[]{:S(2)}) collective-permute-start(f32[32,384]{1,0:T(8,128)S(1)} %collective-permute-done.45), channel_id=1, source_target_pairs={{8,4},{10,6},{4,0},{6,2},{9,5},{11,7},{5,1},{7,3},{24,20},{26,22},... | collective-permute-start | bytes 147464 | tf_op jit(solution)/shard_map/ppermute | solution.py:990
  336.9 6.9 %collective-permute-start.48 = (f32[32,384]{1,0:T(8,128)S(1)}, f32[32,384]{1,0:T(8,128)S(1)}, u32[]{:S(2)}, u32[]{:S(2)}) collective-permute-start(f32[32,384]{1,0:T(8,128)S(1)} %broadcast_select_fusion.7), channel_id=1, source_target_pairs={{4,12},{6,14},{8,0},{10,2},{5,13},{7,15},{9,1},{11,3},{20,28},{22,... | collective-permute-start | bytes 147464 | tf_op jit(solution)/shard_map/ppermute | solution.py:990
  338.2 5.6 %collective-permute-start.46 = (f32[32,384]{1,0:T(8,128)S(1)}, f32[32,384]{1,0:T(8,128)S(1)}, u32[]{:S(2)}, u32[]{:S(2)}) collective-permute-start(f32[32,384]{1,0:T(8,128)S(1)} %collective-permute-done.44), channel_id=1, source_target_pairs={{4,8},{6,10},{8,12},{10,14},{5,9},{7,11},{9,13},{11,15},{20,24},{2... | collective-permute-start | bytes 147464 | tf_op jit(solution)/shard_map/ppermute | solution.py:990
  352.2 6.2 %collective-permute-start.49 = (bf16[96,1408]{1,0:T(8,128)(2,1)S(1)}, bf16[96,1408]{1,0:T(8,128)(2,1)S(1)}, u32[]{:S(2)}, u32[]{:S(2)}) collective-permute-start(bf16[96,1408]{1,0:T(8,128)(2,1)S(1)} %broadcast_select_fusion.4), channel_id=1, source_target_pairs={{0,16},{16,0},{1,17},{17,1},{2,18},{18,2},{3,19},{19,3},{4,20},{20... | collective-permute-start | bytes 811016 | tf_op jit(solution)/shard_map/ppermute | solution.py:930
  (45 other events, 401.7 us)
Sparse Core Ops, SparseCore 0:
  36.3 27.9 all-gather.2
  65.9 49.9 all-gather.4
  276.6 26.4 reduce-scatter.2
  313.0 28.2 reduce-scatter.4

commit v2 on v1

--- a/solution.py
+++ b/solution.py
@@ -11,6 +11,7 @@
 HEAD_DIM = 64
 STATE = 128
 SPAN = 256
+WIDE = 512
 LANES = 128
 
 epsilon = 1e-05
@@ -127,15 +128,24 @@
             weights[pl.ds(row, rows), target : target + last - first] = ref[step * rows : (step + 1) * rows, offset + first : offset + last]
 
 
-def store_grads(refs, columns, acc, start, rows, place_ref):
+def store_grads(refs, columns, acc, start, rows, place_ref, base=0):
     first, last = columns
+    places = acc.shape[0] // (2 * rows)
     mine = place_ref[0]
-    for ref, (moved, turned, base, count) in zip(refs, pieces_of(rows, acc.shape[0] // (2 * rows))):
+    size = refs[0].shape[1] // 4
+    for index, (moved, turned, origin, count) in enumerate(pieces_of(rows, places)):
+        if len(refs) == 1:
+            if index == 4:
+                break
+            ref, offset, origin, count = refs[0], index * size + base, 0, places
+        else:
+            ref, offset = refs[index], 0
         place = 1 - mine if moved else mine
         source = start + (last - first if turned else 0)
         for step in range(count):
-            row = pl.multiple_of((2 * (base + step) + place) * rows, 32)
-            ref[step * rows : (step + 1) * rows, first:last] = acc[pl.ds(row, rows), source : source + last - first].astype(bf16)
+            row = pl.multiple_of((2 * (origin + step) + place) * rows, 32)
+            block = acc[pl.ds(row, rows), source : source + last - first]
+            ref[step * rows : (step + 1) * rows, offset + first : offset + last] = block.astype(bf16)
 
 
 def scan_forward_kernel(second, heads, rows, pieces, *refs):
@@ -254,7 +264,7 @@
     part_ref[:, width:] = jnp.where(lane == 0, high, jnp.where(lane == 1, low, jnp.zeros_like(low)))
 
 
-def gate_backward_kernel(second, rows, pieces, *refs):
+def gate_backward_kernel(second, rows, pieces, grad_arrays, base, *refs):
     place_ref, refs = refs[0], refs[1:]
     if second:
         (h_ref, own_ref, other_ref, target_ref), refs = refs[:4], refs[4:]
@@ -264,7 +274,8 @@
     (marks_ref, small_ref), refs = refs[:2], refs[2:]
     if second:
         out_ref, refs = refs[0], refs[1:]
-    (grad_out_ref, grad_y_ref, part_ref), grads, sums_ref, refs = refs[:3], refs[3:8], refs[8], refs[9:]
+    (grad_out_ref, grad_y_ref, part_ref), refs = refs[:3], refs[3:]
+    grads, sums_ref, refs = refs[:grad_arrays], refs[grad_arrays], refs[grad_arrays + 1 :]
     weights, out_weights, acc_z, acc_o, sums = refs
     units = y_ref.shape[1]
 
@@ -305,8 +316,8 @@
 
     @pl.when(pl.program_id(0) == pl.num_programs(0) - 1)
     def _():
-        store_grads(grads, (0, units // 2), acc_z, 0, rows, place_ref)
-        store_grads(grads, (units // 2, units), acc_o, 0, rows, place_ref)
+        store_grads(grads, (0, units // 2), acc_z, 0, rows, place_ref, base)
+        store_grads(grads, (units // 2, units), acc_o, 0, rows, place_ref, base)
         sums_ref[...] = sums[...]
 
 
@@ -347,8 +358,8 @@
     through_row = spread(jnp.broadcast_to(through, (8, LANES)), spreader)[0:1]
     scaled_low = (values * spread_steps).astype(bf16)
     scaled = scaled_low.astype(f32)
-    mask = linked_mask(row, column, marks, segment_ref[...])
-    scores = nt(c_rows, b_rows)
+    mask = linked_mask(column, row, marks, segment_ref[...])
+    scores = nt(b_rows, c_rows)
     logs_across = jnp.transpose(logs)
     lane = lax.broadcasted_iota(jnp.int32, (1, LANES), 1)
     is_left = lane < HEAD_DIM
@@ -362,10 +373,10 @@
         grad_right = jnp.where(is_left, zero, grad)
         mixes = []
         for head, grad_one in ((2 * pair, grad_left), (2 * pair + 1, grad_right)):
-            factor = jnp.exp(logs[:, head : head + 1] - logs_across[head : head + 1, :] + mask)
+            factor = jnp.exp(logs_across[head : head + 1, :] - logs[:, head : head + 1] + mask)
             mixes.append((factor * scores).astype(bf16))
-            grad_scores = grad_scores + nt(grad_one, block) * factor
-        pieces.append(tn(jnp.concatenate(mixes, axis=0), jnp.concatenate([grad_left, grad_right], axis=0)))
+            grad_scores = grad_scores + nt(block, grad_one) * factor
+        pieces.append(nn(jnp.concatenate(mixes, axis=1), jnp.concatenate([grad_left, grad_right], axis=0)))
     held = entry_state_ref[0]
     held_low = held.astype(bf16)
     gradient = dstate[...]
@@ -373,8 +384,8 @@
     grad_scaled = jnp.concatenate(pieces, axis=1) + spread_tail * nn(b_rows, gradient_low)
     grad_entry = (spread_entry * grad_y).astype(bf16)
     grad_scores_low = grad_scores.astype(bf16)
-    grad_c = nn(grad_scores_low, b_rows) + nt(grad_entry, held_low)
-    grad_b = tn(grad_scores_low, c_rows) + nt((spread_tail * scaled).astype(bf16), gradient_low)
+    grad_c = tn(grad_scores_low, b_rows) + nt(grad_entry, held_low)
+    grad_b = nn(grad_scores_low, c_rows) + nt((spread_tail * scaled).astype(bf16), gradient_low)
     state_term = jnp.sum(gradient * next_state[...], axis=0, keepdims=True)
     dstate[...] = through_row * gradient + tn(c_rows, grad_entry)
     next_state[...] = held
@@ -432,20 +443,50 @@
         states_sums_ref[...] = states_sums[...]
 
 
-def weight_grads_kernel(rows, place_ref, normed_ref, grads_ref, *refs):
-    outs, acc = refs[-6:-1], refs[-1]
+def scan_grads_kernel(heads, rows, pieces, grad_arrays, *refs):
+    normed_ref, refs = refs[0], refs[1:]
+    inputs, refs = refs[: 16 + pieces], refs[16 + pieces :]
+    outs, refs = refs[:grad_arrays], refs[grad_arrays:]
+    results, scratch, grads, acc = refs[:3], refs[3:-2], refs[-2], refs[-1]
+    place_ref = inputs[0]
     units = acc.shape[1] - 4 * STATE
 
     @pl.when(pl.program_id(0) == 0)
     def _():
         acc[...] = jnp.zeros_like(acc)
 
-    acc[...] += tn(normed_ref[...], grads_ref[...])
+    scan_backward_kernel(heads, rows, pieces, *inputs, grads, *results, *scratch)
+    acc[...] += tn(normed_ref[...], grads[...])
 
     @pl.when(pl.program_id(0) == pl.num_programs(0) - 1)
     def _():
         store_grads(outs, (0, units // 2), acc, 0, rows, place_ref)
         store_grads(outs, (units // 2, units // 2 + 2 * STATE), acc, units, rows, place_ref)
+
+
+def second_forward_kernel(heads, rows, *refs):
+    inputs, gate_weights, refs = refs[:15], refs[15], refs[16:]
+    outputs, (gate_ref, part_ref), refs = refs[:10], refs[10:12], refs[12:]
+    scan_forward_kernel(True, heads, rows, 5, *inputs, *outputs, *refs[:5])
+    normed_ref, y_ref, small_ref = outputs[2], outputs[5], inputs[11]
+    gate_forward_kernel(rows, 1, inputs[0], normed_ref, y_ref, gate_weights, small_ref, gate_ref, part_ref, *refs[5:])
+
+
+def second_backward_kernel(heads, rows, *refs):
+    gate_inputs, refs = refs[:11], refs[11:]
+    scan_weights, (segment_ref, states_small_ref, head_ref, spread_ref), refs = refs[:5], refs[5:9], refs[9:]
+    (raw_ref, conv_ref, raw_states_ref, conv_states_ref, steps_ref, entry_state_ref), refs = refs[:6], refs[6:]
+    (out_ref, grad_out_ref, grads_ref, gate_sums_ref, part_ref, sums_ref, states_sums_ref), refs = refs[:7], refs[7:]
+    grad_y, gate_part, refs = refs[0], refs[1], refs[2:]
+    gate_scratch, scan_scratch = refs[:5], refs[5:]
+    place_ref, normed_ref, y_ref, marks_ref, small_ref = gate_inputs[0], gate_inputs[5], gate_inputs[7], gate_inputs[9], gate_inputs[10]
+    base = scan_weights[0].shape[1]
+    gate_backward_kernel(
+        True, rows, 1, 1, base, *gate_inputs, out_ref, grad_out_ref, grad_y, gate_part, grads_ref, gate_sums_ref, *gate_scratch
+    )
+    scan_inputs = (place_ref, grad_y, gate_part, *scan_weights, marks_ref, segment_ref, small_ref, states_small_ref, head_ref, spread_ref)
+    saved = (raw_ref, conv_ref, y_ref, raw_states_ref, conv_states_ref, steps_ref, entry_state_ref)
+    scan_grads_kernel(heads, rows, 5, 1, normed_ref, *scan_inputs, *saved, grads_ref, part_ref, sums_ref, states_sums_ref, *scan_scratch)
 
 
 def norm_backward(grad_normed, hidden, grad_out, gain):
@@ -467,6 +508,10 @@
     if last is None:
         return pl.BlockSpec((SPAN, width), lambda i: (i, 0))
     return pl.BlockSpec((SPAN, width), lambda i: (last - i, 0))
+
+
+def wide_spec(width):
+    return pl.BlockSpec((WIDE, width), lambda i: (i, 0))
 
 
 def whole_spec(array):
@@ -541,10 +586,10 @@
 def gate_forward(place, rows, normed, y, weights, params):
     length, width = normed.shape
     units = params[0].shape[1]
-    inputs = [scalars(place), (normed, rows_spec(width)), (y, rows_spec(units))] + [fixed(w) for w in weights] + [fixed(params[0])]
-    outputs = [((length, units), f32, rows_spec(units)), ((length, width + LANES), bf16, rows_spec(width + LANES))]
+    inputs = [scalars(place), (normed, wide_spec(width)), (y, wide_spec(units))] + [fixed(w) for w in weights] + [fixed(params[0])]
+    outputs = [((length, units), f32, wide_spec(units)), ((length, width + LANES), bf16, wide_spec(width + LANES))]
     scratch = [((width, units), bf16)] * 2
-    return call(functools.partial(gate_forward_kernel, rows, len(weights)), inputs, outputs, scratch, length // SPAN, 1_000_000_000)
+    return call(functools.partial(gate_forward_kernel, rows, len(weights)), inputs, outputs, scratch, length // WIDE, 1_000_000_000)
 
 
 def gate_backward(place, rows, h, parts, extra, normed, gate, y, weights, marks, params):
@@ -561,28 +606,14 @@
     outputs += grad_outputs(width, rows, units)
     outputs.append(((8, units), f32, pl.BlockSpec((8, units), lambda i: (0, 0))))
     scratch = [((width, units), bf16)] * 2 + [((width, units), f32)] * 2 + [((8, units), f32)]
-    results = call(functools.partial(gate_backward_kernel, second, rows, len(weights)), inputs, outputs, scratch, length // SPAN, 2_000_000_000)
+    results = call(functools.partial(gate_backward_kernel, second, rows, len(weights), 5, 0), inputs, outputs, scratch, length // SPAN, 2_000_000_000)
     if not second:
         results = [None] + list(results)
     return results
 
 
-def scan_backward(place, rows, grad_y, gate_part, weights, marks, segment_row, params, saved):
-    length, width = gate_part.shape
-    units = params[0].shape[1]
-    chunks = length // SPAN
-    last = chunks - 1
-    inputs = [scalars(place), (grad_y, rows_spec(units, last)), (gate_part, rows_spec(width, last))]
-    inputs += [fixed(w) for w in weights]
-    inputs += [(marks, rows_spec(LANES, last)), (segment_row, pl.BlockSpec((1, SPAN), lambda i: (0, last - i)))]
-    inputs += [fixed(p) for p in params] + [fixed(spreader_of(units))]
-    inputs += [(s, rows_spec(s.shape[1], last)) for s in saved[:6]]
-    inputs.append((saved[6], pl.BlockSpec((1, STATE, units), lambda i: (last - i, 0, 0))))
-    columns = units + 4 * STATE
-    outputs = [((length, columns), bf16, rows_spec(columns, last)), ((length, width), bf16, rows_spec(width, last))]
-    for columns in (units, 2 * STATE):
-        outputs.append(((8, columns), f32, pl.BlockSpec((8, columns), lambda i: (0, 0))))
-    scratch = [
+def scan_scratch(width, units):
+    return [
         ((width, units + 4 * STATE), bf16),
         ((STATE, units), f32),
         ((STATE, units), f32),
@@ -590,18 +621,76 @@
         ((8, 2 * STATE), f32),
         ((8, units), f32),
         ((8, 2 * STATE), f32),
+        ((SPAN, units + 4 * STATE), bf16),
+        ((width, units + 4 * STATE), f32),
     ]
-    kernel = functools.partial(scan_backward_kernel, units // HEAD_DIM, rows, len(weights))
-    return call(kernel, inputs, outputs, scratch, chunks, 3_000_000_000)
-
-
-def weight_grads(place, rows, normed, grads, ready):
+
+
+def scan_backward(place, rows, grad_y, gate_part, normed, weights, marks, segment_row, params, saved):
+    length, width = gate_part.shape
+    units = params[0].shape[1]
+    chunks = length // SPAN
+    last = chunks - 1
+    inputs = [(normed, rows_spec(width, last)), scalars(place), (grad_y, rows_spec(units, last)), (gate_part, rows_spec(width, last))]
+    inputs += [fixed(w) for w in weights]
+    inputs += [(marks, rows_spec(LANES, last)), (segment_row, pl.BlockSpec((1, SPAN), lambda i: (0, last - i)))]
+    inputs += [fixed(p) for p in params] + [fixed(spreader_of(units))]
+    inputs += [(s, rows_spec(s.shape[1], last)) for s in saved[:6]]
+    inputs.append((saved[6], pl.BlockSpec((1, STATE, units), lambda i: (last - i, 0, 0))))
+    outputs = grad_outputs(width, rows, units // 2 + 2 * STATE)
+    outputs.append(((length, width), bf16, rows_spec(width, last)))
+    for columns in (units, 2 * STATE):
+        outputs.append(((8, columns), f32, pl.BlockSpec((8, columns), lambda i: (0, 0))))
+    kernel = functools.partial(scan_grads_kernel, units // HEAD_DIM, rows, len(weights), len(outputs) - 3)
+    return call(kernel, inputs, outputs, scan_scratch(width, units), chunks, 3_000_000_000)
+
+
+def second_forward(place, rows, h, parts, weights, gate_weights, marks, segment_row, params):
+    length, width = h.shape
+    units = params[0].shape[1]
+    chunks = length // SPAN
+    inputs = [scalars(place), (h, rows_spec(width))] + [(part, rows_spec(width + LANES)) for part in parts]
+    inputs += [fixed(w) for w in weights]
+    inputs += [(marks, rows_spec(LANES)), (segment_row, pl.BlockSpec((1, SPAN), lambda i: (0, i)))]
+    inputs += [fixed(p) for p in params] + [fixed(spreader_of(units)), fixed(gate_weights)]
+    outputs = [((length, width), bf16, rows_spec(width)), ((8, width), f32, pl.BlockSpec((8, width), lambda i: (0, 0)))]
+    outputs.append(((length, width), bf16, rows_spec(width)))
+    for columns in (units, units, units, 2 * STATE, 2 * STATE, LANES):
+        outputs.append(((length, columns), f32, rows_spec(columns)))
+    outputs.append(((chunks, STATE, units), f32, pl.BlockSpec((1, STATE, units), lambda i: (i, 0, 0))))
+    outputs += [((length, units), f32, rows_spec(units)), ((length, width + LANES), bf16, rows_spec(width + LANES))]
+    scratch = [((STATE, units), f32), ((8, units), f32), ((8, 2 * STATE), f32), ((8, width), f32)]
+    scratch += [((width, units + 4 * STATE), bf16)] + [((width, units), bf16)] * 2
+    kernel = functools.partial(second_forward_kernel, units // HEAD_DIM, rows)
+    results = call(kernel, inputs, outputs, scratch, chunks, 3_000_000_000)
+    return results[0], results[1], results[2], results[3:10], results[10], results[11]
+
+
+def second_backward(place, rows, h, parts, target, normed, gate, weights, gate_weights, marks, segment_row, params, saved):
     length, width = normed.shape
-    columns = grads.shape[1]
-    inputs = [scalars(place), (normed, rows_spec(width)), (grads, rows_spec(columns))] + awaited(ready)
-    outputs = grad_outputs(width, rows, columns // 2)
-    scratch = [((width, columns), f32)]
-    return call(functools.partial(weight_grads_kernel, rows), inputs, outputs, scratch, length // SPAN, 500_000_000)
+    units = params[0].shape[1]
+    chunks = length // SPAN
+    last = chunks - 1
+    inputs = [scalars(place), (h, rows_spec(width, last))] + [(part, rows_spec(width + LANES, last)) for part in parts]
+    inputs += [(target, rows_spec(width, last)), (normed, rows_spec(width, last)), (gate, rows_spec(units, last))]
+    inputs += [(saved[2], rows_spec(units, last)), fixed(gate_weights), (marks, rows_spec(LANES, last)), fixed(params[0])]
+    inputs += [fixed(w) for w in weights] + [(segment_row, pl.BlockSpec((1, SPAN), lambda i: (0, last - i)))]
+    inputs += [fixed(params[1]), fixed(params[2]), fixed(spreader_of(units))]
+    inputs += [(saved[i], rows_spec(saved[i].shape[1], last)) for i in (0, 1, 3, 4, 5)]
+    inputs.append((saved[6], pl.BlockSpec((1, STATE, units), lambda i: (last - i, 0, 0))))
+
+    def sums(columns):
+        return (8, columns), f32, pl.BlockSpec((8, columns), lambda i: (0, 0))
+
+    shape = (width // 2, 4 * (units + units // 2 + 2 * STATE))
+    outputs = [((length, width), bf16, rows_spec(width, last)), ((length, width), f32, rows_spec(width, last))]
+    outputs += [(shape, bf16, pl.BlockSpec(shape, lambda i: (0, 0))), sums(units)]
+    outputs += [((length, width), bf16, rows_spec(width, last)), sums(units), sums(2 * STATE)]
+    scratch = [((SPAN, units), bf16), ((SPAN, width), f32)]
+    scratch += [((width, units), bf16)] * 2 + [((width, units), f32)] * 2 + [((8, units), f32)]
+    scratch += scan_scratch(width, units)
+    kernel = functools.partial(second_backward_kernel, units // HEAD_DIM, rows)
+    return call(kernel, inputs, outputs, scratch, chunks, 4_000_000_000)
 
 
 def finish_kernel(place_ref, own_ref, other_ref, h_ref, grad_out_ref, gain_ref, *refs):
@@ -1046,7 +1135,7 @@
     side = plain_call(beside_kernel, place, side, [((block_rows, 4 * units), bf16)], (x_rows, marks, params[0][0]))[0]
     scan_first, side = tied(plane_end(*scan_half), side)
     middle_line, side = tied(middle_line, side)
-    gate_second = (line_gather(side),)
+    gate_second = line_gather(side)
     gate_line, next_line = plain_call(
         split_kernel,
         place,
@@ -1065,13 +1154,16 @@
     (gated_first, part), scan_second = tied(results, plane_end(*next_half))
     parts_first = (part, swapped(part, "section"))
     parts_first, teacher, gate_second = tied(parts_first, teacher, gate_second)
-    results = scan_forward(place, block_rows, x_rows, parts_first, scan_second, marks, segment_row, params[1])
+    results = second_forward(
+        place, block_rows, x_rows, parts_first, scan_second, gate_second, marks, segment_row, params[1]
+    )
     results, here = tied(results, y_swapped(quarter(teacher)))
-    hidden, gain_second, normed_second, saved_second = results
-    results = gate_forward(place, block_rows, normed_second, saved_second[2], gate_second, params[1])
-    (gated_second, part), here, beside = tied(results, here, swapped(here, "section"))
+    hidden, gain_second, normed_second, saved_second, gated_second, part = results
     parts_second = (part, swapped(part, "section"))
-    target = whole_rows(teacher, here, beside)
+    target = whole_rows(teacher, here, swapped(here, "section"))
+
+    def add(*blocks):
+        return sum(block.astype(f32) for block in blocks).astype(bf16)
 
     def plane_start(pieces):
         return tuple(pieces[:3]), (y_swapped(pieces[3]), x_swapped(pieces[4]))
@@ -1095,35 +1187,27 @@
         kernel = functools.partial(join_kernel, spans)
         return plain_call(kernel, place, arrays, [((places * block_rows, columns), bf16)], ready)[0]
 
-    results = gate_backward(
+    def away_rows(rows):
+        return y_swapped(lax.dynamic_slice_in_dim(rows, (1 - turn) * local_rows, local_rows, 0))
+
+    produced, grad_out, grads, gate_sums, part, sums, states_sums = second_backward(
         place,
         block_rows,
         hidden,
         parts_second,
-        (target,),
+        target,
         normed_second,
         gated_second,
-        saved_second[2],
+        scan_second,
         gate_second,
         marks,
+        segment_row,
         params[1],
-    )
-    produced, grad_out, grad_y, gate_part = results[:4]
-    gate_reduce = plane_start(results[4:9])
-    gate_sums_second = results[9]
-
-    def away_rows(rows):
-        return y_swapped(lax.dynamic_slice_in_dim(rows, (1 - turn) * local_rows, local_rows, 0))
-
-    results = scan_backward(
-        place, block_rows, grad_y, gate_part, scan_second, marks, segment_row, params[1], saved_second
-    )
-    results, gate_reduce, produced_away = tied(results, gate_reduce, away_rows(produced))
-    grads, part, sums, states_sums = results
-    sums_second = (gate_sums_second, sums, states_sums)
-    results = weight_grads(place, block_rows, normed_second, grads, ())
-    results, grad_parts = tied(results, (part, swapped(part, "section")))
-    scan_reduce = plane_start(results)
+        saved_second,
+    )
+    quarters = line_reduce(grads)
+    sums_second = (gate_sums, sums, states_sums)
+    grad_parts = (part, swapped(part, "section"))
     results = gate_backward(
         place,
         block_rows,
@@ -1137,36 +1221,41 @@
         marks,
         params[0],
     )
-    results, scan_reduce = tied(results[1:], scan_reduce)
+    results, produced_away = tied(results[1:], away_rows(produced))
     grad_hidden, grad_y, gate_part = results[:3]
-    crossed_second = crossed(scan_reduce, gate_reduce)
     gate_reduce = plane_start(results[3:8])
     gate_sums_first = results[8]
     results = scan_backward(
-        place, block_rows, grad_y, gate_part, scan_first, marks, segment_row, params[0], saved_first
-    )
-    results, crossed_second, gate_reduce = tied(results, crossed_second, gate_reduce)
-    grads, part, sums, states_sums = results
+        place, block_rows, grad_y, gate_part, normed_first, scan_first, marks, segment_row, params[0], saved_first
+    )
+    results, gate_reduce = tied(results, gate_reduce)
+    scan_reduce = plane_start(results[:5])
+    part, sums, states_sums = results[5:]
     sums_first = (gate_sums_first, sums, states_sums)
-    results = weight_grads(place, block_rows, normed_first, grads, ())
-    results, grad_parts = tied(results, (part, swapped(part, "section")))
-    scan_reduce = plane_start(results)
-    blocks_second = joined(crossed_second, ready=(results[0],))
-    owned_second = line_reduce(blocks_second)
-    gate_reduce, blocks_second = tied(gate_reduce, blocks_second)
     crossed_gate = crossed(gate_reduce)
-    results = finish(place, *grad_parts, x_rows, grad_hidden, gain_first, (crossed_gate[0][0],))
+    results = finish(
+        place, part, swapped(part, "section"), x_rows, grad_hidden, gain_first, (crossed_gate[0][0],)
+    )
     (grad_rows, grad_low, gain_sums), scan_reduce = tied(results, scan_reduce)
+    scan_reduce, gain_sums = tied(scan_reduce, gain_sums)
     crossed_scan = crossed(scan_reduce)
     layer_outputs = placed_rows(place, produced, produced_away, (crossed_scan[0][0],))
-    blocks = joined(crossed_scan, crossed_gate, ready=(layer_outputs, owned_second))
+    blocks = joined(crossed_scan, crossed_gate, ready=(layer_outputs, quarters))
     owned_first = line_reduce(blocks)
+    columns = scan_columns + units
+    quarters = plain_call(split_kernel, place, (quarters,), [((block_rows, columns), bf16)] * 4, (blocks,))
+    both_ways = [(2 * d + t, 2 * (d ^ 1) + 1 - t) for d in range(ranks) for t in range(2)]
+    owned_second = add(
+        quarters[0],
+        x_swapped(quarters[1]),
+        y_swapped(quarters[2]),
+        lax.ppermute(quarters[3], ("dp", "tensor"), both_ways),
+    )
     smalls = plain_call(
         lambda place_ref, *refs: small_kernel(*refs),
         place,
         sums_first + sums_second + (gain_sums,),
         [((32, units), f32)],
-        (blocks,),
     )[0]
     smalls_away = y_swapped(smalls)
     grad_low, smalls = tied(grad_low, smalls)

time: 376 us -> 358 us (0.952)
  Pallas kernels: 207 us -> 185 us
    pallas_call x11 -> x7, Pallas kernels: 164 us -> 147 us  [call(): pl.pallas_call(kernel, grid=(chunks,), in_specs=[spec for _, spec in inpu...]
    ppermute x31 -> x29, waiting for transfers between devices: 16.1 us -> 21.3 us  [swapped(): return lax.ppermute(block, axis, [(0, 1), (1, 0)])]
    ppermute x5, waiting for transfers between devices: 7.6 us -> 2.65 us  [send(): lax.ppermute(rows, 'dp', [(2 * a + start, 2 * b + start) for a, b in move...]
    pallas_call x14 -> x13, Pallas kernels: 33.6 us -> 28.7 us  [plain_call(): pl.pallas_call(body, in_specs=[pl.BlockSpec(memory_space=pltpu.SMEM)] + [...]
    unnamed x79 -> x73, local copies, waits for them, and re-layouts: 12.2 us -> 15.4 us
    ppermute x15 -> x13, starting transfers between devices: 15.5 us -> 13.7 us  [x_swapped(): return lax.ppermute(block, 'dp', [(i, i ^ 1) for i in range(ranks)])]
    ppermute x15 -> x13, waiting for transfers between devices: 19.2 us -> 18.2 us  [x_swapped(): return lax.ppermute(block, 'dp', [(i, i ^ 1) for i in range(ranks)])]
    ppermute x31 -> x29, starting transfers between devices: 24.5 us -> 24.9 us  [swapped(): return lax.ppermute(block, axis, [(0, 1), (1, 0)])]
  transfers between devices with their start and end apart: 56 -> 53, of which waited for: 18 -> 17; matrix products, arithmetic and copies ran while one was open for 7% -> 7% of each run, Pallas kernels for 47% -> 38%
where the time goes in v2:
time: 358 us; the launch traced here: 352 us
  Pallas kernels  185 us (52%)
  starting transfers between devices  51.6 us (14%)
  waiting for transfers between devices  42.2 us (12%)
  local copies, waits for them, and re-layouts  30.6 us (9%)
  blocking collectives  17.8 us (5%)
  between operations  14.5 us (4%)
  other arithmetic  9.64 us (3%)
    pallas_call x7, Pallas kernels, call(): pl.pallas_call(kernel, grid=(chunks,), in_specs=[spec for _, spec in inpu...  147 us
    pallas_call x13, Pallas kernels, plain_call(): pl.pallas_call(body, in_specs=[pl.BlockSpec(memory_space=pltpu.SMEM)] + [...  28.7 us
    ppermute x29, starting transfers between devices, swapped(): return lax.ppermute(block, axis, [(0, 1), (1, 0)])  24.9 us
    ppermute x29, waiting for transfers between devices, swapped(): return lax.ppermute(block, axis, [(0, 1), (1, 0)])  21.3 us
    ppermute x13, waiting for transfers between devices, x_swapped(): return lax.ppermute(block, 'dp', [(i, i ^ 1) for i in range(ranks)])  18.2 us
    all_gather x1, blocking collectives, line_gather(): lax.all_gather(block, 'dp', axis_index_groups=line_groups, axis=0, tiled=...  17.8 us
    unnamed x73, local copies, waits for them, and re-layouts  15.4 us
    ppermute x13, starting transfers between devices, x_swapped(): return lax.ppermute(block, 'dp', [(i, i ^ 1) for i in range(ranks)])  13.7 us
  transfers between devices with their start and end apart: 53, of which 17 were waited for; matrix products, arithmetic and copies ran while one was open for 7% of the time, Pallas kernels for 38%

profile of v2, /device:TPU:0, one launch (start us, length us, event | category | flops | bytes accessed | tf_op | source)
XLA Modules:
  0.0 351.8 jit_solution(3628368063921721837)
XLA Ops:
  7.9 3.2 shard_map.291
  12.6 2.6 collective-permute-start.1
  15.9 1.9 shard_map.292
  18.5 17.8 %all_gather.9.refs_2_.refs_4_ = bf16[384,640]{1,0:T(8,128)(2,1)} all-gather(bf16[96,640]{1,0:T(8,128)(2,1)} %get-tuple-element.194), channel_id=1, replica_groups={{0,4,8,12},{2,6,10,14},{1,5,9,13},{3,7,11,15},{16,20,24,28},{18,22,26,3..., dimensions={0}, use_global_device_ids=true | all-gather | bytes 614400 | tf_op jit(solution)/shard_map/all_gather | solution.py:1069
  41.2 2.0 shard_map.293
  45.0 2.1 shard_map.294
  47.1 4.8 %collective-permute-done.8.refs_4_ = bf16[96,768]{1,0:T(8,128)(2,1)S(1)} collective-permute-done((bf16[96,768]{1,0:T(8,128)(2,1)}, bf16[96,768]{1,0:T(8,128)(2,1)S(1)}, u32[]{:S(2)}, u32[]{:S(2)}) %collective-permute-start.8) | collective-permute-done | bytes 147488 | tf_op jit(solution)/shard_map/ppermute | solution.py:1063
  52.3 1.7 slice.45
  55.4 1.7 slice.44
  57.1 1.7 collective-permute-start.6
  60.0 1.8 maximum_select_fusion.1.refs_0_.refs_1_.h_ref
  62.4 2.0 shard_map.295
  64.7 2.3 shard_map.297
  71.0 17.7 %shard_map.296 = (f32[8,768]{1,0:T(8,128)}, bf16[1024,768]{1,0:T(8,128)(2,1)}, f32[1024,768]{1,0:T(8,128)}, f32[1024,768]{1,0:T(8,128)}, f32[1024,768]{1,0:T(8,1...) custom-call(s32[4]{0:T(128)} %pad_add_fusion.place_ref.refs_0_.refs_1_, ...), custom_call_target="tpu_custom_call" | custom-call | flops 2000000000 | bytes 500000 | tf_op jit(solution)/shard_map/pallas_call | solution.py:522
  88.7 3.9 %collective-permute-done.14.refs_6_.refs_13_ = bf16[384,640]{1,0:T(8,128)(2,1)S(1)} collective-permute-done((bf16[384,640]{1,0:T(8,128)(2,1)}, bf16[384,640]{1,0:T(8,128)(2,1)S(1)}, u32[]{:S(2)}, u32[]{:S(2)}) %collective-permute-start.14) | collective-permute-done | bytes 491552 | tf_op jit(solution)/shard_map/ppermute | solution.py:1019
  99.0 1.7 slice.38
  102.8 2.6 collective-permute-done.16.refs_4_.refs_15_
  105.4 2.0 collective-permute-done.15.refs_3_.refs_14_
  108.1 6.6 %shard_map.298 = (f32[1024,768]{1,0:T(8,128)}, bf16[1024,896]{1,0:T(8,128)(2,1)}) custom-call(s32[4]{0:T(128)} %pad_add_fusion.place_ref.refs_0_.refs_1_, bf16[1024,768]{1,0:T(8,128)(2,1)} %get-tuple-element.227.normed_ref.refs_8_.refs_0_, f32[1024,768]{1,0:T(8,128)} %get-tuple-element.228.y_ref.refs_10_.refs_17_, ...), custom_call_target="tpu_custom_call" | custom-call | flops 1000000000 | bytes 500000 | tf_op jit(solution)/shard_map/pallas_call | solution.py:522
  114.8 4.1 %collective-permute-done.19.refs_3_.refs_2_ = bf16[1024,896]{1,0:T(8,128)(2,1)} collective-permute-done((bf16[1024,896]{1,0:T(8,128)(2,1)}, bf16[1024,896]{1,0:T(8,128)(2,1)}, u32[]{:S(2)}, u32[]{:S(2)}) %collective-permute-start.19) | collective-permute-done | bytes 1835040 | tf_op jit(solution)/shard_map/ppermute | solution.py:1019
  119.3 24.3 %shard_map.299 = (bf16[1024,768]{1,0:T(8,128)(2,1)}, f32[8,768]{1,0:T(8,128)}, bf16[1024,768]{1,0:T(8,128)(2,1)}, f32[1024,768]{1,0:T(8,128)}, f32[1024,768]{1,0...) custom-call(s32[4]{0:T(128)} %pad_add_fusion.place_ref.refs_0_.refs_, ...), custom_call_target="tpu_custom_call" | custom-call | flops 3000000000 | bytes 500000 | tf_op jit(solution)/shard_map/pallas_call | solution.py:522
  144.3 4.1 %collective-permute-done.22 = f32[256,768]{1,0:T(8,128)S(1)} collective-permute-done((f32[256,768]{1,0:T(8,128)}, f32[256,768]{1,0:T(8,128)S(1)}, u32[]{:S(2)}, u32[]{:S(2)}) %collective-permute-start.22) | collective-permute-done | bytes 786464 | tf_op jit(solution)/shard_map/ppermute | solution.py:1019
  149.7 1.9 maximum_select_fusion.refs_4_
  151.6 42.9 %shard_map.300 = (bf16[1024,768]{1,0:T(8,128)(2,1)}, f32[1024,768]{1,0:T(8,128)}, bf16[384,5632]{1,0:T(8,128)(2,1)}, f32[8,768]{1,0:T(8,128)}, bf16[1024,768]{1,...) custom-call(s32[4]{0:T(128)} %pad_add_fusion.place_ref.refs_0_.refs_1_, ...), custom_call_target="tpu_custom_call" | custom-call | flops 4000000000 | bytes 500000 | tf_op jit(solution)/shard_map/pallas_call | solution.py:522
  197.3 1.8 collective-permute-start.24
  199.4 17.8 %shard_map.301 = (f32[1024,768]{1,0:T(8,128)}, bf16[1024,768]{1,0:T(8,128)(2,1)}, f32[1024,768]{1,0:T(8,128)}, bf16[384,768]{1,0:T(8,128)(2,1)}, bf16[384,768]{1...) custom-call(s32[4]{0:T(128)} %pad_add_fusion.place_ref.refs_0_.refs_, ...), custom_call_target="tpu_custom_call" | custom-call | flops 2000000000 | bytes 500000 | tf_op jit(solution)/shard_map/pallas_call | solution.py:522
  217.3 1.8 collective-permute-start.25
  220.3 31.1 %shard_map.302 = (bf16[384,640]{1,0:T(8,128)(2,1)}, bf16[384,640]{1,0:T(8,128)(2,1)}, bf16[384,640]{1,0:T(8,128)(2,1)}, bf16[192,640]{1,0:T(8,128)(2,1)}, bf16[1...) custom-call(bf16[1024,768]{1,0:T(8,128)(2,1)} %get-tuple-element.227.normed_ref.refs_8_.ref, ...), custom_call_target="tpu_custom_call" | custom-call | flops 3000000000 | bytes 500000 | tf_op jit(solution)/shard_map/pallas_call | solution.py:522
  252.7 2.5 shard_map.306
  256.4 1.7 collective-permute-start.33
  259.3 6.7 %shard_map.303 = (f32[1024,768]{1,0:T(8,128)}, bf16[1024,768]{1,0:T(8,128)(2,1)}, f32[8,768]{1,0:T(8,128)}) custom-call(s32[4]{0:T(128)} %pad_add_fusion.place_ref.refs_0_.refs_1_, bf16[1024,768]{1,0:T(8,128)(2,1)} %get-tuple-element.311.own_ref, bf16[1024,768]{1,0:T(8,128)(2,1)} %copy-done.3, bf16[1024,768]{1,0:T(8,128)(2,1)} %maximum_select_fusion.1.refs_0_.refs_1_.h_ref, ...), custom_call_target="tpu_custom_call" | custom-call | flops 30000000 | bytes 500000 | tf_op jit(solution)/shard_map/pallas_call | solution.py:522
  266.8 2.4 shard_map.305
  270.4 3.6 %shard_map.304.refs_0_.refs_1_ = bf16[2,512,768]{2,1,0:T(8,128)(2,1)} custom-call(s32[4]{0:T(128)} %pad_add_fusion.place_ref.refs_0_.refs_1_, bf16[1024,768]{1,0:T(8,128)(2,1)} %get-tuple-element.275.own_ref, bf16[512,768]{1,0:T(8,128)(2,1)} %copy-done.10, bf16[384,640]{1,0:T(8,128)(2,1)} %get-tuple-element.329.refs_0_.refs_2_), custom_call_target="tpu_custom_call" | custom-call | bytes 500000 | tf_op jit(solution)/shard_map/pallas_call | solution.py:730
  274.0 9.3 %collective-permute-done.30.refs_3_ = bf16[384,640]{1,0:T(8,128)(2,1)S(1)} collective-permute-done((bf16[384,640]{1,0:T(8,128)(2,1)}, bf16[384,640]{1,0:T(8,128)(2,1)S(1)}, u32[]{:S(2)}, u32[]{:S(2)}) %collective-permute-start.30) | collective-permute-done | bytes 491552 | tf_op jit(solution)/shard_map/ppermute | solution.py:1063
  284.2 3.3 shard_map.307.refs_0_
  289.0 1.7 collective-permute-start.35
  290.8 3.1 collective-permute-done.35.away_ref
  294.5 1.6 shard_map.310
  299.6 1.8 collective-permute-start.34
  302.9 4.5 %collective-permute-start.38 = (f32[32,384]{1,0:T(8,128)S(1)}, f32[32,384]{1,0:T(8,128)S(1)}, u32[]{:S(2)}, u32[]{:S(2)}) collective-permute-start(f32[32,384]{1,0:T(8,128)S(1)} %add.69), channel_id=1, source_target_pairs={{0,4},{2,6},{4,8},{6,10},{8,12},{10,14},{1,5},{3,7},{5,9},{7,11},{... | collective-permute-start | bytes 147464 | tf_op jit(solution)/shard_map/ppermute | solution.py:1079
  307.5 2.3 collective-permute-done.39
  313.1 2.2 shard_map.312
  316.5 1.8 collective-permute-start.44
  318.6 1.7 collective-permute-start.45
  324.7 4.1 %shard_map.309.refs_0_ = f32[2,512,768]{2,1,0:T(8,128)} custom-call(s32[4]{0:T(128)} %pad_add_fusion.place_ref.refs_0_.refs_1_, f32[1024,768]{1,0:T(8,128)} %get-tuple-element.343.own_ref, bf16[512,768]{1,0:T(8,128)(2,1)} %copy-done.11), custom_call_target="tpu_custom_call" | custom-call | bytes 500000 | tf_op jit(solution)/shard_map/pallas_call | solution.py:730
  328.8 1.8 collective-permute-done.44
  334.4 1.8 collective-permute-start.48
  341.3 2.3 shard_map.313
  (184 shorter events, 67.3 us)
Async XLA Ops:
  7.2 57.2 %all-gather.3.cloned.1.call-start = ((), (), s32[]{:S(2)}) async-start(), calls=%async_computation.2 | async-start | bytes 1351680 | tf_op jit(solution)/shard_map/all_gather | solution.py:1069
  12.6 23.7 %collective-permute-start.1 = (bf16[256,768]{1,0:T(8,128)(2,1)S(1)}, bf16[256,768]{1,0:T(8,128)(2,1)}, u32[]{:S(2)}, u32[]{:S(2)}) collective-permute-start(bf16[256,768]{1,0:T(8,128)(2,1)S(1)} %dynamic-slice_bitcast_fusion.3), channel_id=1, source_target_pairs={{0,1},{1,0},{2,3},{3,2},{4,5},{5,4},{6,7},{7,6},{8,9},{9,8},{10,11... | collective-permute-start | bytes 1179656 | tf_op jit(solution)/shard_map/ppermute | solution.py:1019
  17.9 18.4 %collective-permute-start.2 = (bf16[32,384]{1,0:T(8,128)(2,1)}, bf16[32,384]{1,0:T(8,128)(2,1)S(1)}, u32[]{:S(2)}, u32[]{:S(2)}) collective-permute-start(bf16[32,384]{1,0:T(8,128)(2,1)} %get-tuple-element.195), channel_id=1, source_target_pairs={{0,1},{1,0},{2,3},{3,2},{4,5},{5,4},{6,7},{7,6},{8,9},{9,8},{10,11... | collective-permute-start | bytes 73736 | tf_op jit(solution)/shard_map/ppermute | solution.py:1019
  36.3 82.6 %all-gather.5.cloned.1.call-start = ((), (), s32[]{:S(2)}) async-start(), calls=%async_computation.3 | async-start | bytes 2949120 | tf_op jit(solution)/shard_map/all_gather | solution.py:1069
  36.4 15.9 %collective-permute-start.5 = (bf16[384,640]{1,0:T(8,128)(2,1)}, bf16[384,640]{1,0:T(8,128)(2,1)}, u32[]{:S(2)}, u32[]{:S(2)}) collective-permute-start(bf16[384,640]{1,0:T(8,128)(2,1)} %all_gather.9.refs_2_.refs_4_), channel_id=1, source_target_pairs={{0,1},{1,0},{2,3},{3,2},{4,5},{5,4},{6,7},{7,6},{8,9},{9,8},{10,11... | collective-permute-start | bytes 1474568 | tf_op jit(solution)/shard_map/ppermute | solution.py:1019
  37.9 17.6 %collective-permute-start.4 = (bf16[384,640]{1,0:T(8,128)(2,1)}, bf16[384,640]{1,0:T(8,128)(2,1)}, u32[]{:S(2)}, u32[]{:S(2)}) collective-permute-start(bf16[384,640]{1,0:T(8,128)(2,1)} %all_gather.9.refs_2_.refs_4_), channel_id=1, source_target_pairs={{0,2},{2,0},{4,6},{6,4},{8,10},{10,8},{12,14},{14,12},{1,3},{3,1},... | collective-permute-start | bytes 1474568 | tf_op jit(solution)/shard_map/ppermute | solution.py:1063
  39.4 19.4 %collective-permute-start.3 = (bf16[256,768]{1,0:T(8,128)(2,1)}, bf16[256,768]{1,0:T(8,128)(2,1)}, u32[]{:S(2)}, u32[]{:S(2)}) collective-permute-start(bf16[256,768]{1,0:T(8,128)(2,1)} %collective-permute-done.1), channel_id=1, source_target_pairs={{0,16},{16,0},{1,17},{17,1},{2,18},{18,2},{3,19},{19,3},{4,20},{20... | collective-permute-start | bytes 1179656 | tf_op jit(solution)/shard_map/ppermute | solution.py:1019
  39.4 12.5 %collective-permute-start.8 = (bf16[96,768]{1,0:T(8,128)(2,1)}, bf16[96,768]{1,0:T(8,128)(2,1)S(1)}, u32[]{:S(2)}, u32[]{:S(2)}) collective-permute-start(bf16[96,768]{1,0:T(8,128)(2,1)} %get-tuple-element.204.refs_3_), channel_id=1, source_target_pairs={{0,2},{2,0},{4,6},{6,4},{8,10},{10,8},{12,14},{14,12},{1,3},{3,1},... | collective-permute-start | bytes 442376 | tf_op jit(solution)/shard_map/ppermute | solution.py:1063
  44.4 17.4 %collective-permute-start.9 = (bf16[96,768]{1,0:T(8,128)(2,1)}, bf16[96,768]{1,0:T(8,128)(2,1)}, u32[]{:S(2)}, u32[]{:S(2)}) collective-permute-start(bf16[96,768]{1,0:T(8,128)(2,1)} %get-tuple-element.204.refs_3_), channel_id=1, source_target_pairs={{0,1},{1,0},{2,3},{3,2},{4,5},{5,4},{6,7},{7,6},{8,9},{9,8},{10,11... | collective-permute-start | bytes 442376 | tf_op jit(solution)/shard_map/ppermute | solution.py:1019
  51.9 9.9 %collective-permute-start.10 = (bf16[96,768]{1,0:T(8,128)(2,1)S(1)}, bf16[96,768]{1,0:T(8,128)(2,1)S(1)}, u32[]{:S(2)}, u32[]{:S(2)}) collective-permute-start(bf16[96,768]{1,0:T(8,128)(2,1)S(1)} %collective-permute-done.8.refs_4_), channel_id=1, source_target_pairs={{0,1},{1,0},{2,3},{3,2},{4,5},{5,4},{6,7},{7,6},{8,9},{9,8},{10,11... | collective-permute-start | bytes 442376 | tf_op jit(solution)/shard_map/ppermute | solution.py:1019
  53.9 10.5 %collective-permute-start.7 = (bf16[192,640]{1,0:T(8,128)(2,1)}, bf16[192,640]{1,0:T(8,128)(2,1)}, u32[]{:S(2)}, u32[]{:S(2)}) collective-permute-start(bf16[192,640]{1,0:T(8,128)(2,1)} %slice.45), channel_id=1, source_target_pairs={{0,2},{2,0},{4,6},{6,4},{8,10},{10,8},{12,14},{14,12},{1,3},{3,1},... | collective-permute-start | bytes 737288 | tf_op jit(solution)/shard_map/ppermute | solution.py:1063
  57.1 7.3 %collective-permute-start.6 = (bf16[192,640]{1,0:T(8,128)(2,1)}, bf16[192,640]{1,0:T(8,128)(2,1)}, u32[]{:S(2)}, u32[]{:S(2)}) collective-permute-start(bf16[192,640]{1,0:T(8,128)(2,1)} %slice.44), channel_id=1, source_target_pairs={{0,1},{1,0},{2,3},{3,2},{4,5},{5,4},{6,7},{7,6},{8,9},{9,8},{10,11... | collective-permute-start | bytes 737288 | tf_op jit(solution)/shard_map/ppermute | solution.py:1019
  64.5 218.8 %reduce-scatter.3.cloned.1.call-start = ((), (), s32[]{:S(2)}) async-start(), calls=%async_computation.4 | async-start | bytes 5406720 | tf_op jit(solution)/shard_map/reduce_scatter | solution.py:1072
  67.0 26.8 %collective-permute-start.12 = (bf16[384,768]{1,0:T(8,128)(2,1)}, bf16[384,768]{1,0:T(8,128)(2,1)}, u32[]{:S(2)}, u32[]{:S(2)}) collective-permute-start(bf16[384,768]{1,0:T(8,128)(2,1)} %get-tuple-element.229.refs_0_.refs_11_), channel_id=1, source_target_pairs={{0,1},{1,0},{2,3},{3,2},{4,5},{5,4},{6,7},{7,6},{8,9},{9,8},{10,11... | collective-permute-start | bytes 1769480 | tf_op jit(solution)/shard_map/ppermute | solution.py:1019
  68.4 25.4 %collective-permute-start.11 = (bf16[384,768]{1,0:T(8,128)(2,1)}, bf16[384,768]{1,0:T(8,128)(2,1)}, u32[]{:S(2)}, u32[]{:S(2)}) collective-permute-start(bf16[384,768]{1,0:T(8,128)(2,1)} %get-tuple-element.229.refs_0_.refs_11_), channel_id=1, source_target_pairs={{0,2},{2,0},{4,6},{6,4},{8,10},{10,8},{12,14},{14,12},{1,3},{3,1},... | collective-permute-start | bytes 1769480 | tf_op jit(solution)/shard_map/ppermute | solution.py:1063
  69.9 22.7 %collective-permute-start.14 = (bf16[384,640]{1,0:T(8,128)(2,1)}, bf16[384,640]{1,0:T(8,128)(2,1)S(1)}, u32[]{:S(2)}, u32[]{:S(2)}) collective-permute-start(bf16[384,640]{1,0:T(8,128)(2,1)} %get-tuple-element.241.refs_4_.refs_11_), channel_id=1, source_target_pairs={{0,1},{1,0},{2,3},{3,2},{4,5},{5,4},{6,7},{7,6},{8,9},{9,8},{10,11... | collective-permute-start | bytes 1474568 | tf_op jit(solution)/shard_map/ppermute | solution.py:1019
  70.4 23.4 %collective-permute-start.13 = (bf16[384,640]{1,0:T(8,128)(2,1)}, bf16[384,640]{1,0:T(8,128)(2,1)S(1)}, u32[]{:S(2)}, u32[]{:S(2)}) collective-permute-start(bf16[384,640]{1,0:T(8,128)(2,1)} %get-tuple-element.241.refs_4_.refs_11_), channel_id=1, source_target_pairs={{0,2},{2,0},{4,6},{6,4},{8,10},{10,8},{12,14},{14,12},{1,3},{3,1},... | collective-permute-start | bytes 1474568 | tf_op jit(solution)/shard_map/ppermute | solution.py:1063
  96.0 9.4 %collective-permute-start.16 = (bf16[192,768]{1,0:T(8,128)(2,1)S(1)}, bf16[192,768]{1,0:T(8,128)(2,1)S(1)}, u32[]{:S(2)}, u32[]{:S(2)}) collective-permute-start(bf16[192,768]{1,0:T(8,128)(2,1)S(1)} %slice.36), channel_id=1, source_target_pairs={{0,2},{2,0},{4,6},{6,4},{8,10},{10,8},{12,14},{14,12},{1,3},{3,1},... | collective-permute-start | bytes 884744 | tf_op jit(solution)/shard_map/ppermute | solution.py:1063
  97.5 9.8 %collective-permute-start.15 = (bf16[192,768]{1,0:T(8,128)(2,1)S(1)}, bf16[192,768]{1,0:T(8,128)(2,1)S(1)}, u32[]{:S(2)}, u32[]{:S(2)}) collective-permute-start(bf16[192,768]{1,0:T(8,128)(2,1)S(1)} %slice.35), channel_id=1, source_target_pairs={{0,1},{1,0},{2,3},{3,2},{4,5},{5,4},{6,7},{7,6},{8,9},{9,8},{10,11... | collective-permute-start | bytes 884744 | tf_op jit(solution)/shard_map/ppermute | solution.py:1019
  100.7 14.0 %collective-permute-start.18 = (bf16[192,640]{1,0:T(8,128)(2,1)}, bf16[192,640]{1,0:T(8,128)(2,1)}, u32[]{:S(2)}, u32[]{:S(2)}) collective-permute-start(bf16[192,640]{1,0:T(8,128)(2,1)} %slice.38), channel_id=1, source_target_pairs={{0,2},{2,0},{4,6},{6,4},{8,10},{10,8},{12,14},{14,12},{1,3},{3,1},... | collective-permute-start | bytes 737288 | tf_op jit(solution)/shard_map/ppermute | solution.py:1063
  101.3 13.4 %collective-permute-start.17 = (bf16[192,640]{1,0:T(8,128)(2,1)S(1)}, bf16[192,640]{1,0:T(8,128)(2,1)}, u32[]{:S(2)}, u32[]{:S(2)}) collective-permute-start(bf16[192,640]{1,0:T(8,128)(2,1)S(1)} %slice.37), channel_id=1, source_target_pairs={{0,1},{1,0},{2,3},{3,2},{4,5},{5,4},{6,7},{7,6},{8,9},{9,8},{10,11... | collective-permute-start | bytes 737288 | tf_op jit(solution)/shard_map/ppermute | solution.py:1019
  114.7 4.2 %collective-permute-start.19 = (bf16[1024,896]{1,0:T(8,128)(2,1)}, bf16[1024,896]{1,0:T(8,128)(2,1)}, u32[]{:S(2)}, u32[]{:S(2)}) collective-permute-start(bf16[1024,896]{1,0:T(8,128)(2,1)} %get-tuple-element.239.refs_2_.refs_1_), channel_id=1, source_target_pairs={{0,16},{16,0},{1,17},{17,1},{2,18},{18,2},{3,19},{19,3},{4,20},{20... | collective-permute-start | bytes 5505032 | tf_op jit(solution)/shard_map/ppermute | solution.py:1019
  119.0 24.7 %collective-permute-start.20 = (f32[256,768]{1,0:T(8,128)S(1)}, f32[256,768]{1,0:T(8,128)}, u32[]{:S(2)}, u32[]{:S(2)}) collective-permute-start(f32[256,768]{1,0:T(8,128)S(1)} %dynamic-slice_bitcast_fusion.1), channel_id=1, source_target_pairs={{0,1},{1,0},{2,3},{3,2},{4,5},{5,4},{6,7},{7,6},{8,9},{9,8},{10,11... | collective-permute-start | bytes 2359304 | tf_op jit(solution)/shard_map/ppermute | solution.py:1019
  143.6 8.0 %collective-permute-start.21 = (bf16[1024,896]{1,0:T(8,128)(2,1)}, bf16[1024,896]{1,0:T(8,128)(2,1)}, u32[]{:S(2)}, u32[]{:S(2)}) collective-permute-start(bf16[1024,896]{1,0:T(8,128)(2,1)} %get-tuple-element.264.refs_2_), channel_id=1, source_target_pairs={{0,16},{16,0},{1,17},{17,1},{2,18},{18,2},{3,19},{19,3},{4,20},{20... | collective-permute-start | bytes 5505032 | tf_op jit(solution)/shard_map/ppermute | solution.py:1019
  143.7 4.7 %collective-permute-start.22 = (f32[256,768]{1,0:T(8,128)}, f32[256,768]{1,0:T(8,128)S(1)}, u32[]{:S(2)}, u32[]{:S(2)}) collective-permute-start(f32[256,768]{1,0:T(8,128)} %collective-permute-done.20), channel_id=1, source_target_pairs={{0,16},{16,0},{1,17},{17,1},{2,18},{18,2},{3,19},{19,3},{4,20},{20... | collective-permute-start | bytes 2359304 | tf_op jit(solution)/shard_map/ppermute | solution.py:1019
  194.5 134.3 %reduce-scatter.5.cloned.1.call-start = ((), (), s32[]{:S(2)}) async-start(), calls=%async_computation.5 | async-start | bytes 1351680 | tf_op jit(solution)/shard_map/reduce_scatter | solution.py:1072
  197.3 20.1 %collective-permute-start.24 = (bf16[512,768]{1,0:T(8,128)(2,1)}, bf16[512,768]{1,0:T(8,128)(2,1)S(1)}, u32[]{:S(2)}, u32[]{:S(2)}) collective-permute-start(bf16[512,768]{1,0:T(8,128)(2,1)} %constant_dynamic-slice_fusion.2), channel_id=1, source_target_pairs={{0,1},{1,0},{2,3},{3,2},{4,5},{5,4},{6,7},{7,6},{8,9},{9,8},{10,11... | collective-permute-start | bytes 2359304 | tf_op jit(solution)/shard_map/ppermute | solution.py:1019
  217.3 34.1 %collective-permute-start.25 = (bf16[192,768]{1,0:T(8,128)(2,1)}, bf16[192,768]{1,0:T(8,128)(2,1)S(1)}, u32[]{:S(2)}, u32[]{:S(2)}) collective-permute-start(bf16[192,768]{1,0:T(8,128)(2,1)} %get-tuple-element.309), channel_id=1, source_target_pairs={{0,1},{1,0},{2,3},{3,2},{4,5},{5,4},{6,7},{7,6},{8,9},{9,8},{10,11... | collective-permute-start | bytes 884744 | tf_op jit(solution)/shard_map/ppermute | solution.py:1019
  219.1 32.3 %collective-permute-start.26 = (bf16[192,768]{1,0:T(8,128)(2,1)}, bf16[192,768]{1,0:T(8,128)(2,1)S(1)}, u32[]{:S(2)}, u32[]{:S(2)}) collective-permute-start(bf16[192,768]{1,0:T(8,128)(2,1)} %get-tuple-element.310), channel_id=1, source_target_pairs={{0,2},{2,0},{4,6},{6,4},{8,10},{10,8},{12,14},{14,12},{1,3},{3,1},... | collective-permute-start | bytes 884744 | tf_op jit(solution)/shard_map/ppermute | solution.py:1063
  251.4 6.7 %collective-permute-start.27 = (bf16[1024,768]{1,0:T(8,128)(2,1)}, bf16[1024,768]{1,0:T(8,128)(2,1)S(1)}, u32[]{:S(2)}, u32[]{:S(2)}) collective-permute-start(bf16[1024,768]{1,0:T(8,128)(2,1)} %get-tuple-element.311.own_ref), channel_id=1, source_target_pairs={{0,16},{16,0},{1,17},{17,1},{2,18},{18,2},{3,19},{19,3},{4,20},{20... | collective-permute-start | bytes 4718600 | tf_op jit(solution)/shard_map/ppermute | solution.py:1019
  251.5 14.5 %collective-permute-start.28 = (bf16[192,640]{1,0:T(8,128)(2,1)}, bf16[192,640]{1,0:T(8,128)(2,1)S(1)}, u32[]{:S(2)}, u32[]{:S(2)}) collective-permute-start(bf16[192,640]{1,0:T(8,128)(2,1)} %get-tuple-element.321), channel_id=1, source_target_pairs={{0,1},{1,0},{2,3},{3,2},{4,5},{5,4},{6,7},{7,6},{8,9},{9,8},{10,11... | collective-permute-start | bytes 737288 | tf_op jit(solution)/shard_map/ppermute | solution.py:1019
  251.9 14.2 %collective-permute-start.29 = (bf16[192,640]{1,0:T(8,128)(2,1)}, bf16[192,640]{1,0:T(8,128)(2,1)S(1)}, u32[]{:S(2)}, u32[]{:S(2)}) collective-permute-start(bf16[192,640]{1,0:T(8,128)(2,1)} %get-tuple-element.322), channel_id=1, source_target_pairs={{0,2},{2,0},{4,6},{6,4},{8,10},{10,8},{12,14},{14,12},{1,3},{3,1},... | collective-permute-start | bytes 737288 | tf_op jit(solution)/shard_map/ppermute | solution.py:1063
  255.2 18.7 %collective-permute-start.32 = (bf16[384,768]{1,0:T(8,128)(2,1)}, bf16[384,768]{1,0:T(8,128)(2,1)S(1)}, u32[]{:S(2)}, u32[]{:S(2)}) collective-permute-start(bf16[384,768]{1,0:T(8,128)(2,1)} %get-tuple-element.341), channel_id=1, source_target_pairs={{0,2},{2,0},{4,6},{6,4},{8,10},{10,8},{12,14},{14,12},{1,3},{3,1},... | collective-permute-start | bytes 1769480 | tf_op jit(solution)/shard_map/ppermute | solution.py:1063
  256.4 17.5 %collective-permute-start.33 = (bf16[384,768]{1,0:T(8,128)(2,1)}, bf16[384,768]{1,0:T(8,128)(2,1)S(1)}, u32[]{:S(2)}, u32[]{:S(2)}) collective-permute-start(bf16[384,768]{1,0:T(8,128)(2,1)} %get-tuple-element.342), channel_id=1, source_target_pairs={{0,1},{1,0},{2,3},{3,2},{4,5},{5,4},{6,7},{7,6},{8,9},{9,8},{10,11... | collective-permute-start | bytes 1769480 | tf_op jit(solution)/shard_map/ppermute | solution.py:1019
  269.2 14.1 %collective-permute-start.30 = (bf16[384,640]{1,0:T(8,128)(2,1)}, bf16[384,640]{1,0:T(8,128)(2,1)S(1)}, u32[]{:S(2)}, u32[]{:S(2)}) collective-permute-start(bf16[384,640]{1,0:T(8,128)(2,1)} %get-tuple-element.335), channel_id=1, source_target_pairs={{0,2},{2,0},{4,6},{6,4},{8,10},{10,8},{12,14},{14,12},{1,3},{3,1},... | collective-permute-start | bytes 1474568 | tf_op jit(solution)/shard_map/ppermute | solution.py:1063
  270.1 13.2 %collective-permute-start.31 = (bf16[384,640]{1,0:T(8,128)(2,1)}, bf16[384,640]{1,0:T(8,128)(2,1)S(1)}, u32[]{:S(2)}, u32[]{:S(2)}) collective-permute-start(bf16[384,640]{1,0:T(8,128)(2,1)} %get-tuple-element.336), channel_id=1, source_target_pairs={{0,1},{1,0},{2,3},{3,2},{4,5},{5,4},{6,7},{7,6},{8,9},{9,8},{10,11... | collective-permute-start | bytes 1474568 | tf_op jit(solution)/shard_map/ppermute | solution.py:1019
  289.0 4.8 %collective-permute-start.35 = (f32[32,768]{1,0:T(8,128)}, f32[32,768]{1,0:T(8,128)S(1)}, u32[]{:S(2)}, u32[]{:S(2)}) collective-permute-start(f32[32,768]{1,0:T(8,128)} %shard_map.308.own_ref), channel_id=1, source_target_pairs={{0,1},{1,0},{2,3},{3,2},{4,5},{5,4},{6,7},{7,6},{8,9},{9,8},{10,11... | collective-permute-start | bytes 294920 | tf_op jit(solution)/shard_map/ppermute | solution.py:1019
  299.6 24.2 %collective-permute-start.34 = (bf16[512,768]{1,0:T(8,128)(2,1)S(1)}, bf16[512,768]{1,0:T(8,128)(2,1)S(1)}, u32[]{:S(2)}, u32[]{:S(2)}) collective-permute-start(bf16[512,768]{1,0:T(8,128)(2,1)S(1)} %constant_dynamic-slice_fusion.1), channel_id=1, source_target_pairs={{0,1},{1,0},{2,3},{3,2},{4,5},{5,4},{6,7},{7,6},{8,9},{9,8},{10,11... | collective-permute-start | bytes 2359304 | tf_op jit(solution)/shard_map/ppermute | solution.py:1019
  301.6 8.2 %collective-permute-start.39 = (f32[32,384]{1,0:T(8,128)S(1)}, f32[32,384]{1,0:T(8,128)S(1)}, u32[]{:S(2)}, u32[]{:S(2)}) collective-permute-start(f32[32,384]{1,0:T(8,128)S(1)} %add.69), channel_id=1, source_target_pairs={{4,0},{6,2},{8,4},{10,6},{12,8},{14,10},{5,1},{7,3},{9,5},{11,7},{... | collective-permute-start | bytes 147464 | tf_op jit(solution)/shard_map/ppermute | solution.py:1079
  302.9 8.2 %collective-permute-start.38 = (f32[32,384]{1,0:T(8,128)S(1)}, f32[32,384]{1,0:T(8,128)S(1)}, u32[]{:S(2)}, u32[]{:S(2)}) collective-permute-start(f32[32,384]{1,0:T(8,128)S(1)} %add.69), channel_id=1, source_target_pairs={{0,4},{2,6},{4,8},{6,10},{8,12},{10,14},{1,5},{3,7},{5,9},{7,11},{... | collective-permute-start | bytes 147464 | tf_op jit(solution)/shard_map/ppermute | solution.py:1079
  309.8 6.7 %collective-permute-start.41 = (f32[32,384]{1,0:T(8,128)S(1)}, f32[32,384]{1,0:T(8,128)S(1)}, u32[]{:S(2)}, u32[]{:S(2)}) collective-permute-start(f32[32,384]{1,0:T(8,128)S(1)} %collective-permute-done.39), channel_id=1, source_target_pairs={{8,4},{10,6},{4,0},{6,2},{9,5},{11,7},{5,1},{7,3},{24,20},{26,22},... | collective-permute-start | bytes 147464 | tf_op jit(solution)/shard_map/ppermute | solution.py:1079
  311.1 7.5 %collective-permute-start.42 = (f32[32,384]{1,0:T(8,128)S(1)}, f32[32,384]{1,0:T(8,128)S(1)}, u32[]{:S(2)}, u32[]{:S(2)}) collective-permute-start(f32[32,384]{1,0:T(8,128)S(1)} %broadcast_select_fusion.7), channel_id=1, source_target_pairs={{4,12},{6,14},{8,0},{10,2},{5,13},{7,15},{9,1},{11,3},{20,28},{22,... | collective-permute-start | bytes 147464 | tf_op jit(solution)/shard_map/ppermute | solution.py:1079
  312.4 7.9 %collective-permute-start.40 = (f32[32,384]{1,0:T(8,128)S(1)}, f32[32,384]{1,0:T(8,128)S(1)}, u32[]{:S(2)}, u32[]{:S(2)}) collective-permute-start(f32[32,384]{1,0:T(8,128)S(1)} %collective-permute-done.38), channel_id=1, source_target_pairs={{4,8},{6,10},{8,12},{10,14},{5,9},{7,11},{9,13},{11,15},{20,24},{2... | collective-permute-start | bytes 147464 | tf_op jit(solution)/shard_map/ppermute | solution.py:1079
  315.4 13.4 %collective-permute-start.43 = (bf16[96,1408]{1,0:T(8,128)(2,1)}, bf16[96,1408]{1,0:T(8,128)(2,1)S(1)}, u32[]{:S(2)}, u32[]{:S(2)}) collective-permute-start(bf16[96,1408]{1,0:T(8,128)(2,1)} %get-tuple-element.361), channel_id=1, source_target_pairs={{0,2},{2,0},{4,6},{6,4},{8,10},{10,8},{12,14},{14,12},{1,3},{3,1},... | collective-permute-start | bytes 811016 | tf_op jit(solution)/shard_map/ppermute | solution.py:1063
  316.5 14.1 %collective-permute-start.44 = (bf16[96,1408]{1,0:T(8,128)(2,1)}, bf16[96,1408]{1,0:T(8,128)(2,1)S(1)}, u32[]{:S(2)}, u32[]{:S(2)}) collective-permute-start(bf16[96,1408]{1,0:T(8,128)(2,1)} %get-tuple-element.362), channel_id=1, source_target_pairs={{0,1},{1,0},{2,3},{3,2},{4,5},{5,4},{6,7},{7,6},{8,9},{9,8},{10,11... | collective-permute-start | bytes 811016 | tf_op jit(solution)/shard_map/ppermute | solution.py:1019
  318.6 12.0 %collective-permute-start.45 = (bf16[96,1408]{1,0:T(8,128)(2,1)}, bf16[96,1408]{1,0:T(8,128)(2,1)S(1)}, u32[]{:S(2)}, u32[]{:S(2)}) collective-permute-start(bf16[96,1408]{1,0:T(8,128)(2,1)} %get-tuple-element.363), channel_id=1, source_target_pairs={{0,3},{1,2},{2,1},{3,0},{4,7},{5,6},{6,5},{7,4},{8,11},{9,10},{10,... | collective-permute-start | bytes 811016 | tf_op jit(solution)/shard_map/ppermute | solution.py:1252
  333.5 6.5 %collective-permute-start.46 = (bf16[96,1408]{1,0:T(8,128)(2,1)S(1)}, bf16[96,1408]{1,0:T(8,128)(2,1)S(1)}, u32[]{:S(2)}, u32[]{:S(2)}) collective-permute-start(bf16[96,1408]{1,0:T(8,128)(2,1)S(1)} %get-tuple-element.384), channel_id=1, source_target_pairs={{0,16},{16,0},{1,17},{17,1},{2,18},{18,2},{3,19},{19,3},{4,20},{20... | collective-permute-start | bytes 811016 | tf_op jit(solution)/shard_map/ppermute | solution.py:1019
  334.4 4.6 %collective-permute-start.48 = (bf16[96,128]{1,0:T(8,128)(2,1)S(1)}, bf16[96,128]{1,0:T(8,128)(2,1)S(1)}, u32[]{:S(2)}, u32[]{:S(2)}) collective-permute-start(bf16[96,128]{1,0:T(8,128)(2,1)S(1)} %get-tuple-element.390), channel_id=1, source_target_pairs={{0,17},{1,16},{16,1},{17,0},{2,19},{3,18},{18,3},{19,2},{4,21},{5,... | collective-permute-start | bytes 73736 | tf_op jit(solution)/shard_map/ppermute | solution.py:1024
  (39 other events, 283.2 us)
Sparse Core Ops, SparseCore 0:
  36.4 27.9 all-gather.2
  66.0 49.9 all-gather.4
  194.6 78.3 reduce-scatter.2
  287.6 28.6 reduce-scatter.4

commit v3 on v2

--- a/solution.py
+++ b/solution.py
@@ -104,46 +104,35 @@
     return total * inverse, total, inverse
 
 
-def pieces_of(rows, places):
-    half = places // 2
-    return ((False, False, 0, places), (True, False, 0, places), (False, True, 0, places), (True, True, 0, half), (True, True, half, places - half))
+PLANE = ((False, False), (True, False), (False, True), (True, True))
 
 
 def load_weights(weights, start, refs, columns, rows, place_ref):
     first, last = columns
-    places = weights.shape[0] // (2 * rows)
     mine = place_ref[0]
     size = refs[0].shape[1] // 4
-    for index, (moved, turned, base, count) in enumerate(pieces_of(rows, places)):
-        if len(refs) == 1:
-            if index == 4:
-                break
-            ref, offset, base, count = refs[0], index * size, 0, places
-        else:
-            ref, offset = refs[index], 0
+    base = 0
+    for index in range(len(refs) if len(refs) > 1 else 4):
+        moved, turned = PLANE[min(index, 3)]
+        ref, offset = (refs[0], index * size) if len(refs) == 1 else (refs[index], 0)
         place = 1 - mine if moved else mine
         target = start + (last - first if turned else 0)
-        for step in range(count):
+        for step in range(ref.shape[0] // rows):
             row = pl.multiple_of((2 * (base + step) + place) * rows, 32)
             weights[pl.ds(row, rows), target : target + last - first] = ref[step * rows : (step + 1) * rows, offset + first : offset + last]
+        base = ref.shape[0] // rows if index == 3 else 0
 
 
 def store_grads(refs, columns, acc, start, rows, place_ref, base=0):
     first, last = columns
-    places = acc.shape[0] // (2 * rows)
     mine = place_ref[0]
     size = refs[0].shape[1] // 4
-    for index, (moved, turned, origin, count) in enumerate(pieces_of(rows, places)):
-        if len(refs) == 1:
-            if index == 4:
-                break
-            ref, offset, origin, count = refs[0], index * size + base, 0, places
-        else:
-            ref, offset = refs[index], 0
+    for index, (moved, turned) in enumerate(PLANE):
+        ref, offset = (refs[0], index * size + base) if len(refs) == 1 else (refs[index], 0)
         place = 1 - mine if moved else mine
         source = start + (last - first if turned else 0)
-        for step in range(count):
-            row = pl.multiple_of((2 * (origin + step) + place) * rows, 32)
+        for step in range(ref.shape[0] // rows):
+            row = pl.multiple_of((2 * step + place) * rows, 32)
             block = acc[pl.ds(row, rows), source : source + last - first]
             ref[step * rows : (step + 1) * rows, offset + first : offset + last] = block.astype(bf16)
 
@@ -267,7 +256,7 @@
 def gate_backward_kernel(second, rows, pieces, grad_arrays, base, *refs):
     place_ref, refs = refs[0], refs[1:]
     if second:
-        (h_ref, own_ref, other_ref, target_ref), refs = refs[:4], refs[4:]
+        (h_ref, own_ref, other_ref, teacher_ref, here_ref, beside_ref), refs = refs[:6], refs[6:]
     else:
         (own_ref, other_ref, next_h_ref, next_out_ref, grad_own_ref, grad_other_ref, next_gain_ref), refs = refs[:7], refs[7:]
     (normed_ref, gate_ref, y_ref), parts, refs = refs[:3], refs[3 : 3 + pieces], refs[3 + pieces :]
@@ -290,7 +279,12 @@
     if second:
         produced = h_ref[...].astype(f32) + branch
         out_ref[...] = jnp.where(place_ref[3] == 0, h_ref[...].astype(f32), produced).astype(bf16)
-        grad_out = marks_ref[:, 9:10] * (produced - target_ref[...])
+        steps = pl.num_programs(0)
+        chunk = steps - 1 - pl.program_id(0)
+        held = jnp.where(place_ref[1] == 0, teacher_ref[0], teacher_ref[1])
+        came = jnp.where(chunk % (steps // 2) == place_ref[3], here_ref[...], beside_ref[...])
+        target = jnp.where(chunk // (steps // 2) == place_ref[1], held, came)
+        grad_out = marks_ref[:, 9:10] * (produced - target)
     else:
         grad_normed = grad_own_ref[...].astype(f32) + grad_other_ref[...].astype(f32)
         grad_out, gain_term = norm_backward(grad_normed, next_h_ref[...].astype(f32), next_out_ref[...], next_gain_ref[0:1, :])
@@ -473,13 +467,13 @@
 
 
 def second_backward_kernel(heads, rows, *refs):
-    gate_inputs, refs = refs[:11], refs[11:]
+    gate_inputs, refs = refs[:13], refs[13:]
     scan_weights, (segment_ref, states_small_ref, head_ref, spread_ref), refs = refs[:5], refs[5:9], refs[9:]
     (raw_ref, conv_ref, raw_states_ref, conv_states_ref, steps_ref, entry_state_ref), refs = refs[:6], refs[6:]
     (out_ref, grad_out_ref, grads_ref, gate_sums_ref, part_ref, sums_ref, states_sums_ref), refs = refs[:7], refs[7:]
     grad_y, gate_part, refs = refs[0], refs[1], refs[2:]
     gate_scratch, scan_scratch = refs[:5], refs[5:]
-    place_ref, normed_ref, y_ref, marks_ref, small_ref = gate_inputs[0], gate_inputs[5], gate_inputs[7], gate_inputs[9], gate_inputs[10]
+    place_ref, normed_ref, y_ref, marks_ref, small_ref = gate_inputs[0], gate_inputs[7], gate_inputs[9], gate_inputs[11], gate_inputs[12]
     base = scan_weights[0].shape[1]
     gate_backward_kernel(
         True, rows, 1, 1, base, *gate_inputs, out_ref, grad_out_ref, grad_y, gate_part, grads_ref, gate_sums_ref, *gate_scratch
@@ -539,12 +533,9 @@
     return array, pl.BlockSpec(memory_space=pltpu.SMEM)
 
 
-def grad_outputs(width, rows, columns):
-    outputs = []
-    for _, _, _, count in pieces_of(rows, width // (2 * rows)):
-        shape = (count * rows, columns)
-        outputs.append((shape, bf16, pl.BlockSpec(shape, lambda i: (0, 0))))
-    return outputs
+def grad_outputs(width, columns):
+    shape = (width // 2, columns)
+    return [(shape, bf16, pl.BlockSpec(shape, lambda i: (0, 0)))] * 4
 
 
 def awaited(arrays):
@@ -603,10 +594,10 @@
     inputs += [fixed(w) for w in weights] + [(marks, rows_spec(LANES)), fixed(params[0])]
     outputs = [((length, width), bf16, rows_spec(width))] if second else []
     outputs += [((length, width), f32, rows_spec(width)), ((length, units), bf16, rows_spec(units)), ((length, width), f32, rows_spec(width))]
-    outputs += grad_outputs(width, rows, units)
+    outputs += grad_outputs(width, units)
     outputs.append(((8, units), f32, pl.BlockSpec((8, units), lambda i: (0, 0))))
     scratch = [((width, units), bf16)] * 2 + [((width, units), f32)] * 2 + [((8, units), f32)]
-    results = call(functools.partial(gate_backward_kernel, second, rows, len(weights), 5, 0), inputs, outputs, scratch, length // SPAN, 2_000_000_000)
+    results = call(functools.partial(gate_backward_kernel, second, rows, len(weights), 4, 0), inputs, outputs, scratch, length // SPAN, 2_000_000_000)
     if not second:
         results = [None] + list(results)
     return results
@@ -637,7 +628,7 @@
     inputs += [fixed(p) for p in params] + [fixed(spreader_of(units))]
     inputs += [(s, rows_spec(s.shape[1], last)) for s in saved[:6]]
     inputs.append((saved[6], pl.BlockSpec((1, STATE, units), lambda i: (last - i, 0, 0))))
-    outputs = grad_outputs(width, rows, units // 2 + 2 * STATE)
+    outputs = grad_outputs(width, units // 2 + 2 * STATE)
     outputs.append(((length, width), bf16, rows_spec(width, last)))
     for columns in (units, 2 * STATE):
         outputs.append(((8, columns), f32, pl.BlockSpec((8, columns), lambda i: (0, 0))))
@@ -666,13 +657,14 @@
     return results[0], results[1], results[2], results[3:10], results[10], results[11]
 
 
-def second_backward(place, rows, h, parts, target, normed, gate, weights, gate_weights, marks, segment_row, params, saved):
+def second_backward(place, rows, h, parts, teacher, here, beside, normed, gate, weights, gate_weights, marks, segment_row, params, saved):
     length, width = normed.shape
     units = params[0].shape[1]
     chunks = length // SPAN
     last = chunks - 1
     inputs = [scalars(place), (h, rows_spec(width, last))] + [(part, rows_spec(width + LANES, last)) for part in parts]
-    inputs += [(target, rows_spec(width, last)), (normed, rows_spec(width, last)), (gate, rows_spec(units, last))]
+    inputs.append((teacher, pl.BlockSpec((2, SPAN, width), lambda i: (0, (last - i) % (chunks // 2), 0))))
+    inputs += [fixed(here), fixed(beside), (normed, rows_spec(width, last)), (gate, rows_spec(units, last))]
     inputs += [(saved[2], rows_spec(units, last)), fixed(gate_weights), (marks, rows_spec(LANES, last)), fixed(params[0])]
     inputs += [fixed(w) for w in weights] + [(segment_row, pl.BlockSpec((1, SPAN), lambda i: (0, last - i)))]
     inputs += [fixed(params[1]), fixed(params[2]), fixed(spreader_of(units))]
@@ -693,10 +685,12 @@
     return call(kernel, inputs, outputs, scratch, chunks, 4_000_000_000)
 
 
-def finish_kernel(place_ref, own_ref, other_ref, h_ref, grad_out_ref, gain_ref, *refs):
-    grad_ref, low_ref, sums_ref, sums = refs[-4:]
-
-    @pl.when(pl.program_id(0) == 0)
+def finish_kernel(
+    place_ref, own_ref, other_ref, h_ref, grad_out_ref, gain_ref, rows_ref, away_ref, grad_ref, low_ref, sums_ref, placed_ref, sums
+):
+    step = pl.program_id(0)
+
+    @pl.when(step == 0)
     def _():
         sums[...] = jnp.zeros_like(sums)
 
@@ -704,45 +698,89 @@
     next_grad = grad_out_ref[...]
     grad, gain_term = norm_backward(grad_normed, h_ref[...].astype(f32), next_grad.astype(bf16).astype(f32), gain_ref[0:1, :])
     rows = jnp.where(place_ref[3] == 0, grad, next_grad)
-    grad_ref[...] = rows
-    low_ref[...] = rows.astype(bf16)
     sums[0:1, :] += jnp.sum(gain_term, axis=0, keepdims=True)
     sums_ref[...] = sums[...]
 
-
-def finish(place, own, other, h, grad_out, gain, ready):
+    @pl.when(step < pl.num_programs(0) // 2)
+    def _():
+        low_ref[...] = rows.astype(bf16)
+        placed_ref[0] = away_ref[...]
+
+    @pl.when(step >= pl.num_programs(0) // 2)
+    def _():
+        grad_ref[0] = rows
+        placed_ref[0] = rows_ref[...]
+
+
+def finish(place, own, other, h, grad_out, gain, produced, produced_away):
     length, width = h.shape
-    inputs = [scalars(place)] + [(rows, rows_spec(width)) for rows in (own, other, h, grad_out)] + [fixed(gain)]
-    inputs += awaited(ready)
-    outputs = [((length, width), f32, rows_spec(width)), ((length, width), bf16, rows_spec(width))]
-    outputs.append(((8, width), f32, pl.BlockSpec((8, width), lambda i: (0, 0))))
-    return call(finish_kernel, inputs, outputs, [((8, width), f32)], length // SPAN, 30_000_000)
-
-
-def placed_kernel(place_ref, own_ref, away_ref, *refs):
-    out_ref = refs[-1]
-    own = pl.program_id(0) == place_ref[1]
-    out_ref[0] = jnp.where(own, own_ref[...].astype(f32), away_ref[...].astype(f32)).astype(out_ref.dtype)
-
-
-def placed_rows(place, rows, away, ready=()):
+    steps = length // SPAN
+    part = steps // 2
+
+    def rows(i, place):
+        return ((i + part * (1 - place[1])) % steps, 0)
+
+    block = pl.BlockSpec((SPAN, width), rows)
+    whole = pl.BlockSpec((8, width), lambda i, place: (0, 0))
+
+    def early(i):
+        return jnp.minimum(i, part - 1)
+
+    def late(i):
+        return jnp.maximum(i - part, 0)
+
+    def placed(i, place):
+        return (jnp.where(i < part, 1 - place[1], place[1]), jnp.where(i < part, i, i - part), 0)
+
+    return pl.pallas_call(
+        finish_kernel,
+        grid_spec=pltpu.PrefetchScalarGridSpec(
+            num_scalar_prefetch=1,
+            grid=(steps,),
+            in_specs=[block] * 4
+            + [
+                whole,
+                pl.BlockSpec((SPAN, width), lambda i, place: (part * place[1] + late(i), 0)),
+                pl.BlockSpec((SPAN, width), lambda i, place: (early(i), 0)),
+            ],
+            out_specs=[
+                pl.BlockSpec((1, SPAN, width), lambda i, place: (place[1], late(i), 0)),
+                pl.BlockSpec((SPAN, width), lambda i, place: (early(i), 0)),
+                whole,
+                pl.BlockSpec((1, SPAN, width), placed),
+            ],
+            scratch_shapes=[pltpu.VMEM((8, width), f32)],
+        ),
+        out_shape=[
+            jax.ShapeDtypeStruct((2, length // 2, width), f32),
+            jax.ShapeDtypeStruct((length // 2, width), bf16),
+            jax.ShapeDtypeStruct((8, width), f32),
+            jax.ShapeDtypeStruct((2, length // 2, width), bf16),
+        ],
+        compiler_params=pltpu.CompilerParams(vmem_limit_bytes=VMEM_LIMIT, dimension_semantics=("arbitrary",)),
+        cost_estimate=pl.CostEstimate(flops=0, bytes_accessed=500_000, transcendentals=0),
+    )(place, own, other, h, grad_out, gain, produced, produced_away)
+
+
+def placed_kernel(place_ref, away_ref, rows_ref, out_ref):
+    out_ref[0] = away_ref[...].astype(f32)
+
+
+def placed_rows(place, rows, away):
     half, width = away.shape
     return pl.pallas_call(
         placed_kernel,
         grid_spec=pltpu.PrefetchScalarGridSpec(
             num_scalar_prefetch=1,
-            grid=(2,),
-            in_specs=[
-                pl.BlockSpec((half, width), lambda m, place: (place[1], 0)),
-                pl.BlockSpec((half, width), lambda m, place: (0, 0)),
-            ]
-            + [pl.BlockSpec(memory_space=pl.ANY)] * len(ready),
-            out_specs=pl.BlockSpec((1, half, width), lambda m, place: (m, 0, 0)),
+            grid=(half // SPAN,),
+            in_specs=[pl.BlockSpec((SPAN, width), lambda i, place: (i, 0)), pl.BlockSpec(memory_space=pl.ANY)],
+            out_specs=pl.BlockSpec((1, SPAN, width), lambda i, place: (1 - place[1], i, 0)),
         ),
-        out_shape=jax.ShapeDtypeStruct((2, half, width), rows.dtype),
+        out_shape=jax.ShapeDtypeStruct(rows.shape, rows.dtype),
+        input_output_aliases={2: 0},
         compiler_params=pltpu.CompilerParams(vmem_limit_bytes=VMEM_LIMIT, dimension_semantics=("arbitrary",)),
         cost_estimate=pl.CostEstimate(flops=0, bytes_accessed=500_000, transcendentals=0),
-    )(place, rows, away, *ready)
+    )(place, away, rows)
 
 
 def marks_kernel(place_ref, lengths_ref, segments_ref, marks_ref, row_ref):
@@ -912,27 +950,13 @@
         start += out.shape[1]
 
 
-def cross_kernel(place_ref, *refs):
-    over_x, over_tensor = refs[-2:]
-    start = 0
-    for group in range(len(refs[:-2]) // 4):
-        x_ref, y_ref, first_ref, second_ref = refs[4 * group : 4 * group + 4]
-        columns = slice(start, start + x_ref.shape[1])
-        start += x_ref.shape[1]
-        half = first_ref.shape[0]
-        over_x[:half, columns] = (x_ref[:half].astype(f32) + first_ref[...].astype(f32)).astype(bf16)
-        over_x[half:, columns] = x_ref[half:]
-        over_tensor[:half, columns] = y_ref[:half]
-        over_tensor[half:, columns] = (y_ref[half:].astype(f32) + second_ref[...].astype(f32)).astype(bf16)
-
-
-def join_kernel(groups, place_ref, *refs):
+def join_kernel(place_ref, *refs):
     out = refs[-1]
     start = 0
-    for own, over_x, over_tensor, offset in groups:
-        width = refs[own].shape[1]
-        there = slice(offset, offset + width)
-        total = refs[own][...].astype(f32) + refs[over_x][:, there].astype(f32) + refs[over_tensor][:, there].astype(f32)
+    for group in range(len(refs) // 4):
+        parts = refs[4 * group : 4 * group + 4]
+        width = parts[0].shape[1]
+        total = sum(part[...].astype(f32) for part in parts)
         out[:, start : start + width] = total.astype(bf16)
         start += width
 
@@ -940,7 +964,7 @@
 def owned_kernel(place_ref, first_ref, second_ref, beside_ref, across_ref, both_ref, zx_ref, bc_ref, dt_ref, out_ref):
     first = place_ref[3] == 0
     half = out_ref.shape[1] // 2
-    heads_half = dt_ref.shape[1] // 2
+    heads_half = dt_ref.shape[0] // 2
     mine = jnp.where(first, first_ref[...], second_ref[...]).astype(f32)
     beside = beside_ref[...].astype(f32)
     lower, upper = jnp.where(first, mine, beside), jnp.where(first, beside, mine)
@@ -957,8 +981,9 @@
     bc_ref[:, STATE:] = jnp.where(straight, other, own)
     lane = lax.broadcasted_iota(jnp.int32, (1, LANES), 1)
     steps = slice(half + STATE, half + 2 * STATE)
-    both = jnp.where(lane < heads_half, lower[:, steps], pltpu.roll(upper[:, steps], heads_half, 1))
-    dt_ref[...] = both[:, : 2 * heads_half]
+    both = jnp.transpose(jnp.where(lane < heads_half, lower[:, steps], pltpu.roll(upper[:, steps], heads_half, 1)))
+    for head in range(2 * heads_half):
+        dt_ref[head] = both[head : head + 1]
 
 
 def small_kernel(gate0, scan0, states0, gate1, scan1, states1, gain_ref, out_ref):
@@ -997,18 +1022,24 @@
     half = total_ref.shape[1]
     here, there = total_ref[0:16], total_ref[16:32]
     lower, upper = jnp.where(first, here, there), jnp.where(first, there, here)
-    conv_ref[:, :half] = lower[0:5]
-    conv_ref[:, half:] = upper[0:5]
+    states = here[8:13, : 2 * STATE] + there[8:13, : 2 * STATE]
+    for row in range(5):
+        conv_ref[row, :, :half] = lower[row : row + 1]
+        conv_ref[row, :, half:] = upper[row : row + 1]
+        states_conv_ref[row] = states[row : row + 1]
     gate_gain_ref[:, :half] = lower[5:6]
     gate_gain_ref[:, half:] = upper[5:6]
-    states_conv_ref[...] = here[8:13, : 2 * STATE] + there[8:13, : 2 * STATE]
     lane = lax.broadcasted_iota(jnp.int32, (1, LANES), 1)
     for row in range(3):
         own = lower[13:14, row * LANES : (row + 1) * LANES]
         other = pltpu.roll(jnp.broadcast_to(upper[13:14, row * LANES : (row + 1) * LANES], (8, LANES)), heads_half, 1)[0:1]
         heads_ref[row : row + 1, :] = jnp.where(lane < heads_half, own, other)[:, : 2 * heads_half]
-    gain_ref[:, :half] = here[6:7]
-    gain_ref[:, half:] = here[7:8]
+    gain = jnp.concatenate([here[6:7], here[7:8]], axis=1)
+    size = gain_ref.shape[1]
+    share = jnp.zeros(gain_ref.shape, f32)
+    for rank in range(2 * half // size):
+        share = jnp.where(place_ref[2] == rank, gain[:, rank * size : (rank + 1) * size], share)
+    gain_ref[...] = share
 
 
 def tied(*values):
@@ -1071,9 +1102,9 @@
     def line_reduce(block):
         return lax.psum_scatter(block, "dp", axis_index_groups=line_groups, scatter_dimension=0, tiled=True)
 
-    def line_total(block):
+    def line_total(block, beside):
         if places != 4:
-            return lax.psum(block, "dp", axis_index_groups=line_groups)
+            return lax.psum(block, "dp", axis_index_groups=line_groups), beside
 
         def send(rows, moves):
             return lax.ppermute(rows, "dp", [(2 * a + start, 2 * b + start) for a, b in moves for start in range(2)])
@@ -1081,7 +1112,8 @@
         up, down = send(block, [(0, 1), (1, 2), (2, 3)]), send(block, [(1, 0), (2, 1), (3, 2)])
         up2, down2 = send(up, [(1, 2), (2, 3)]), send(down, [(2, 1), (1, 0)])
         far = send(jnp.where(rank // 2 == 1, up, down), [(1, 3), (2, 0)])
-        return block + up + down + up2 + down2 + far
+        up2, down2, far, beside = tied(up2, down2, far, beside)
+        return block + up + down + up2 + down2 + far, beside
 
     pack_shape = (block_rows + PARAM_ROWS, scan_columns + units)
     kept, sent = plain_call(
@@ -1103,6 +1135,12 @@
             ((2 * PARAM_ROWS, half), bf16),
         ],
     )
+
+    both_ways = [(2 * d + t, 2 * (d ^ 1) + 1 - t) for d in range(ranks) for t in range(2)]
+
+    def over_plane(own, x_block, y_block, far_block):
+        far = lax.ppermute(far_block, ("dp", "tensor"), both_ways)
+        return own, x_swapped(x_block), y_swapped(y_block), far
 
     def plane_end(block, over_x, over_tensor):
         cut = places // 2 * block_rows
@@ -1147,7 +1185,7 @@
     gate_half = gate_line, x_swapped(gate_line), y_swapped(gate_line)
     next_half = next_line, x_swapped(next_line), y_swapped(next_line)
     results = scan_forward(place, block_rows, x_rows, None, scan_first, marks, segment_row, params[0])
-    results, gate_half, next_half = tied(results, gate_half, next_half)
+    results, gate_half = tied(results, gate_half)
     _, gain_first, normed_first, saved_first = results
     gate_first = plane_end(*gate_half)
     results = gate_forward(place, block_rows, normed_first, saved_first[2], gate_first, params[0])
@@ -1160,32 +1198,10 @@
     results, here = tied(results, y_swapped(quarter(teacher)))
     hidden, gain_second, normed_second, saved_second, gated_second, part = results
     parts_second = (part, swapped(part, "section"))
-    target = whole_rows(teacher, here, swapped(here, "section"))
+    beside = swapped(here, "section")
 
     def add(*blocks):
         return sum(block.astype(f32) for block in blocks).astype(bf16)
-
-    def plane_start(pieces):
-        return tuple(pieces[:3]), (y_swapped(pieces[3]), x_swapped(pieces[4]))
-
-    def crossed(*groups):
-        arrays = [array for pieces, came in groups for array in pieces[1:] + came]
-        columns = sum(pieces[0].shape[1] for pieces, _ in groups)
-        over_x, over_tensor = plain_call(cross_kernel, place, arrays, [((places * block_rows, columns), bf16)] * 2)
-        return [pieces[0] for pieces, _ in groups], x_swapped(over_x), y_swapped(over_tensor)
-
-    def joined(*groups, ready=()):
-        arrays, spans = [], []
-        for owns, over_x, over_tensor in groups:
-            base = len(arrays)
-            arrays += list(owns) + [over_x, over_tensor]
-            offset = 0
-            for index, own in enumerate(owns):
-                spans.append((base + index, base + len(owns), base + len(owns) + 1, offset))
-                offset += own.shape[1]
-        columns = sum(arrays[span[0]].shape[1] for span in spans)
-        kernel = functools.partial(join_kernel, spans)
-        return plain_call(kernel, place, arrays, [((places * block_rows, columns), bf16)], ready)[0]
 
     def away_rows(rows):
         return y_swapped(lax.dynamic_slice_in_dim(rows, (1 - turn) * local_rows, local_rows, 0))
@@ -1195,7 +1211,9 @@
         block_rows,
         hidden,
         parts_second,
-        target,
+        teacher,
+        here,
+        beside,
         normed_second,
         gated_second,
         scan_second,
@@ -1223,54 +1241,46 @@
     )
     results, produced_away = tied(results[1:], away_rows(produced))
     grad_hidden, grad_y, gate_part = results[:3]
-    gate_reduce = plane_start(results[3:8])
-    gate_sums_first = results[8]
+    gate_reduce = over_plane(*results[3:7])
+    gate_sums_first = results[7]
     results = scan_backward(
         place, block_rows, grad_y, gate_part, normed_first, scan_first, marks, segment_row, params[0], saved_first
     )
     results, gate_reduce = tied(results, gate_reduce)
-    scan_reduce = plane_start(results[:5])
-    part, sums, states_sums = results[5:]
+    scan_reduce = over_plane(*results[:4])
+    part, sums, states_sums = results[4:]
     sums_first = (gate_sums_first, sums, states_sums)
-    crossed_gate = crossed(gate_reduce)
-    results = finish(
-        place, part, swapped(part, "section"), x_rows, grad_hidden, gain_first, (crossed_gate[0][0],)
-    )
-    (grad_rows, grad_low, gain_sums), scan_reduce = tied(results, scan_reduce)
-    scan_reduce, gain_sums = tied(scan_reduce, gain_sums)
-    crossed_scan = crossed(scan_reduce)
-    layer_outputs = placed_rows(place, produced, produced_away, (crossed_scan[0][0],))
-    blocks = joined(crossed_scan, crossed_gate, ready=(layer_outputs, quarters))
+    grad_rows, grad_low, gain_sums, layer_outputs = finish(
+        place, part, swapped(part, "section"), x_rows, grad_hidden, gain_first, produced, produced_away
+    )
+    smalls = plain_call(
+        lambda place_ref, *refs: small_kernel(*refs), place, sums_first + sums_second + (gain_sums,), [((32, units), f32)]
+    )[0]
+    smalls, scan_reduce = line_total(smalls, scan_reduce)
+    blocks = plain_call(
+        join_kernel,
+        place,
+        scan_reduce + gate_reduce,
+        [((places * block_rows, scan_columns + units), bf16)],
+        (quarters,),
+    )[0]
     owned_first = line_reduce(blocks)
-    columns = scan_columns + units
-    quarters = plain_call(split_kernel, place, (quarters,), [((block_rows, columns), bf16)] * 4, (blocks,))
-    both_ways = [(2 * d + t, 2 * (d ^ 1) + 1 - t) for d in range(ranks) for t in range(2)]
-    owned_second = add(
-        quarters[0],
-        x_swapped(quarters[1]),
-        y_swapped(quarters[2]),
-        lax.ppermute(quarters[3], ("dp", "tensor"), both_ways),
-    )
-    smalls = plain_call(
-        lambda place_ref, *refs: small_kernel(*refs),
-        place,
-        sums_first + sums_second + (gain_sums,),
-        [((32, units), f32)],
-    )[0]
-    smalls_away = y_swapped(smalls)
-    grad_low, smalls = tied(grad_low, smalls)
+    quarters = plain_call(
+        split_kernel, place, (quarters,), [((block_rows, scan_columns + units), bf16)] * 4, (blocks,)
+    )
+    owned_second = add(*over_plane(*quarters))
+    smalls_away, grad_low = tied(y_swapped(smalls), grad_low)
     mine, others = plain_call(
         functools.partial(fold_kernel, heads_half), place, (smalls, smalls_away), [((16, half), f32)] * 2
     )
     total = jnp.concatenate([mine, swapped(others, "section")])
+    owned_first, boundary = tied(owned_first, placed_rows(place, grad_rows, y_swapped(grad_low)))
     total = total + x_swapped(total)
-    owned_first, boundary = tied(owned_first, placed_rows(place, grad_rows, away_rows(grad_low)))
-    total = line_total(total)
     grad_conv, grad_states_conv, grad_gate_gain, grad_heads, gain_total = plain_call(
         functools.partial(small_outputs_kernel, heads_half),
         place,
         (total,),
-        [((5, units), f32), ((5, 2 * STATE), f32), ((1, units), f32), ((3, 2 * heads_half), f32), ((1, width), f32)],
+        [((5, 1, units), f32), ((5, 1, 2 * STATE), f32), ((1, units), f32), ((3, 2 * heads_half), f32), ((1, block_rows), f32)],
     )
 
     others = jnp.where(on_first, owned_second, owned_first)
@@ -1279,18 +1289,18 @@
         owned_kernel,
         place,
         (owned_first, owned_second, swapped(others, "section"), y_swapped(own_states), far_swapped(other_states)),
-        [((block_rows, 2, units), f32)] + [((block_rows, columns), f32) for columns in (2 * STATE, 2 * heads_half, units)],
+        [((block_rows, 2, units), f32), ((block_rows, 2 * STATE), f32), ((2 * heads_half, 1, block_rows), f32), ((block_rows, units), f32)],
         (boundary, layer_outputs, grad_conv),
     )
     return (
         layer_outputs[None],
         boundary[None],
-        lax.dynamic_slice_in_dim(gain_total, rank * block_rows, block_rows, 1),
+        gain_total,
         grad_zx[None],
         grad_bc[None],
-        grad_dt[None],
-        grad_conv[None],
-        grad_states_conv[None],
+        grad_dt.transpose(1, 2, 0),
+        grad_conv.transpose(1, 0, 2),
+        grad_states_conv.transpose(1, 0, 2),
         grad_heads[1:2],
         grad_heads[2:3],
         grad_heads[0:1],

time: 358 us -> 343 us (0.958)
  local copies, waits for them, and re-layouts: 30.6 us -> 15.4 us
  waiting for transfers between devices: 42.2 us -> 55.5 us
  Pallas kernels: 185 us -> 178 us
  other arithmetic: 9.64 us -> 5.32 us
    pallas_call x0 -> x1, Pallas kernels: none -> 7.66 us  [finish(): pl.pallas_call(finish_kernel, grid_spec=pltpu.PrefetchScalarGridSpec(num_...]
    ppermute x5, waiting for transfers between devices: 2.65 us -> 8.93 us  [send(): lax.ppermute(rows, 'dp', [(2 * a + start, 2 * b + start) for a, b in move...]
    pallas_call x7 -> x6, Pallas kernels: 147 us -> 141 us  [call(): pl.pallas_call(kernel, grid=(chunks,), in_specs=[spec for _, spec in inpu...]
    unnamed x73 -> x86, local copies, waits for them, and re-layouts: 15.4 us -> 10.1 us
    pallas_call x2 -> x1, Pallas kernels: 7.64 us -> 2.99 us  [placed_rows(): pl.pallas_call(placed_kernel, grid_spec=pltpu.PrefetchScalarGridSpec(num_...]
    all_gather x2, waiting for transfers between devices: 0.02 us -> 4.21 us  [line_gather(): lax.all_gather(block, 'dp', axis_index_groups=line_groups, axis=0, tiled=...]
    pallas_call x13 -> x11, Pallas kernels: 28.7 us -> 24.7 us  [plain_call(): pl.pallas_call(body, in_specs=[pl.BlockSpec(memory_space=pltpu.SMEM)] + [...]
    ppermute x13 -> x11, waiting for transfers between devices: 18.2 us -> 21.4 us  [x_swapped(): return lax.ppermute(block, 'dp', [(i, i ^ 1) for i in range(ranks)])]
  transfers between devices with their start and end apart: 53 -> 51, of which waited for: 17 -> 20; matrix products, arithmetic and copies ran while one was open for 7% -> 3% of each run, Pallas kernels for 38% -> 37%
where the time goes in v3:
time: 343 us; the launch traced here: 337 us
  Pallas kernels  178 us (52%)
  waiting for transfers between devices  55.5 us (16%)
  starting transfers between devices  51.8 us (15%)
  blocking collectives  15.9 us (5%)
  local copies, waits for them, and re-layouts  15.4 us (4%)
  between operations  14.9 us (4%)
  other arithmetic  5.32 us (2%)
    pallas_call x6, Pallas kernels, call(): pl.pallas_call(kernel, grid=(chunks,), in_specs=[spec for _, spec in inpu...  141 us
    pallas_call x11, Pallas kernels, plain_call(): pl.pallas_call(body, in_specs=[pl.BlockSpec(memory_space=pltpu.SMEM)] + [...  24.7 us
    ppermute x27, starting transfers between devices, swapped(): return lax.ppermute(block, axis, [(0, 1), (1, 0)])  22.3 us
    ppermute x11, waiting for transfers between devices, x_swapped(): return lax.ppermute(block, 'dp', [(i, i ^ 1) for i in range(ranks)])  21.4 us
    ppermute x27, waiting for transfers between devices, swapped(): return lax.ppermute(block, axis, [(0, 1), (1, 0)])  20.2 us
    all_gather x1, blocking collectives, line_gather(): lax.all_gather(block, 'dp', axis_index_groups=line_groups, axis=0, tiled=...  15.9 us
    ppermute x11, starting transfers between devices, x_swapped(): return lax.ppermute(block, 'dp', [(i, i ^ 1) for i in range(ranks)])  14.4 us
    unnamed x86, local copies, waits for them, and re-layouts  10.1 us
  transfers between devices with their start and end apart: 51, of which 20 were waited for; matrix products, arithmetic and copies ran while one was open for 3% of the time, Pallas kernels for 37%

profile of v3, /device:TPU:0, one launch (start us, length us, event | category | flops | bytes accessed | tf_op | source)
XLA Modules:
  0.0 337.2 jit_solution(14859681086891023977)
XLA Ops:
  7.9 2.9 shard_map.291
  11.4 2.6 collective-permute-start.1
  14.7 1.9 shard_map.292
  16.6 1.6 collective-permute-start.2
  18.3 15.9 %all_gather.9.refs_2_.refs_4_ = bf16[384,640]{1,0:T(8,128)(2,1)S(1)} all-gather(bf16[96,640]{1,0:T(8,128)(2,1)} %get-tuple-element.176), channel_id=1, replica_groups={{0,4,8,12},{2,6,10,14},{1,5,9,13},{3,7,11,15},{16,20,24,28},{18,22,26,3..., dimensions={0}, use_global_device_ids=true | all-gather | bytes 614400 | tf_op jit(solution)/shard_map/all_gather | solution.py:1100
  34.8 1.5 collective-permute-start.4
  37.4 1.9 shard_map.293
  39.4 1.6 collective-permute-start.9
  41.0 2.1 shard_map.294
  43.1 5.7 %collective-permute-done.8.refs_4_ = bf16[96,768]{1,0:T(8,128)(2,1)} collective-permute-done((bf16[96,768]{1,0:T(8,128)(2,1)}, bf16[96,768]{1,0:T(8,128)(2,1)}, u32[]{:S(2)}, u32[]{:S(2)}) %collective-permute-start.8) | collective-permute-done | bytes 147488 | tf_op jit(solution)/shard_map/ppermute | solution.py:1094
  48.8 1.5 collective-permute-start.10
  51.1 1.5 collective-permute-start.7
  52.6 1.7 slice.44
  56.0 1.9 maximum_select_fusion.refs_0_.refs_1_.h_ref
  58.6 2.0 shard_map.295
  60.7 2.9 all-gather.3.cloned.1.call-done.refs_1_
  63.8 2.3 shard_map.297
  70.2 17.7 %shard_map.296 = (f32[8,768]{1,0:T(8,128)}, bf16[1024,768]{1,0:T(8,128)(2,1)}, f32[1024,768]{1,0:T(8,128)}, f32[1024,768]{1,0:T(8,128)}, f32[1024,768]{1,0:T(8,1...) custom-call(s32[4]{0:T(128)} %pad_add_fusion.place_ref.refs_0_.refs_1_, ...), custom_call_target="tpu_custom_call" | custom-call | flops 2000000000 | bytes 500000 | tf_op jit(solution)/shard_map/pallas_call | solution.py:516
  88.0 1.5 collective-permute-start.14
  89.4 1.5 collective-permute-start.13
  90.9 2.2 collective-permute-done.16.refs_6_.refs_15_
  93.1 1.5 collective-permute-start.18
  94.7 1.5 collective-permute-start.17
  96.2 4.7 %collective-permute-done.14.refs_4_.refs_15_ = bf16[192,768]{1,0:T(8,128)(2,1)S(1)} collective-permute-done((bf16[192,768]{1,0:T(8,128)(2,1)S(1)}, bf16[192,768]{1,0:T(8,128)(2,1)S(1)}, u32[]{:S(2)}, u32[]{:S(2)}) %collective-permute-start.14) | collective-permute-done | bytes 294944 | tf_op jit(solution)/shard_map/ppermute | solution.py:1094
  102.4 6.7 %shard_map.298 = (f32[1024,768]{1,0:T(8,128)}, bf16[1024,896]{1,0:T(8,128)(2,1)}) custom-call(s32[4]{0:T(128)} %pad_add_fusion.place_ref.refs_0_.refs_1_, bf16[1024,768]{1,0:T(8,128)(2,1)} %get-tuple-element.208.normed_ref.refs_8_.refs_0_, f32[1024,768]{1,0:T(8,128)} %get-tuple-element.209.y_ref.refs_10_.refs_17_, ...), custom_call_target="tpu_custom_call" | custom-call | flops 1000000000 | bytes 500000 | tf_op jit(solution)/shard_map/pallas_call | solution.py:516
  109.9 4.0 %collective-permute-done.19.refs_3_.refs_2_ = bf16[1024,896]{1,0:T(8,128)(2,1)S(1)} collective-permute-done((bf16[1024,896]{1,0:T(8,128)(2,1)}, bf16[1024,896]{1,0:T(8,128)(2,1)S(1)}, u32[]{:S(2)}, u32[]{:S(2)}) %collective-permute-start.19) | collective-permute-done | bytes 1835040 | tf_op jit(solution)/shard_map/ppermute | solution.py:1050
  116.4 1.5 collective-permute-start.20
  117.9 24.4 %shard_map.299 = (bf16[1024,768]{1,0:T(8,128)(2,1)}, f32[8,768]{1,0:T(8,128)}, bf16[1024,768]{1,0:T(8,128)(2,1)}, f32[1024,768]{1,0:T(8,128)}, f32[1024,768]{1,0...) custom-call(s32[4]{0:T(128)} %pad_add_fusion.place_ref.refs_0_.refs_, ...), custom_call_target="tpu_custom_call" | custom-call | flops 3000000000 | bytes 500000 | tf_op jit(solution)/shard_map/pallas_call | solution.py:516
  142.9 4.0 %collective-permute-done.22.refs_6_ = f32[256,768]{1,0:T(8,128)S(1)} collective-permute-done((f32[256,768]{1,0:T(8,128)S(1)}, f32[256,768]{1,0:T(8,128)S(1)}, u32[]{:S(2)}, u32[]{:S(2)}) %collective-permute-start.22) | collective-permute-done | bytes 786464 | tf_op jit(solution)/shard_map/ppermute | solution.py:1050
  149.0 44.1 %shard_map.300 = (bf16[1024,768]{1,0:T(8,128)(2,1)}, f32[1024,768]{1,0:T(8,128)}, bf16[384,5632]{1,0:T(8,128)(2,1)}, f32[8,768]{1,0:T(8,128)}, bf16[1024,768]{1,...) custom-call(s32[4]{0:T(128)} %pad_add_fusion.place_ref.refs_0_.refs_1_, ...), custom_call_target="tpu_custom_call" | custom-call | flops 4000000000 | bytes 500000 | tf_op jit(solution)/shard_map/pallas_call | solution.py:516
  196.5 1.6 collective-permute-done.23.refs_6_
  198.1 17.3 %shard_map.301 = (f32[1024,768]{1,0:T(8,128)}, bf16[1024,768]{1,0:T(8,128)(2,1)}, f32[1024,768]{1,0:T(8,128)}, bf16[384,768]{1,0:T(8,128)(2,1)}, bf16[384,768]{1...) custom-call(s32[4]{0:T(128)} %pad_add_fusion.place_ref.refs_0_.refs_1_, ...), custom_call_target="tpu_custom_call" | custom-call | flops 2000000000 | bytes 500000 | tf_op jit(solution)/shard_map/pallas_call | solution.py:516
  219.5 31.0 %shard_map.302 = (bf16[384,640]{1,0:T(8,128)(2,1)}, bf16[384,640]{1,0:T(8,128)(2,1)}, bf16[384,640]{1,0:T(8,128)(2,1)}, bf16[384,640]{1,0:T(8,128)(2,1)}, bf16[1...) custom-call(bf16[1024,768]{1,0:T(8,128)(2,1)} %get-tuple-element.208.normed_ref.refs_8_.refs_0_, ...), custom_call_target="tpu_custom_call" | custom-call | flops 3000000000 | bytes 500000 | tf_op jit(solution)/shard_map/pallas_call | solution.py:516
  250.7 1.5 collective-permute-start.34
  255.5 7.7 %shard_map.303 = (f32[2,512,768]{2,1,0:T(8,128)}, bf16[512,768]{1,0:T(8,128)(2,1)}, f32[8,768]{1,0:T(8,128)}, bf16[2,512,768]{2,1,0:T(8,128)(2,1)}) custom-call(s32[4]{0:T(128)} %pad_add_fusion.place_ref.refs_0_.refs_1_, bf16[1024,768]{1,0:T(8,128)(2,1)} %get-tuple-element.286.own_ref, bf16[1024,768]{1,0:T(8,128)(2,1)} %copy-done.8, ...), custom_call_target="tpu_custom_call" | custom-call | bytes 500000 | tf_op jit(solution)/shard_map/pallas_call | solution.py:735
  263.1 1.5 shard_map.304
  265.9 4.6 %collective-permute-start.29 = (f32[32,768]{1,0:T(8,128)}, f32[32,768]{1,0:T(8,128)S(1)}, u32[]{:S(2)}, u32[]{:S(2)}) collective-permute-start(f32[32,768]{1,0:T(8,128)} %shard_map.304), channel_id=1, source_target_pairs={{0,4},{2,6},{4,8},{6,10},{8,12},{10,14},{1,5},{3,7},{5,9},{7,11},{... | collective-permute-start | bytes 294920 | tf_op jit(solution)/shard_map/ppermute | solution.py:1110
  276.8 6.4 %collective-permute-done.32 = f32[32,768]{1,0:T(8,128)S(1)} collective-permute-done((f32[32,768]{1,0:T(8,128)S(1)}, f32[32,768]{1,0:T(8,128)S(1)}, u32[]{:S(2)}, u32[]{:S(2)}) %collective-permute-start.32) | collective-permute-done | bytes 98336 | tf_op jit(solution)/shard_map/ppermute | solution.py:1110
  283.2 3.7 %shard_map.305.refs_0_ = bf16[384,1408]{1,0:T(8,128)(2,1)} custom-call(s32[4]{0:T(128)} %pad_add_fusion.place_ref.refs_0_.refs_1_, bf16[96,5632]{1,0:T(8,128)(2,1)} %reduce-scatter.3.cloned.1.call-done.refs_0_.refs_1_, bf16[384,640]{1,0:T(8,128)(2,1)} %get-tuple-element.303.refs_1_, bf16[384,640]{1,0:T(8,128)(2,1)} %collective-permute-done.34.refs_2_, ...), custom_call_target="tpu_custom_call" | custom-call | bytes 500000 | tf_op jit(solution)/shard_map/pallas_call | solution.py:881
  288.0 3.8 %collective-permute-done.37.away_ref = f32[32,768]{1,0:T(8,128)S(1)} collective-permute-done((f32[32,768]{1,0:T(8,128)S(1)}, f32[32,768]{1,0:T(8,128)S(1)}, u32[]{:S(2)}, u32[]{:S(2)}) %collective-permute-start.37) | collective-permute-done | bytes 98336 | tf_op jit(solution)/shard_map/ppermute | solution.py:1050
  293.0 1.6 shard_map.307
  294.7 2.4 shard_map.309
  302.0 11.0 %collective-permute-done.40 = f32[32,384]{1,0:T(8,128)S(1)} collective-permute-done((f32[32,384]{1,0:T(8,128)S(1)}, f32[32,384]{1,0:T(8,128)S(1)}, u32[]{:S(2)}, u32[]{:S(2)}) %collective-permute-start.40) | collective-permute-done | bytes 49184 | tf_op jit(solution)/shard_map/ppermute | solution.py:1094
  313.6 1.9 shard_map.308
  315.5 1.8 collective-permute-done.38.away_ref
  318.2 3.0 shard_map.306.refs_0_
  325.5 1.5 collective-permute-done.45.refs_6_
  327.8 2.3 shard_map.310
  (185 shorter events, 50.9 us)
Async XLA Ops:
  7.2 56.4 %all-gather.3.cloned.1.call-start = ((), (), s32[]{:S(2)}) async-start(), calls=%async_computation.2 | async-start | bytes 1351680 | tf_op jit(solution)/shard_map/all_gather | solution.py:1100
  11.4 22.8 %collective-permute-start.1 = (bf16[256,768]{1,0:T(8,128)(2,1)S(1)}, bf16[256,768]{1,0:T(8,128)(2,1)}, u32[]{:S(2)}, u32[]{:S(2)}) collective-permute-start(bf16[256,768]{1,0:T(8,128)(2,1)S(1)} %dynamic-slice_bitcast_fusion.2), channel_id=1, source_target_pairs={{0,1},{1,0},{2,3},{3,2},{4,5},{5,4},{6,7},{7,6},{8,9},{9,8},{10,11... | collective-permute-start | bytes 1179656 | tf_op jit(solution)/shard_map/ppermute | solution.py:1050
  16.6 17.5 %collective-permute-start.2 = (bf16[32,384]{1,0:T(8,128)(2,1)}, bf16[32,384]{1,0:T(8,128)(2,1)S(1)}, u32[]{:S(2)}, u32[]{:S(2)}) collective-permute-start(bf16[32,384]{1,0:T(8,128)(2,1)} %get-tuple-element.177), channel_id=1, source_target_pairs={{0,1},{1,0},{2,3},{3,2},{4,5},{5,4},{6,7},{7,6},{8,9},{9,8},{10,11... | collective-permute-start | bytes 73736 | tf_op jit(solution)/shard_map/ppermute | solution.py:1050
  34.2 81.0 %all-gather.5.cloned.1.call-start = ((), (), s32[]{:S(2)}) async-start(), calls=%async_computation.3 | async-start | bytes 2949120 | tf_op jit(solution)/shard_map/all_gather | solution.py:1100
  34.2 16.1 %collective-permute-start.5 = (bf16[384,640]{1,0:T(8,128)(2,1)S(1)}, bf16[384,640]{1,0:T(8,128)(2,1)S(1)}, u32[]{:S(2)}, u32[]{:S(2)}) collective-permute-start(bf16[384,640]{1,0:T(8,128)(2,1)S(1)} %all_gather.9.refs_2_.refs_4_), channel_id=1, source_target_pairs={{0,1},{1,0},{2,3},{3,2},{4,5},{5,4},{6,7},{7,6},{8,9},{9,8},{10,11... | collective-permute-start | bytes 1474568 | tf_op jit(solution)/shard_map/ppermute | solution.py:1050
  34.8 17.9 %collective-permute-start.4 = (bf16[384,640]{1,0:T(8,128)(2,1)S(1)}, bf16[384,640]{1,0:T(8,128)(2,1)}, u32[]{:S(2)}, u32[]{:S(2)}) collective-permute-start(bf16[384,640]{1,0:T(8,128)(2,1)S(1)} %all_gather.9.refs_2_.refs_4_), channel_id=1, source_target_pairs={{0,2},{2,0},{4,6},{6,4},{8,10},{10,8},{12,14},{14,12},{1,3},{3,1},... | collective-permute-start | bytes 1474568 | tf_op jit(solution)/shard_map/ppermute | solution.py:1094
  36.3 18.5 %collective-permute-start.3 = (bf16[256,768]{1,0:T(8,128)(2,1)}, bf16[256,768]{1,0:T(8,128)(2,1)}, u32[]{:S(2)}, u32[]{:S(2)}) collective-permute-start(bf16[256,768]{1,0:T(8,128)(2,1)} %collective-permute-done.1), channel_id=1, source_target_pairs={{0,16},{16,0},{1,17},{17,1},{2,18},{18,2},{3,19},{19,3},{4,20},{20... | collective-permute-start | bytes 1179656 | tf_op jit(solution)/shard_map/ppermute | solution.py:1050
  36.3 12.5 %collective-permute-start.8 = (bf16[96,768]{1,0:T(8,128)(2,1)}, bf16[96,768]{1,0:T(8,128)(2,1)}, u32[]{:S(2)}, u32[]{:S(2)}) collective-permute-start(bf16[96,768]{1,0:T(8,128)(2,1)} %get-tuple-element.186.refs_3_), channel_id=1, source_target_pairs={{0,2},{2,0},{4,6},{6,4},{8,10},{10,8},{12,14},{14,12},{1,3},{3,1},... | collective-permute-start | bytes 442376 | tf_op jit(solution)/shard_map/ppermute | solution.py:1094
  39.4 18.5 %collective-permute-start.9 = (bf16[96,768]{1,0:T(8,128)(2,1)S(1)}, bf16[96,768]{1,0:T(8,128)(2,1)S(1)}, u32[]{:S(2)}, u32[]{:S(2)}) collective-permute-start(bf16[96,768]{1,0:T(8,128)(2,1)S(1)} %copy-done.32), channel_id=1, source_target_pairs={{0,1},{1,0},{2,3},{3,2},{4,5},{5,4},{6,7},{7,6},{8,9},{9,8},{10,11... | collective-permute-start | bytes 442376 | tf_op jit(solution)/shard_map/ppermute | solution.py:1050
  48.8 9.1 %collective-permute-start.10 = (bf16[96,768]{1,0:T(8,128)(2,1)}, bf16[96,768]{1,0:T(8,128)(2,1)S(1)}, u32[]{:S(2)}, u32[]{:S(2)}) collective-permute-start(bf16[96,768]{1,0:T(8,128)(2,1)} %collective-permute-done.8.refs_4_), channel_id=1, source_target_pairs={{0,1},{1,0},{2,3},{3,2},{4,5},{5,4},{6,7},{7,6},{8,9},{9,8},{10,11... | collective-permute-start | bytes 442376 | tf_op jit(solution)/shard_map/ppermute | solution.py:1050
  51.1 9.5 %collective-permute-start.7 = (bf16[192,640]{1,0:T(8,128)(2,1)}, bf16[192,640]{1,0:T(8,128)(2,1)S(1)}, u32[]{:S(2)}, u32[]{:S(2)}) collective-permute-start(bf16[192,640]{1,0:T(8,128)(2,1)} %slice.45), channel_id=1, source_target_pairs={{0,2},{2,0},{4,6},{6,4},{8,10},{10,8},{12,14},{14,12},{1,3},{3,1},... | collective-permute-start | bytes 737288 | tf_op jit(solution)/shard_map/ppermute | solution.py:1094
  54.3 6.4 %collective-permute-start.6 = (bf16[192,640]{1,0:T(8,128)(2,1)}, bf16[192,640]{1,0:T(8,128)(2,1)S(1)}, u32[]{:S(2)}, u32[]{:S(2)}) collective-permute-start(bf16[192,640]{1,0:T(8,128)(2,1)} %slice.44), channel_id=1, source_target_pairs={{0,1},{1,0},{2,3},{3,2},{4,5},{5,4},{6,7},{7,6},{8,9},{9,8},{10,11... | collective-permute-start | bytes 737288 | tf_op jit(solution)/shard_map/ppermute | solution.py:1050
  63.6 219.6 %reduce-scatter.3.cloned.1.call-start = ((), (), s32[]{:S(2)}) async-start(), calls=%async_computation.4 | async-start | bytes 5406720 | tf_op jit(solution)/shard_map/reduce_scatter | solution.py:1103
  66.1 21.7 %collective-permute-start.12 = (bf16[384,768]{1,0:T(8,128)(2,1)}, bf16[384,768]{1,0:T(8,128)(2,1)S(1)}, u32[]{:S(2)}, u32[]{:S(2)}) collective-permute-start(bf16[384,768]{1,0:T(8,128)(2,1)} %get-tuple-element.210.refs_0_.refs_11_), channel_id=1, source_target_pairs={{0,1},{1,0},{2,3},{3,2},{4,5},{5,4},{6,7},{7,6},{8,9},{9,8},{10,11... | collective-permute-start | bytes 1769480 | tf_op jit(solution)/shard_map/ppermute | solution.py:1050
  67.6 20.3 %collective-permute-start.11 = (bf16[384,768]{1,0:T(8,128)(2,1)}, bf16[384,768]{1,0:T(8,128)(2,1)S(1)}, u32[]{:S(2)}, u32[]{:S(2)}) collective-permute-start(bf16[384,768]{1,0:T(8,128)(2,1)} %get-tuple-element.210.refs_0_.refs_11_), channel_id=1, source_target_pairs={{0,2},{2,0},{4,6},{6,4},{8,10},{10,8},{12,14},{14,12},{1,3},{3,1},... | collective-permute-start | bytes 1769480 | tf_op jit(solution)/shard_map/ppermute | solution.py:1094
  69.1 24.0 %collective-permute-start.16 = (bf16[384,640]{1,0:T(8,128)(2,1)}, bf16[384,640]{1,0:T(8,128)(2,1)S(1)}, u32[]{:S(2)}, u32[]{:S(2)}) collective-permute-start(bf16[384,640]{1,0:T(8,128)(2,1)} %get-tuple-element.220.refs_4_.refs_13_), channel_id=1, source_target_pairs={{0,1},{1,0},{2,3},{3,2},{4,5},{5,4},{6,7},{7,6},{8,9},{9,8},{10,11... | collective-permute-start | bytes 1474568 | tf_op jit(solution)/shard_map/ppermute | solution.py:1050
  69.6 25.1 %collective-permute-start.15 = (bf16[384,640]{1,0:T(8,128)(2,1)}, bf16[384,640]{1,0:T(8,128)(2,1)S(1)}, u32[]{:S(2)}, u32[]{:S(2)}) collective-permute-start(bf16[384,640]{1,0:T(8,128)(2,1)} %get-tuple-element.220.refs_4_.refs_13_), channel_id=1, source_target_pairs={{0,2},{2,0},{4,6},{6,4},{8,10},{10,8},{12,14},{14,12},{1,3},{3,1},... | collective-permute-start | bytes 1474568 | tf_op jit(solution)/shard_map/ppermute | solution.py:1094
  88.0 13.0 %collective-permute-start.14 = (bf16[192,768]{1,0:T(8,128)(2,1)S(1)}, bf16[192,768]{1,0:T(8,128)(2,1)S(1)}, u32[]{:S(2)}, u32[]{:S(2)}) collective-permute-start(bf16[192,768]{1,0:T(8,128)(2,1)S(1)} %slice.36), channel_id=1, source_target_pairs={{0,2},{2,0},{4,6},{6,4},{8,10},{10,8},{12,14},{14,12},{1,3},{3,1},... | collective-permute-start | bytes 884744 | tf_op jit(solution)/shard_map/ppermute | solution.py:1094
  89.4 11.5 %collective-permute-start.13 = (bf16[192,768]{1,0:T(8,128)(2,1)S(1)}, bf16[192,768]{1,0:T(8,128)(2,1)S(1)}, u32[]{:S(2)}, u32[]{:S(2)}) collective-permute-start(bf16[192,768]{1,0:T(8,128)(2,1)S(1)} %slice.35), channel_id=1, source_target_pairs={{0,1},{1,0},{2,3},{3,2},{4,5},{5,4},{6,7},{7,6},{8,9},{9,8},{10,11... | collective-permute-start | bytes 884744 | tf_op jit(solution)/shard_map/ppermute | solution.py:1050
  93.1 15.9 %collective-permute-start.18 = (bf16[192,640]{1,0:T(8,128)(2,1)S(1)}, bf16[192,640]{1,0:T(8,128)(2,1)S(1)}, u32[]{:S(2)}, u32[]{:S(2)}) collective-permute-start(bf16[192,640]{1,0:T(8,128)(2,1)S(1)} %slice.47), channel_id=1, source_target_pairs={{0,2},{2,0},{4,6},{6,4},{8,10},{10,8},{12,14},{14,12},{1,3},{3,1},... | collective-permute-start | bytes 737288 | tf_op jit(solution)/shard_map/ppermute | solution.py:1094
  94.7 14.4 %collective-permute-start.17 = (bf16[192,640]{1,0:T(8,128)(2,1)S(1)}, bf16[192,640]{1,0:T(8,128)(2,1)S(1)}, u32[]{:S(2)}, u32[]{:S(2)}) collective-permute-start(bf16[192,640]{1,0:T(8,128)(2,1)S(1)} %slice.46), channel_id=1, source_target_pairs={{0,1},{1,0},{2,3},{3,2},{4,5},{5,4},{6,7},{7,6},{8,9},{9,8},{10,11... | collective-permute-start | bytes 737288 | tf_op jit(solution)/shard_map/ppermute | solution.py:1050
  109.9 4.0 %collective-permute-start.19 = (bf16[1024,896]{1,0:T(8,128)(2,1)}, bf16[1024,896]{1,0:T(8,128)(2,1)S(1)}, u32[]{:S(2)}, u32[]{:S(2)}) collective-permute-start(bf16[1024,896]{1,0:T(8,128)(2,1)} %get-tuple-element.218.refs_2_.refs_1_), channel_id=1, source_target_pairs={{0,16},{16,0},{1,17},{17,1},{2,18},{18,2},{3,19},{19,3},{4,20},{20... | collective-permute-start | bytes 5505032 | tf_op jit(solution)/shard_map/ppermute | solution.py:1050
  116.4 25.9 %collective-permute-start.20 = (f32[256,768]{1,0:T(8,128)S(1)}, f32[256,768]{1,0:T(8,128)S(1)}, u32[]{:S(2)}, u32[]{:S(2)}) collective-permute-start(f32[256,768]{1,0:T(8,128)S(1)} %dynamic-slice_bitcast_fusion), channel_id=1, source_target_pairs={{0,1},{1,0},{2,3},{3,2},{4,5},{5,4},{6,7},{7,6},{8,9},{9,8},{10,11... | collective-permute-start | bytes 2359304 | tf_op jit(solution)/shard_map/ppermute | solution.py:1050
  142.3 5.2 %collective-permute-start.21 = (bf16[1024,896]{1,0:T(8,128)(2,1)}, bf16[1024,896]{1,0:T(8,128)(2,1)S(1)}, u32[]{:S(2)}, u32[]{:S(2)}) collective-permute-start(bf16[1024,896]{1,0:T(8,128)(2,1)} %get-tuple-element.243.refs_2_), channel_id=1, source_target_pairs={{0,16},{16,0},{1,17},{17,1},{2,18},{18,2},{3,19},{19,3},{4,20},{20... | collective-permute-start | bytes 5505032 | tf_op jit(solution)/shard_map/ppermute | solution.py:1050
  142.4 4.5 %collective-permute-start.22 = (f32[256,768]{1,0:T(8,128)S(1)}, f32[256,768]{1,0:T(8,128)S(1)}, u32[]{:S(2)}, u32[]{:S(2)}) collective-permute-start(f32[256,768]{1,0:T(8,128)S(1)} %collective-permute-done.20.refs_5_), channel_id=1, source_target_pairs={{0,16},{16,0},{1,17},{17,1},{2,18},{18,2},{3,19},{19,3},{4,20},{20... | collective-permute-start | bytes 2359304 | tf_op jit(solution)/shard_map/ppermute | solution.py:1050
  193.2 128.0 %reduce-scatter.5.cloned.1.call-start = ((), (), s32[]{:S(2)}) async-start(), calls=%async_computation.5 | async-start | bytes 1351680 | tf_op jit(solution)/shard_map/reduce_scatter | solution.py:1103
  196.0 20.0 %collective-permute-start.24 = (bf16[512,768]{1,0:T(8,128)(2,1)}, bf16[512,768]{1,0:T(8,128)(2,1)S(1)}, u32[]{:S(2)}, u32[]{:S(2)}) collective-permute-start(bf16[512,768]{1,0:T(8,128)(2,1)} %constant_dynamic-slice_fusion), channel_id=1, source_target_pairs={{0,1},{1,0},{2,3},{3,2},{4,5},{5,4},{6,7},{7,6},{8,9},{9,8},{10,11... | collective-permute-start | bytes 2359304 | tf_op jit(solution)/shard_map/ppermute | solution.py:1050
  216.0 34.5 %collective-permute-start.25 = (bf16[384,768]{1,0:T(8,128)(2,1)}, bf16[384,768]{1,0:T(8,128)(2,1)S(1)}, u32[]{:S(2)}, u32[]{:S(2)}) collective-permute-start(bf16[384,768]{1,0:T(8,128)(2,1)} %get-tuple-element.283), channel_id=1, source_target_pairs={{0,2},{2,0},{4,6},{6,4},{8,10},{10,8},{12,14},{14,12},{1,3},{3,1},... | collective-permute-start | bytes 1769480 | tf_op jit(solution)/shard_map/ppermute | solution.py:1094
  217.5 33.1 %collective-permute-start.26 = (bf16[384,768]{1,0:T(8,128)(2,1)}, bf16[384,768]{1,0:T(8,128)(2,1)S(1)}, u32[]{:S(2)}, u32[]{:S(2)}) collective-permute-start(bf16[384,768]{1,0:T(8,128)(2,1)} %get-tuple-element.284), channel_id=1, source_target_pairs={{0,1},{1,0},{2,3},{3,2},{4,5},{5,4},{6,7},{7,6},{8,9},{9,8},{10,11... | collective-permute-start | bytes 1769480 | tf_op jit(solution)/shard_map/ppermute | solution.py:1050
  218.0 32.5 %collective-permute-start.27 = (bf16[384,768]{1,0:T(8,128)(2,1)}, bf16[384,768]{1,0:T(8,128)(2,1)S(1)}, u32[]{:S(2)}, u32[]{:S(2)}) collective-permute-start(bf16[384,768]{1,0:T(8,128)(2,1)} %get-tuple-element.285), channel_id=1, source_target_pairs={{0,3},{1,2},{2,1},{3,0},{4,7},{5,6},{6,5},{7,4},{8,11},{9,10},{10,... | collective-permute-start | bytes 1769480 | tf_op jit(solution)/shard_map/ppermute | solution.py:1142
  250.6 3.7 %collective-permute-start.28 = (bf16[1024,768]{1,0:T(8,128)(2,1)}, bf16[1024,768]{1,0:T(8,128)(2,1)S(1)}, u32[]{:S(2)}, u32[]{:S(2)}) collective-permute-start(bf16[1024,768]{1,0:T(8,128)(2,1)} %get-tuple-element.286.own_ref), channel_id=1, source_target_pairs={{0,16},{16,0},{1,17},{17,1},{2,18},{18,2},{3,19},{19,3},{4,20},{20... | collective-permute-start | bytes 4718600 | tf_op jit(solution)/shard_map/ppermute | solution.py:1050
  250.7 25.1 %collective-permute-start.34 = (bf16[384,640]{1,0:T(8,128)(2,1)}, bf16[384,640]{1,0:T(8,128)(2,1)}, u32[]{:S(2)}, u32[]{:S(2)}) collective-permute-start(bf16[384,640]{1,0:T(8,128)(2,1)} %get-tuple-element.300), channel_id=1, source_target_pairs={{0,2},{2,0},{4,6},{6,4},{8,10},{10,8},{12,14},{14,12},{1,3},{3,1},... | collective-permute-start | bytes 1474568 | tf_op jit(solution)/shard_map/ppermute | solution.py:1094
  252.2 24.5 %collective-permute-start.35 = (bf16[384,640]{1,0:T(8,128)(2,1)}, bf16[384,640]{1,0:T(8,128)(2,1)}, u32[]{:S(2)}, u32[]{:S(2)}) collective-permute-start(bf16[384,640]{1,0:T(8,128)(2,1)} %get-tuple-element.301), channel_id=1, source_target_pairs={{0,1},{1,0},{2,3},{3,2},{4,5},{5,4},{6,7},{7,6},{8,9},{9,8},{10,11... | collective-permute-start | bytes 1474568 | tf_op jit(solution)/shard_map/ppermute | solution.py:1050
  252.8 24.0 %collective-permute-start.36 = (bf16[384,640]{1,0:T(8,128)(2,1)}, bf16[384,640]{1,0:T(8,128)(2,1)}, u32[]{:S(2)}, u32[]{:S(2)}) collective-permute-start(bf16[384,640]{1,0:T(8,128)(2,1)} %get-tuple-element.302), channel_id=1, source_target_pairs={{0,3},{1,2},{2,1},{3,0},{4,7},{5,6},{6,5},{7,4},{8,11},{9,10},{10,... | collective-permute-start | bytes 1474568 | tf_op jit(solution)/shard_map/ppermute | solution.py:1142
  264.6 6.9 %collective-permute-start.31 = (f32[32,768]{1,0:T(8,128)}, f32[32,768]{1,0:T(8,128)S(1)}, u32[]{:S(2)}, u32[]{:S(2)}) collective-permute-start(f32[32,768]{1,0:T(8,128)} %shard_map.304), channel_id=1, source_target_pairs={{4,0},{6,2},{8,4},{10,6},{12,8},{14,10},{5,1},{7,3},{9,5},{11,7},{... | collective-permute-start | bytes 294920 | tf_op jit(solution)/shard_map/ppermute | solution.py:1110
  265.9 7.1 %collective-permute-start.29 = (f32[32,768]{1,0:T(8,128)}, f32[32,768]{1,0:T(8,128)S(1)}, u32[]{:S(2)}, u32[]{:S(2)}) collective-permute-start(f32[32,768]{1,0:T(8,128)} %shard_map.304), channel_id=1, source_target_pairs={{0,4},{2,6},{4,8},{6,10},{8,12},{10,14},{1,5},{3,7},{5,9},{7,11},{... | collective-permute-start | bytes 294920 | tf_op jit(solution)/shard_map/ppermute | solution.py:1110
  273.0 10.2 %collective-permute-start.33 = (f32[32,768]{1,0:T(8,128)S(1)}, f32[32,768]{1,0:T(8,128)S(1)}, u32[]{:S(2)}, u32[]{:S(2)}) collective-permute-start(f32[32,768]{1,0:T(8,128)S(1)} %broadcast_select_fusion.3), channel_id=1, source_target_pairs={{4,12},{6,14},{8,0},{10,2},{5,13},{7,15},{9,1},{11,3},{20,28},{22,... | collective-permute-start | bytes 294920 | tf_op jit(solution)/shard_map/ppermute | solution.py:1110
  274.5 8.7 %collective-permute-start.32 = (f32[32,768]{1,0:T(8,128)S(1)}, f32[32,768]{1,0:T(8,128)S(1)}, u32[]{:S(2)}, u32[]{:S(2)}) collective-permute-start(f32[32,768]{1,0:T(8,128)S(1)} %collective-permute-done.31), channel_id=1, source_target_pairs={{8,4},{10,6},{4,0},{6,2},{9,5},{11,7},{5,1},{7,3},{24,20},{26,22},... | collective-permute-start | bytes 294920 | tf_op jit(solution)/shard_map/ppermute | solution.py:1110
  275.8 7.4 %collective-permute-start.30 = (f32[32,768]{1,0:T(8,128)S(1)}, f32[32,768]{1,0:T(8,128)S(1)}, u32[]{:S(2)}, u32[]{:S(2)}) collective-permute-start(f32[32,768]{1,0:T(8,128)S(1)} %collective-permute-done.29), channel_id=1, source_target_pairs={{4,8},{6,10},{8,12},{10,14},{5,9},{7,11},{9,13},{11,15},{20,24},{2... | collective-permute-start | bytes 294920 | tf_op jit(solution)/shard_map/ppermute | solution.py:1110
  287.1 4.8 %collective-permute-start.37 = (f32[32,768]{1,0:T(8,128)S(1)}, f32[32,768]{1,0:T(8,128)S(1)}, u32[]{:S(2)}, u32[]{:S(2)}) collective-permute-start(f32[32,768]{1,0:T(8,128)S(1)} %add_add_fusion.own_ref), channel_id=1, source_target_pairs={{0,1},{1,0},{2,3},{3,2},{4,5},{5,4},{6,7},{7,6},{8,9},{9,8},{10,11... | collective-permute-start | bytes 294920 | tf_op jit(solution)/shard_map/ppermute | solution.py:1050
  291.8 25.4 %collective-permute-start.38 = (bf16[512,768]{1,0:T(8,128)(2,1)}, bf16[512,768]{1,0:T(8,128)(2,1)S(1)}, u32[]{:S(2)}, u32[]{:S(2)}) collective-permute-start(bf16[512,768]{1,0:T(8,128)(2,1)} %get-tuple-element.315), channel_id=1, source_target_pairs={{0,1},{1,0},{2,3},{3,2},{4,5},{5,4},{6,7},{7,6},{8,9},{9,8},{10,11... | collective-permute-start | bytes 2359304 | tf_op jit(solution)/shard_map/ppermute | solution.py:1050
  294.7 5.9 %collective-permute-start.39 = (f32[16,384]{1,0:T(8,128)}, f32[16,384]{1,0:T(8,128)S(1)}, u32[]{:S(2)}, u32[]{:S(2)}) collective-permute-start(f32[16,384]{1,0:T(8,128)} %get-tuple-element.320), channel_id=1, source_target_pairs={{0,16},{16,0},{1,17},{17,1},{2,18},{18,2},{3,19},{19,3},{4,20},{20... | collective-permute-start | bytes 73736 | tf_op jit(solution)/shard_map/ppermute | solution.py:1050
  297.0 24.1 %collective-permute-start.41 = (bf16[96,1408]{1,0:T(8,128)(2,1)}, bf16[96,1408]{1,0:T(8,128)(2,1)S(1)}, u32[]{:S(2)}, u32[]{:S(2)}) collective-permute-start(bf16[96,1408]{1,0:T(8,128)(2,1)} %get-tuple-element.325), channel_id=1, source_target_pairs={{0,2},{2,0},{4,6},{6,4},{8,10},{10,8},{12,14},{14,12},{1,3},{3,1},... | collective-permute-start | bytes 811016 | tf_op jit(solution)/shard_map/ppermute | solution.py:1094
  298.4 22.7 %collective-permute-start.42 = (bf16[96,1408]{1,0:T(8,128)(2,1)}, bf16[96,1408]{1,0:T(8,128)(2,1)S(1)}, u32[]{:S(2)}, u32[]{:S(2)}) collective-permute-start(bf16[96,1408]{1,0:T(8,128)(2,1)} %get-tuple-element.326), channel_id=1, source_target_pairs={{0,1},{1,0},{2,3},{3,2},{4,5},{5,4},{6,7},{7,6},{8,9},{9,8},{10,11... | collective-permute-start | bytes 811016 | tf_op jit(solution)/shard_map/ppermute | solution.py:1050
  299.2 22.0 %collective-permute-start.43 = (bf16[96,1408]{1,0:T(8,128)(2,1)}, bf16[96,1408]{1,0:T(8,128)(2,1)S(1)}, u32[]{:S(2)}, u32[]{:S(2)}) collective-permute-start(bf16[96,1408]{1,0:T(8,128)(2,1)} %get-tuple-element.327), channel_id=1, source_target_pairs={{0,3},{1,2},{2,1},{3,0},{4,7},{5,6},{6,5},{7,4},{8,11},{9,10},{10,... | collective-permute-start | bytes 811016 | tf_op jit(solution)/shard_map/ppermute | solution.py:1142
  300.6 12.4 %collective-permute-start.40 = (f32[32,384]{1,0:T(8,128)S(1)}, f32[32,384]{1,0:T(8,128)S(1)}, u32[]{:S(2)}, u32[]{:S(2)}) collective-permute-start(f32[32,384]{1,0:T(8,128)S(1)} %constant_dynamic-update-slice_fusion), channel_id=1, source_target_pairs={{0,2},{2,0},{4,6},{6,4},{8,10},{10,8},{12,14},{14,12},{1,3},{3,1},... | collective-permute-start | bytes 147464 | tf_op jit(solution)/shard_map/ppermute | solution.py:1094
  321.4 5.7 %collective-permute-start.44 = (bf16[96,1408]{1,0:T(8,128)(2,1)S(1)}, bf16[96,1408]{1,0:T(8,128)(2,1)S(1)}, u32[]{:S(2)}, u32[]{:S(2)}) collective-permute-start(bf16[96,1408]{1,0:T(8,128)(2,1)S(1)} %get-tuple-element.335), channel_id=1, source_target_pairs={{0,16},{16,0},{1,17},{17,1},{2,18},{18,2},{3,19},{19,3},{4,20},{20... | collective-permute-start | bytes 811016 | tf_op jit(solution)/shard_map/ppermute | solution.py:1050
  323.2 3.8 %collective-permute-start.45 = (bf16[96,128]{1,0:T(8,128)(2,1)S(1)}, bf16[96,128]{1,0:T(8,128)(2,1)S(1)}, u32[]{:S(2)}, u32[]{:S(2)}) collective-permute-start(bf16[96,128]{1,0:T(8,128)(2,1)S(1)} %get-tuple-element.340), channel_id=1, source_target_pairs={{0,1},{1,0},{2,3},{3,2},{4,5},{5,4},{6,7},{7,6},{8,9},{9,8},{10,11... | collective-permute-start | bytes 73736 | tf_op jit(solution)/shard_map/ppermute | solution.py:1050
  (45 other events, 371.0 us)
Sparse Core Ops, SparseCore 0:
  34.3 29.2 all-gather.2
  65.2 49.9 all-gather.4
  193.3 76.8 reduce-scatter.2
  287.1 30.0 reduce-scatter.4

commit v4 on v3

--- a/solution.py
+++ b/solution.py
@@ -60,11 +60,18 @@
 
 
 def moved_down(block, edge, lag):
-    return jnp.concatenate([edge, block], axis=0)[8 - lag : 8 - lag + block.shape[0]]
+    rolled = pltpu.roll(block, lag, 0)
+    row = lax.broadcasted_iota(jnp.int32, (8, 1), 0)
+    first = jnp.where(row < lag, pltpu.roll(edge, lag, 0), rolled[:8])
+    return jnp.concatenate([first, rolled[8:]], axis=0)
 
 
 def moved_up(block, edge, lag):
-    return jnp.concatenate([block, edge], axis=0)[lag : lag + block.shape[0]]
+    length = block.shape[0]
+    rolled = pltpu.roll(block, length - lag, 0)
+    row = lax.broadcasted_iota(jnp.int32, (8, 1), 0)
+    last = jnp.where(row >= 8 - lag, pltpu.roll(edge, 8 - lag, 0), rolled[length - 8 :])
+    return jnp.concatenate([rolled[: length - 8], last], axis=0)
 
 
 def decay_parts(steps_in, head_rows, marks, heads):
@@ -212,16 +219,20 @@
     mask = linked_mask(row, column, marks, segment_ref[...])
     scores = nt(c_rows, b_rows)
     logs_across = jnp.transpose(logs)
+    cut = SPAN // 2
     pieces = []
     for pair in range(heads // 2):
-        mixes = []
-        for head in (2 * pair, 2 * pair + 1):
-            factor = jnp.exp(logs[:, head : head + 1] - logs_across[head : head + 1, :] + mask)
-            mixes.append((factor * scores).astype(bf16))
         block = scaled[:, pair * LANES : (pair + 1) * LANES]
         left = jnp.where(lane < HEAD_DIM, block, 0.0).astype(bf16)
         right = jnp.where(lane < HEAD_DIM, 0.0, block).astype(bf16)
-        pieces.append(nn(jnp.concatenate(mixes, axis=1), jnp.concatenate([left, right], axis=0)))
+        halves = []
+        for rows_of, seen in ((slice(0, cut), cut), (slice(cut, SPAN), SPAN)):
+            mixes = []
+            for head in (2 * pair, 2 * pair + 1):
+                gap = logs[rows_of, head : head + 1] - logs_across[head : head + 1, :seen]
+                mixes.append((jnp.exp(gap + mask[rows_of, :seen]) * scores[rows_of, :seen]).astype(bf16))
+            halves.append(nn(jnp.concatenate(mixes, axis=1), jnp.concatenate([left[:seen], right[:seen]], axis=0)))
+        pieces.append(jnp.concatenate(halves, axis=0))
     inside = jnp.concatenate(pieces, axis=1)
     held = state[...]
     entry_state_ref[0] = held
@@ -358,19 +369,27 @@
     lane = lax.broadcasted_iota(jnp.int32, (1, LANES), 1)
     is_left = lane < HEAD_DIM
     zero = jnp.zeros((), bf16)
-    grad_scores = jnp.zeros((SPAN, SPAN), f32)
+    cut = SPAN // 2
+    spans = ((slice(0, cut), slice(0, SPAN)), (slice(cut, SPAN), slice(cut, SPAN)))
+    grad_scores = [jnp.zeros((cut, SPAN), f32), jnp.zeros((cut, cut), f32)]
     pieces = []
     for pair in range(heads // 2):
         columns = slice(pair * LANES, (pair + 1) * LANES)
         block, grad = scaled_low[:, columns], grad_y_low[:, columns]
         grad_left = jnp.where(is_left, grad, zero)
         grad_right = jnp.where(is_left, zero, grad)
-        mixes = []
-        for head, grad_one in ((2 * pair, grad_left), (2 * pair + 1, grad_right)):
-            factor = jnp.exp(logs_across[head : head + 1, :] - logs[:, head : head + 1] + mask)
-            mixes.append((factor * scores).astype(bf16))
-            grad_scores = grad_scores + nt(block, grad_one) * factor
-        pieces.append(nn(jnp.concatenate(mixes, axis=1), jnp.concatenate([grad_left, grad_right], axis=0)))
+        halves = []
+        for index, (rows_of, seen) in enumerate(spans):
+            mixes = []
+            for head, grad_one in ((2 * pair, grad_left), (2 * pair + 1, grad_right)):
+                gap = logs_across[head : head + 1, seen] - logs[rows_of, head : head + 1]
+                factor = jnp.exp(gap + mask[rows_of, seen])
+                mixes.append((factor * scores[rows_of, seen]).astype(bf16))
+                grad_scores[index] = grad_scores[index] + nt(block[rows_of], grad_one[seen]) * factor
+            halves.append(nn(jnp.concatenate(mixes, axis=1), jnp.concatenate([grad_left[seen], grad_right[seen]], axis=0)))
+        pieces.append(jnp.concatenate(halves, axis=0))
+    lower_scores = jnp.concatenate([jnp.zeros((cut, cut), f32), grad_scores[1]], axis=1)
+    grad_scores = jnp.concatenate([grad_scores[0], lower_scores], axis=0)
     held = entry_state_ref[0]
     held_low = held.astype(bf16)
     gradient = dstate[...]
@@ -390,7 +409,7 @@
     last_row = lax.broadcasted_iota(jnp.int32, (SPAN, 1), 0) == SPAN - 1
     grad_logs = grad_logs + jnp.where(last_row, state_heads, 0.0)
     grad_log_steps = running_sum((row <= column).astype(bf16), grad_logs)
-    grad_steps = gathered_heads(grad_scaled * values, spreader) - head_ref[1:2, :LANES] * grad_log_steps
+    grad_steps = nt((grad_scaled * values).astype(bf16), spreader[:LANES]) - head_ref[1:2, :LANES] * grad_log_steps
     grad_steps_in = jnp.where(lane < heads, grad_steps * jax.nn.sigmoid(shifted), 0.0)
     states_sums[5:6, :] += jnp.concatenate(
         [
@@ -441,19 +460,18 @@
     normed_ref, refs = refs[0], refs[1:]
     inputs, refs = refs[: 16 + pieces], refs[16 + pieces :]
     outs, refs = refs[:grad_arrays], refs[grad_arrays:]
-    results, scratch, grads, acc = refs[:3], refs[3:-2], refs[-2], refs[-1]
+    results, scratch, grads, kept, acc = refs[:3], refs[3:-3], refs[-3], refs[-2], refs[-1]
     place_ref = inputs[0]
     units = acc.shape[1] - 4 * STATE
 
-    @pl.when(pl.program_id(0) == 0)
+    step = pl.program_id(0)
+    here = pl.ds(pl.multiple_of(step * SPAN, SPAN), SPAN)
+    scan_backward_kernel(heads, rows, pieces, *inputs, grads.at[here], *results, *scratch)
+    kept[here] = normed_ref[...]
+
+    @pl.when(step == pl.num_programs(0) - 1)
     def _():
-        acc[...] = jnp.zeros_like(acc)
-
-    scan_backward_kernel(heads, rows, pieces, *inputs, grads, *results, *scratch)
-    acc[...] += tn(normed_ref[...], grads[...])
-
-    @pl.when(pl.program_id(0) == pl.num_programs(0) - 1)
-    def _():
+        acc[...] = tn(kept[...], grads[...])
         store_grads(outs, (0, units // 2), acc, 0, rows, place_ref)
         store_grads(outs, (units // 2, units // 2 + 2 * STATE), acc, units, rows, place_ref)
 
@@ -603,7 +621,7 @@
     return results
 
 
-def scan_scratch(width, units):
+def scan_scratch(length, width, units):
     return [
         ((width, units + 4 * STATE), bf16),
         ((STATE, units), f32),
@@ -612,7 +630,8 @@
         ((8, 2 * STATE), f32),
         ((8, units), f32),
         ((8, 2 * STATE), f32),
-        ((SPAN, units + 4 * STATE), bf16),
+        ((length, units + 4 * STATE), bf16),
+        ((length, width), bf16),
         ((width, units + 4 * STATE), f32),
     ]
 
@@ -633,7 +652,7 @@
     for columns in (units, 2 * STATE):
         outputs.append(((8, columns), f32, pl.BlockSpec((8, columns), lambda i: (0, 0))))
     kernel = functools.partial(scan_grads_kernel, units // HEAD_DIM, rows, len(weights), len(outputs) - 3)
-    return call(kernel, inputs, outputs, scan_scratch(width, units), chunks, 3_000_000_000)
+    return call(kernel, inputs, outputs, scan_scratch(length, width, units), chunks, 3_000_000_000)
 
 
 def second_forward(place, rows, h, parts, weights, gate_weights, marks, segment_row, params):
@@ -680,7 +699,7 @@
     outputs += [((length, width), bf16, rows_spec(width, last)), sums(units), sums(2 * STATE)]
     scratch = [((SPAN, units), bf16), ((SPAN, width), f32)]
     scratch += [((width, units), bf16)] * 2 + [((width, units), f32)] * 2 + [((8, units), f32)]
-    scratch += scan_scratch(width, units)
+    scratch += scan_scratch(length, width, units)
     kernel = functools.partial(second_backward_kernel, units // HEAD_DIM, rows)
     return call(kernel, inputs, outputs, scratch, chunks, 4_000_000_000)
 

time: 343 us -> 335 us (0.977)
  Pallas kernels: 178 us -> 167 us
    pallas_call x6, Pallas kernels: 141 us -> 130 us  [call(): pl.pallas_call(kernel, grid=(chunks,), in_specs=[spec for _, spec in inpu...]
  transfers between devices with their start and end apart: 51 -> 51, of which waited for: 20 -> 19; matrix products, arithmetic and copies ran while one was open for 3% -> 3% of each run, Pallas kernels for 37% -> 36%
where the time goes in v4:
time: 335 us; the launch traced here: 330 us
  Pallas kernels  167 us (50%)
  waiting for transfers between devices  58.7 us (18%)
  starting transfers between devices  52.7 us (16%)
  blocking collectives  15.9 us (5%)
  local copies, waits for them, and re-layouts  15.4 us (5%)
  between operations  14.9 us (4%)
  other arithmetic  5.32 us (2%)
    pallas_call x6, Pallas kernels, call(): pl.pallas_call(kernel, grid=(chunks,), in_specs=[spec for _, spec in inpu...  130 us
    pallas_call x11, Pallas kernels, plain_call(): pl.pallas_call(body, in_specs=[pl.BlockSpec(memory_space=pltpu.SMEM)] + [...  24.7 us
    ppermute x27, starting transfers between devices, swapped(): return lax.ppermute(block, axis, [(0, 1), (1, 0)])  22.6 us
    ppermute x27, waiting for transfers between devices, swapped(): return lax.ppermute(block, axis, [(0, 1), (1, 0)])  21.7 us
    ppermute x11, waiting for transfers between devices, x_swapped(): return lax.ppermute(block, 'dp', [(i, i ^ 1) for i in range(ranks)])  21.5 us
    all_gather x1, blocking collectives, line_gather(): lax.all_gather(block, 'dp', axis_index_groups=line_groups, axis=0, tiled=...  15.9 us
    ppermute x11, starting transfers between devices, x_swapped(): return lax.ppermute(block, 'dp', [(i, i ^ 1) for i in range(ranks)])  14.4 us
    ppermute x5, waiting for transfers between devices, send(): lax.ppermute(rows, 'dp', [(2 * a + start, 2 * b + start) for a, b in move...  10.5 us
  transfers between devices with their start and end apart: 51, of which 19 were waited for; matrix products, arithmetic and copies ran while one was open for 3% of the time, Pallas kernels for 36%

profile of v4, /device:TPU:0, one launch (start us, length us, event | category | flops | bytes accessed | tf_op | source)
XLA Modules:
  0.0 330.0 jit_solution(17281800306580498038)
XLA Ops:
  7.9 2.9 shard_map.291
  11.4 2.6 collective-permute-start.1
  14.7 1.9 shard_map.292
  16.6 1.6 collective-permute-start.2
  18.3 15.9 %all_gather.9.refs_2_.refs_4_ = bf16[384,640]{1,0:T(8,128)(2,1)S(1)} all-gather(bf16[96,640]{1,0:T(8,128)(2,1)} %get-tuple-element.176), channel_id=1, replica_groups={{0,4,8,12},{2,6,10,14},{1,5,9,13},{3,7,11,15},{16,20,24,28},{18,22,26,3..., dimensions={0}, use_global_device_ids=true | all-gather | bytes 614400 | tf_op jit(solution)/shard_map/all_gather | solution.py:1119
  37.4 1.9 shard_map.293
  39.4 1.6 collective-permute-start.9
  41.0 2.1 shard_map.294
  43.1 5.7 %collective-permute-done.8.refs_4_ = bf16[96,768]{1,0:T(8,128)(2,1)} collective-permute-done((bf16[96,768]{1,0:T(8,128)(2,1)}, bf16[96,768]{1,0:T(8,128)(2,1)}, u32[]{:S(2)}, u32[]{:S(2)}) %collective-permute-start.8) | collective-permute-done | bytes 147488 | tf_op jit(solution)/shard_map/ppermute | solution.py:1113
  48.8 1.5 collective-permute-start.10
  52.6 1.7 slice.44
  56.0 1.9 maximum_select_fusion.refs_0_.refs_1_.h_ref
  58.6 2.0 shard_map.295
  60.7 2.9 all-gather.3.cloned.1.call-done.refs_1_
  63.8 2.3 shard_map.297
  70.2 16.7 %shard_map.296 = (f32[8,768]{1,0:T(8,128)}, bf16[1024,768]{1,0:T(8,128)(2,1)}, f32[1024,768]{1,0:T(8,128)}, f32[1024,768]{1,0:T(8,128)}, f32[1024,768]{1,0:T(8,1...) custom-call(s32[4]{0:T(128)} %pad_add_fusion.place_ref.refs_0_.refs_1_, ...), custom_call_target="tpu_custom_call" | custom-call | flops 2000000000 | bytes 500000 | tf_op jit(solution)/shard_map/pallas_call | solution.py:534
  89.9 3.2 collective-permute-done.16.refs_6_.refs_15_
  93.1 1.5 collective-permute-start.18
  94.7 1.5 collective-permute-start.17
  96.2 4.7 %collective-permute-done.14.refs_4_.refs_15_ = bf16[192,768]{1,0:T(8,128)(2,1)S(1)} collective-permute-done((bf16[192,768]{1,0:T(8,128)(2,1)S(1)}, bf16[192,768]{1,0:T(8,128)(2,1)S(1)}, u32[]{:S(2)}, u32[]{:S(2)}) %collective-permute-start.14) | collective-permute-done | bytes 294944 | tf_op jit(solution)/shard_map/ppermute | solution.py:1113
  102.4 6.7 %shard_map.298 = (f32[1024,768]{1,0:T(8,128)}, bf16[1024,896]{1,0:T(8,128)(2,1)}) custom-call(s32[4]{0:T(128)} %pad_add_fusion.place_ref.refs_0_.refs_1_, bf16[1024,768]{1,0:T(8,128)(2,1)} %get-tuple-element.208.normed_ref.refs_8_.refs_0_, f32[1024,768]{1,0:T(8,128)} %get-tuple-element.209.y_ref.refs_10_.refs_17_, ...), custom_call_target="tpu_custom_call" | custom-call | flops 1000000000 | bytes 500000 | tf_op jit(solution)/shard_map/pallas_call | solution.py:534
  109.9 4.0 %collective-permute-done.19.refs_3_.refs_2_ = bf16[1024,896]{1,0:T(8,128)(2,1)S(1)} collective-permute-done((bf16[1024,896]{1,0:T(8,128)(2,1)}, bf16[1024,896]{1,0:T(8,128)(2,1)S(1)}, u32[]{:S(2)}, u32[]{:S(2)}) %collective-permute-start.19) | collective-permute-done | bytes 1835040 | tf_op jit(solution)/shard_map/ppermute | solution.py:1069
  116.4 1.5 collective-permute-start.20
  117.9 23.2 %shard_map.299 = (bf16[1024,768]{1,0:T(8,128)(2,1)}, f32[8,768]{1,0:T(8,128)}, bf16[1024,768]{1,0:T(8,128)(2,1)}, f32[1024,768]{1,0:T(8,128)}, f32[1024,768]{1,0...) custom-call(s32[4]{0:T(128)} %pad_add_fusion.place_ref.refs_0_.refs_, ...), custom_call_target="tpu_custom_call" | custom-call | flops 3000000000 | bytes 500000 | tf_op jit(solution)/shard_map/pallas_call | solution.py:534
  141.7 4.0 %collective-permute-done.22.refs_6_ = f32[256,768]{1,0:T(8,128)S(1)} collective-permute-done((f32[256,768]{1,0:T(8,128)S(1)}, f32[256,768]{1,0:T(8,128)S(1)}, u32[]{:S(2)}, u32[]{:S(2)}) %collective-permute-start.22) | collective-permute-done | bytes 786464 | tf_op jit(solution)/shard_map/ppermute | solution.py:1069
  147.8 39.0 %shard_map.300 = (bf16[1024,768]{1,0:T(8,128)(2,1)}, f32[1024,768]{1,0:T(8,128)}, bf16[384,5632]{1,0:T(8,128)(2,1)}, f32[8,768]{1,0:T(8,128)}, bf16[1024,768]{1,...) custom-call(s32[4]{0:T(128)} %pad_add_fusion.place_ref.refs_0_.refs_1_, ...), custom_call_target="tpu_custom_call" | custom-call | flops 4000000000 | bytes 500000 | tf_op jit(solution)/shard_map/pallas_call | solution.py:534
  190.2 1.6 collective-permute-done.23.refs_6_
  191.8 17.3 %shard_map.301 = (f32[1024,768]{1,0:T(8,128)}, bf16[1024,768]{1,0:T(8,128)(2,1)}, f32[1024,768]{1,0:T(8,128)}, bf16[384,768]{1,0:T(8,128)(2,1)}, bf16[384,768]{1...) custom-call(s32[4]{0:T(128)} %pad_add_fusion.place_ref.refs_0_.refs_1_, ...), custom_call_target="tpu_custom_call" | custom-call | flops 2000000000 | bytes 500000 | tf_op jit(solution)/shard_map/pallas_call | solution.py:534
  213.1 27.0 %shard_map.302 = (bf16[384,640]{1,0:T(8,128)(2,1)}, bf16[384,640]{1,0:T(8,128)(2,1)}, bf16[384,640]{1,0:T(8,128)(2,1)}, bf16[384,640]{1,0:T(8,128)(2,1)}, bf16[1...) custom-call(bf16[1024,768]{1,0:T(8,128)(2,1)} %get-tuple-element.208.normed_ref.refs_8_.refs_0_, ...), custom_call_target="tpu_custom_call" | custom-call | flops 3000000000 | bytes 500000 | tf_op jit(solution)/shard_map/pallas_call | solution.py:534
  240.3 1.5 collective-permute-start.34
  245.1 7.7 %shard_map.303 = (f32[2,512,768]{2,1,0:T(8,128)}, bf16[512,768]{1,0:T(8,128)(2,1)}, f32[8,768]{1,0:T(8,128)}, bf16[2,512,768]{2,1,0:T(8,128)(2,1)}) custom-call(s32[4]{0:T(128)} %pad_add_fusion.place_ref.refs_0_.refs_1_, bf16[1024,768]{1,0:T(8,128)(2,1)} %get-tuple-element.286.own_ref, bf16[1024,768]{1,0:T(8,128)(2,1)} %copy-done.8, ...), custom_call_target="tpu_custom_call" | custom-call | bytes 500000 | tf_op jit(solution)/shard_map/pallas_call | solution.py:754
  252.9 1.5 shard_map.304
  255.7 4.6 %collective-permute-start.29 = (f32[32,768]{1,0:T(8,128)}, f32[32,768]{1,0:T(8,128)S(1)}, u32[]{:S(2)}, u32[]{:S(2)}) collective-permute-start(f32[32,768]{1,0:T(8,128)} %shard_map.304), channel_id=1, source_target_pairs={{0,4},{2,6},{4,8},{6,10},{8,12},{10,14},{1,5},{3,7},{5,9},{7,11},{... | collective-permute-start | bytes 294920 | tf_op jit(solution)/shard_map/ppermute | solution.py:1129
  260.2 4.3 %collective-permute-done.31 = f32[32,768]{1,0:T(8,128)S(1)} collective-permute-done((f32[32,768]{1,0:T(8,128)}, f32[32,768]{1,0:T(8,128)S(1)}, u32[]{:S(2)}, u32[]{:S(2)}) %collective-permute-start.31) | collective-permute-done | bytes 98336 | tf_op jit(solution)/shard_map/ppermute | solution.py:1129
  268.3 6.2 %collective-permute-done.32 = f32[32,768]{1,0:T(8,128)S(1)} collective-permute-done((f32[32,768]{1,0:T(8,128)S(1)}, f32[32,768]{1,0:T(8,128)S(1)}, u32[]{:S(2)}, u32[]{:S(2)}) %collective-permute-start.32) | collective-permute-done | bytes 98336 | tf_op jit(solution)/shard_map/ppermute | solution.py:1129
  274.6 3.7 %shard_map.305.refs_0_ = bf16[384,1408]{1,0:T(8,128)(2,1)} custom-call(s32[4]{0:T(128)} %pad_add_fusion.place_ref.refs_0_.refs_1_, bf16[96,5632]{1,0:T(8,128)(2,1)} %reduce-scatter.3.cloned.1.call-done.refs_0_.refs_1_, bf16[384,640]{1,0:T(8,128)(2,1)} %get-tuple-element.303.refs_1_, bf16[384,640]{1,0:T(8,128)(2,1)} %collective-permute-done.34.refs_2_, ...), custom_call_target="tpu_custom_call" | custom-call | bytes 500000 | tf_op jit(solution)/shard_map/pallas_call | solution.py:900
  278.4 1.6 collective-permute-start.37
  280.0 3.1 collective-permute-done.37.away_ref
  283.1 1.5 collective-permute-start.38
  284.6 1.6 shard_map.307
  286.3 2.3 shard_map.309
  293.6 11.1 %collective-permute-done.40 = f32[32,384]{1,0:T(8,128)S(1)} collective-permute-done((f32[32,384]{1,0:T(8,128)S(1)}, f32[32,384]{1,0:T(8,128)S(1)}, u32[]{:S(2)}, u32[]{:S(2)}) %collective-permute-start.40) | collective-permute-done | bytes 49184 | tf_op jit(solution)/shard_map/ppermute | solution.py:1113
  305.3 1.9 shard_map.308
  307.2 2.4 collective-permute-done.38.away_ref
  310.4 3.0 shard_map.306.refs_0_
  314.6 1.5 collective-permute-start.46
  317.8 2.1 collective-permute-done.45.refs_6_
  320.6 2.3 shard_map.310
  (185 shorter events, 50.7 us)
Async XLA Ops:
  7.2 56.4 %all-gather.3.cloned.1.call-start = ((), (), s32[]{:S(2)}) async-start(), calls=%async_computation.2 | async-start | bytes 1351680 | tf_op jit(solution)/shard_map/all_gather | solution.py:1119
  11.4 22.8 %collective-permute-start.1 = (bf16[256,768]{1,0:T(8,128)(2,1)S(1)}, bf16[256,768]{1,0:T(8,128)(2,1)}, u32[]{:S(2)}, u32[]{:S(2)}) collective-permute-start(bf16[256,768]{1,0:T(8,128)(2,1)S(1)} %dynamic-slice_bitcast_fusion.2), channel_id=1, source_target_pairs={{0,1},{1,0},{2,3},{3,2},{4,5},{5,4},{6,7},{7,6},{8,9},{9,8},{10,11... | collective-permute-start | bytes 1179656 | tf_op jit(solution)/shard_map/ppermute | solution.py:1069
  16.6 17.5 %collective-permute-start.2 = (bf16[32,384]{1,0:T(8,128)(2,1)}, bf16[32,384]{1,0:T(8,128)(2,1)S(1)}, u32[]{:S(2)}, u32[]{:S(2)}) collective-permute-start(bf16[32,384]{1,0:T(8,128)(2,1)} %get-tuple-element.177), channel_id=1, source_target_pairs={{0,1},{1,0},{2,3},{3,2},{4,5},{5,4},{6,7},{7,6},{8,9},{9,8},{10,11... | collective-permute-start | bytes 73736 | tf_op jit(solution)/shard_map/ppermute | solution.py:1069
  34.2 81.0 %all-gather.5.cloned.1.call-start = ((), (), s32[]{:S(2)}) async-start(), calls=%async_computation.3 | async-start | bytes 2949120 | tf_op jit(solution)/shard_map/all_gather | solution.py:1119
  34.2 16.1 %collective-permute-start.5 = (bf16[384,640]{1,0:T(8,128)(2,1)S(1)}, bf16[384,640]{1,0:T(8,128)(2,1)S(1)}, u32[]{:S(2)}, u32[]{:S(2)}) collective-permute-start(bf16[384,640]{1,0:T(8,128)(2,1)S(1)} %all_gather.9.refs_2_.refs_4_), channel_id=1, source_target_pairs={{0,1},{1,0},{2,3},{3,2},{4,5},{5,4},{6,7},{7,6},{8,9},{9,8},{10,11... | collective-permute-start | bytes 1474568 | tf_op jit(solution)/shard_map/ppermute | solution.py:1069
  34.8 17.9 %collective-permute-start.4 = (bf16[384,640]{1,0:T(8,128)(2,1)S(1)}, bf16[384,640]{1,0:T(8,128)(2,1)}, u32[]{:S(2)}, u32[]{:S(2)}) collective-permute-start(bf16[384,640]{1,0:T(8,128)(2,1)S(1)} %all_gather.9.refs_2_.refs_4_), channel_id=1, source_target_pairs={{0,2},{2,0},{4,6},{6,4},{8,10},{10,8},{12,14},{14,12},{1,3},{3,1},... | collective-permute-start | bytes 1474568 | tf_op jit(solution)/shard_map/ppermute | solution.py:1113
  36.3 18.5 %collective-permute-start.3 = (bf16[256,768]{1,0:T(8,128)(2,1)}, bf16[256,768]{1,0:T(8,128)(2,1)}, u32[]{:S(2)}, u32[]{:S(2)}) collective-permute-start(bf16[256,768]{1,0:T(8,128)(2,1)} %collective-permute-done.1), channel_id=1, source_target_pairs={{0,16},{16,0},{1,17},{17,1},{2,18},{18,2},{3,19},{19,3},{4,20},{20... | collective-permute-start | bytes 1179656 | tf_op jit(solution)/shard_map/ppermute | solution.py:1069
  36.3 12.5 %collective-permute-start.8 = (bf16[96,768]{1,0:T(8,128)(2,1)}, bf16[96,768]{1,0:T(8,128)(2,1)}, u32[]{:S(2)}, u32[]{:S(2)}) collective-permute-start(bf16[96,768]{1,0:T(8,128)(2,1)} %get-tuple-element.186.refs_3_), channel_id=1, source_target_pairs={{0,2},{2,0},{4,6},{6,4},{8,10},{10,8},{12,14},{14,12},{1,3},{3,1},... | collective-permute-start | bytes 442376 | tf_op jit(solution)/shard_map/ppermute | solution.py:1113
  39.4 18.5 %collective-permute-start.9 = (bf16[96,768]{1,0:T(8,128)(2,1)S(1)}, bf16[96,768]{1,0:T(8,128)(2,1)S(1)}, u32[]{:S(2)}, u32[]{:S(2)}) collective-permute-start(bf16[96,768]{1,0:T(8,128)(2,1)S(1)} %copy-done.32), channel_id=1, source_target_pairs={{0,1},{1,0},{2,3},{3,2},{4,5},{5,4},{6,7},{7,6},{8,9},{9,8},{10,11... | collective-permute-start | bytes 442376 | tf_op jit(solution)/shard_map/ppermute | solution.py:1069
  48.8 9.1 %collective-permute-start.10 = (bf16[96,768]{1,0:T(8,128)(2,1)}, bf16[96,768]{1,0:T(8,128)(2,1)S(1)}, u32[]{:S(2)}, u32[]{:S(2)}) collective-permute-start(bf16[96,768]{1,0:T(8,128)(2,1)} %collective-permute-done.8.refs_4_), channel_id=1, source_target_pairs={{0,1},{1,0},{2,3},{3,2},{4,5},{5,4},{6,7},{7,6},{8,9},{9,8},{10,11... | collective-permute-start | bytes 442376 | tf_op jit(solution)/shard_map/ppermute | solution.py:1069
  51.1 9.5 %collective-permute-start.7 = (bf16[192,640]{1,0:T(8,128)(2,1)}, bf16[192,640]{1,0:T(8,128)(2,1)S(1)}, u32[]{:S(2)}, u32[]{:S(2)}) collective-permute-start(bf16[192,640]{1,0:T(8,128)(2,1)} %slice.45), channel_id=1, source_target_pairs={{0,2},{2,0},{4,6},{6,4},{8,10},{10,8},{12,14},{14,12},{1,3},{3,1},... | collective-permute-start | bytes 737288 | tf_op jit(solution)/shard_map/ppermute | solution.py:1113
  54.3 6.4 %collective-permute-start.6 = (bf16[192,640]{1,0:T(8,128)(2,1)}, bf16[192,640]{1,0:T(8,128)(2,1)S(1)}, u32[]{:S(2)}, u32[]{:S(2)}) collective-permute-start(bf16[192,640]{1,0:T(8,128)(2,1)} %slice.44), channel_id=1, source_target_pairs={{0,1},{1,0},{2,3},{3,2},{4,5},{5,4},{6,7},{7,6},{8,9},{9,8},{10,11... | collective-permute-start | bytes 737288 | tf_op jit(solution)/shard_map/ppermute | solution.py:1069
  63.6 210.9 %reduce-scatter.3.cloned.1.call-start = ((), (), s32[]{:S(2)}) async-start(), calls=%async_computation.4 | async-start | bytes 5406720 | tf_op jit(solution)/shard_map/reduce_scatter | solution.py:1122
  66.1 20.7 %collective-permute-start.12 = (bf16[384,768]{1,0:T(8,128)(2,1)}, bf16[384,768]{1,0:T(8,128)(2,1)S(1)}, u32[]{:S(2)}, u32[]{:S(2)}) collective-permute-start(bf16[384,768]{1,0:T(8,128)(2,1)} %get-tuple-element.210.refs_0_.refs_11_), channel_id=1, source_target_pairs={{0,1},{1,0},{2,3},{3,2},{4,5},{5,4},{6,7},{7,6},{8,9},{9,8},{10,11... | collective-permute-start | bytes 1769480 | tf_op jit(solution)/shard_map/ppermute | solution.py:1069
  67.6 19.3 %collective-permute-start.11 = (bf16[384,768]{1,0:T(8,128)(2,1)}, bf16[384,768]{1,0:T(8,128)(2,1)S(1)}, u32[]{:S(2)}, u32[]{:S(2)}) collective-permute-start(bf16[384,768]{1,0:T(8,128)(2,1)} %get-tuple-element.210.refs_0_.refs_11_), channel_id=1, source_target_pairs={{0,2},{2,0},{4,6},{6,4},{8,10},{10,8},{12,14},{14,12},{1,3},{3,1},... | collective-permute-start | bytes 1769480 | tf_op jit(solution)/shard_map/ppermute | solution.py:1113
  69.1 24.0 %collective-permute-start.16 = (bf16[384,640]{1,0:T(8,128)(2,1)}, bf16[384,640]{1,0:T(8,128)(2,1)S(1)}, u32[]{:S(2)}, u32[]{:S(2)}) collective-permute-start(bf16[384,640]{1,0:T(8,128)(2,1)} %get-tuple-element.220.refs_4_.refs_13_), channel_id=1, source_target_pairs={{0,1},{1,0},{2,3},{3,2},{4,5},{5,4},{6,7},{7,6},{8,9},{9,8},{10,11... | collective-permute-start | bytes 1474568 | tf_op jit(solution)/shard_map/ppermute | solution.py:1069
  69.6 25.1 %collective-permute-start.15 = (bf16[384,640]{1,0:T(8,128)(2,1)}, bf16[384,640]{1,0:T(8,128)(2,1)S(1)}, u32[]{:S(2)}, u32[]{:S(2)}) collective-permute-start(bf16[384,640]{1,0:T(8,128)(2,1)} %get-tuple-element.220.refs_4_.refs_13_), channel_id=1, source_target_pairs={{0,2},{2,0},{4,6},{6,4},{8,10},{10,8},{12,14},{14,12},{1,3},{3,1},... | collective-permute-start | bytes 1474568 | tf_op jit(solution)/shard_map/ppermute | solution.py:1113
  87.0 14.0 %collective-permute-start.14 = (bf16[192,768]{1,0:T(8,128)(2,1)S(1)}, bf16[192,768]{1,0:T(8,128)(2,1)S(1)}, u32[]{:S(2)}, u32[]{:S(2)}) collective-permute-start(bf16[192,768]{1,0:T(8,128)(2,1)S(1)} %slice.36), channel_id=1, source_target_pairs={{0,2},{2,0},{4,6},{6,4},{8,10},{10,8},{12,14},{14,12},{1,3},{3,1},... | collective-permute-start | bytes 884744 | tf_op jit(solution)/shard_map/ppermute | solution.py:1113
  88.4 12.5 %collective-permute-start.13 = (bf16[192,768]{1,0:T(8,128)(2,1)S(1)}, bf16[192,768]{1,0:T(8,128)(2,1)S(1)}, u32[]{:S(2)}, u32[]{:S(2)}) collective-permute-start(bf16[192,768]{1,0:T(8,128)(2,1)S(1)} %slice.35), channel_id=1, source_target_pairs={{0,1},{1,0},{2,3},{3,2},{4,5},{5,4},{6,7},{7,6},{8,9},{9,8},{10,11... | collective-permute-start | bytes 884744 | tf_op jit(solution)/shard_map/ppermute | solution.py:1069
  93.1 15.9 %collective-permute-start.18 = (bf16[192,640]{1,0:T(8,128)(2,1)S(1)}, bf16[192,640]{1,0:T(8,128)(2,1)S(1)}, u32[]{:S(2)}, u32[]{:S(2)}) collective-permute-start(bf16[192,640]{1,0:T(8,128)(2,1)S(1)} %slice.47), channel_id=1, source_target_pairs={{0,2},{2,0},{4,6},{6,4},{8,10},{10,8},{12,14},{14,12},{1,3},{3,1},... | collective-permute-start | bytes 737288 | tf_op jit(solution)/shard_map/ppermute | solution.py:1113
  94.7 14.4 %collective-permute-start.17 = (bf16[192,640]{1,0:T(8,128)(2,1)S(1)}, bf16[192,640]{1,0:T(8,128)(2,1)S(1)}, u32[]{:S(2)}, u32[]{:S(2)}) collective-permute-start(bf16[192,640]{1,0:T(8,128)(2,1)S(1)} %slice.46), channel_id=1, source_target_pairs={{0,1},{1,0},{2,3},{3,2},{4,5},{5,4},{6,7},{7,6},{8,9},{9,8},{10,11... | collective-permute-start | bytes 737288 | tf_op jit(solution)/shard_map/ppermute | solution.py:1069
  109.9 4.0 %collective-permute-start.19 = (bf16[1024,896]{1,0:T(8,128)(2,1)}, bf16[1024,896]{1,0:T(8,128)(2,1)S(1)}, u32[]{:S(2)}, u32[]{:S(2)}) collective-permute-start(bf16[1024,896]{1,0:T(8,128)(2,1)} %get-tuple-element.218.refs_2_.refs_1_), channel_id=1, source_target_pairs={{0,16},{16,0},{1,17},{17,1},{2,18},{18,2},{3,19},{19,3},{4,20},{20... | collective-permute-start | bytes 5505032 | tf_op jit(solution)/shard_map/ppermute | solution.py:1069
  116.4 24.7 %collective-permute-start.20 = (f32[256,768]{1,0:T(8,128)S(1)}, f32[256,768]{1,0:T(8,128)S(1)}, u32[]{:S(2)}, u32[]{:S(2)}) collective-permute-start(f32[256,768]{1,0:T(8,128)S(1)} %dynamic-slice_bitcast_fusion), channel_id=1, source_target_pairs={{0,1},{1,0},{2,3},{3,2},{4,5},{5,4},{6,7},{7,6},{8,9},{9,8},{10,11... | collective-permute-start | bytes 2359304 | tf_op jit(solution)/shard_map/ppermute | solution.py:1069
  141.1 5.2 %collective-permute-start.21 = (bf16[1024,896]{1,0:T(8,128)(2,1)}, bf16[1024,896]{1,0:T(8,128)(2,1)S(1)}, u32[]{:S(2)}, u32[]{:S(2)}) collective-permute-start(bf16[1024,896]{1,0:T(8,128)(2,1)} %get-tuple-element.243.refs_2_), channel_id=1, source_target_pairs={{0,16},{16,0},{1,17},{17,1},{2,18},{18,2},{3,19},{19,3},{4,20},{20... | collective-permute-start | bytes 5505032 | tf_op jit(solution)/shard_map/ppermute | solution.py:1069
  141.2 4.5 %collective-permute-start.22 = (f32[256,768]{1,0:T(8,128)S(1)}, f32[256,768]{1,0:T(8,128)S(1)}, u32[]{:S(2)}, u32[]{:S(2)}) collective-permute-start(f32[256,768]{1,0:T(8,128)S(1)} %collective-permute-done.20.refs_5_), channel_id=1, source_target_pairs={{0,16},{16,0},{1,17},{17,1},{2,18},{18,2},{3,19},{19,3},{4,20},{20... | collective-permute-start | bytes 2359304 | tf_op jit(solution)/shard_map/ppermute | solution.py:1069
  186.8 126.6 %reduce-scatter.5.cloned.1.call-start = ((), (), s32[]{:S(2)}) async-start(), calls=%async_computation.5 | async-start | bytes 1351680 | tf_op jit(solution)/shard_map/reduce_scatter | solution.py:1122
  189.6 20.0 %collective-permute-start.24 = (bf16[512,768]{1,0:T(8,128)(2,1)}, bf16[512,768]{1,0:T(8,128)(2,1)S(1)}, u32[]{:S(2)}, u32[]{:S(2)}) collective-permute-start(bf16[512,768]{1,0:T(8,128)(2,1)} %constant_dynamic-slice_fusion), channel_id=1, source_target_pairs={{0,1},{1,0},{2,3},{3,2},{4,5},{5,4},{6,7},{7,6},{8,9},{9,8},{10,11... | collective-permute-start | bytes 2359304 | tf_op jit(solution)/shard_map/ppermute | solution.py:1069
  209.7 30.5 %collective-permute-start.25 = (bf16[384,768]{1,0:T(8,128)(2,1)}, bf16[384,768]{1,0:T(8,128)(2,1)S(1)}, u32[]{:S(2)}, u32[]{:S(2)}) collective-permute-start(bf16[384,768]{1,0:T(8,128)(2,1)} %get-tuple-element.283), channel_id=1, source_target_pairs={{0,2},{2,0},{4,6},{6,4},{8,10},{10,8},{12,14},{14,12},{1,3},{3,1},... | collective-permute-start | bytes 1769480 | tf_op jit(solution)/shard_map/ppermute | solution.py:1113
  211.1 29.1 %collective-permute-start.26 = (bf16[384,768]{1,0:T(8,128)(2,1)}, bf16[384,768]{1,0:T(8,128)(2,1)S(1)}, u32[]{:S(2)}, u32[]{:S(2)}) collective-permute-start(bf16[384,768]{1,0:T(8,128)(2,1)} %get-tuple-element.284), channel_id=1, source_target_pairs={{0,1},{1,0},{2,3},{3,2},{4,5},{5,4},{6,7},{7,6},{8,9},{9,8},{10,11... | collective-permute-start | bytes 1769480 | tf_op jit(solution)/shard_map/ppermute | solution.py:1069
  211.7 28.5 %collective-permute-start.27 = (bf16[384,768]{1,0:T(8,128)(2,1)}, bf16[384,768]{1,0:T(8,128)(2,1)S(1)}, u32[]{:S(2)}, u32[]{:S(2)}) collective-permute-start(bf16[384,768]{1,0:T(8,128)(2,1)} %get-tuple-element.285), channel_id=1, source_target_pairs={{0,3},{1,2},{2,1},{3,0},{4,7},{5,6},{6,5},{7,4},{8,11},{9,10},{10,... | collective-permute-start | bytes 1769480 | tf_op jit(solution)/shard_map/ppermute | solution.py:1161
  240.2 3.7 %collective-permute-start.28 = (bf16[1024,768]{1,0:T(8,128)(2,1)}, bf16[1024,768]{1,0:T(8,128)(2,1)S(1)}, u32[]{:S(2)}, u32[]{:S(2)}) collective-permute-start(bf16[1024,768]{1,0:T(8,128)(2,1)} %get-tuple-element.286.own_ref), channel_id=1, source_target_pairs={{0,16},{16,0},{1,17},{17,1},{2,18},{18,2},{3,19},{19,3},{4,20},{20... | collective-permute-start | bytes 4718600 | tf_op jit(solution)/shard_map/ppermute | solution.py:1069
  240.3 27.0 %collective-permute-start.34 = (bf16[384,640]{1,0:T(8,128)(2,1)}, bf16[384,640]{1,0:T(8,128)(2,1)}, u32[]{:S(2)}, u32[]{:S(2)}) collective-permute-start(bf16[384,640]{1,0:T(8,128)(2,1)} %get-tuple-element.300), channel_id=1, source_target_pairs={{0,2},{2,0},{4,6},{6,4},{8,10},{10,8},{12,14},{14,12},{1,3},{3,1},... | collective-permute-start | bytes 1474568 | tf_op jit(solution)/shard_map/ppermute | solution.py:1113
  241.8 26.4 %collective-permute-start.35 = (bf16[384,640]{1,0:T(8,128)(2,1)}, bf16[384,640]{1,0:T(8,128)(2,1)}, u32[]{:S(2)}, u32[]{:S(2)}) collective-permute-start(bf16[384,640]{1,0:T(8,128)(2,1)} %get-tuple-element.301), channel_id=1, source_target_pairs={{0,1},{1,0},{2,3},{3,2},{4,5},{5,4},{6,7},{7,6},{8,9},{9,8},{10,11... | collective-permute-start | bytes 1474568 | tf_op jit(solution)/shard_map/ppermute | solution.py:1069
  242.4 25.9 %collective-permute-start.36 = (bf16[384,640]{1,0:T(8,128)(2,1)}, bf16[384,640]{1,0:T(8,128)(2,1)}, u32[]{:S(2)}, u32[]{:S(2)}) collective-permute-start(bf16[384,640]{1,0:T(8,128)(2,1)} %get-tuple-element.302), channel_id=1, source_target_pairs={{0,3},{1,2},{2,1},{3,0},{4,7},{5,6},{6,5},{7,4},{8,11},{9,10},{10,... | collective-permute-start | bytes 1474568 | tf_op jit(solution)/shard_map/ppermute | solution.py:1161
  254.4 10.2 %collective-permute-start.31 = (f32[32,768]{1,0:T(8,128)}, f32[32,768]{1,0:T(8,128)S(1)}, u32[]{:S(2)}, u32[]{:S(2)}) collective-permute-start(f32[32,768]{1,0:T(8,128)} %shard_map.304), channel_id=1, source_target_pairs={{4,0},{6,2},{8,4},{10,6},{12,8},{14,10},{5,1},{7,3},{9,5},{11,7},{... | collective-permute-start | bytes 294920 | tf_op jit(solution)/shard_map/ppermute | solution.py:1129
  255.7 8.9 %collective-permute-start.29 = (f32[32,768]{1,0:T(8,128)}, f32[32,768]{1,0:T(8,128)S(1)}, u32[]{:S(2)}, u32[]{:S(2)}) collective-permute-start(f32[32,768]{1,0:T(8,128)} %shard_map.304), channel_id=1, source_target_pairs={{0,4},{2,6},{4,8},{6,10},{8,12},{10,14},{1,5},{3,7},{5,9},{7,11},{... | collective-permute-start | bytes 294920 | tf_op jit(solution)/shard_map/ppermute | solution.py:1129
  264.6 9.9 %collective-permute-start.33 = (f32[32,768]{1,0:T(8,128)S(1)}, f32[32,768]{1,0:T(8,128)S(1)}, u32[]{:S(2)}, u32[]{:S(2)}) collective-permute-start(f32[32,768]{1,0:T(8,128)S(1)} %broadcast_select_fusion.3), channel_id=1, source_target_pairs={{4,12},{6,14},{8,0},{10,2},{5,13},{7,15},{9,1},{11,3},{20,28},{22,... | collective-permute-start | bytes 294920 | tf_op jit(solution)/shard_map/ppermute | solution.py:1129
  266.0 8.5 %collective-permute-start.32 = (f32[32,768]{1,0:T(8,128)S(1)}, f32[32,768]{1,0:T(8,128)S(1)}, u32[]{:S(2)}, u32[]{:S(2)}) collective-permute-start(f32[32,768]{1,0:T(8,128)S(1)} %collective-permute-done.31), channel_id=1, source_target_pairs={{8,4},{10,6},{4,0},{6,2},{9,5},{11,7},{5,1},{7,3},{24,20},{26,22},... | collective-permute-start | bytes 294920 | tf_op jit(solution)/shard_map/ppermute | solution.py:1129
  267.3 7.2 %collective-permute-start.30 = (f32[32,768]{1,0:T(8,128)S(1)}, f32[32,768]{1,0:T(8,128)S(1)}, u32[]{:S(2)}, u32[]{:S(2)}) collective-permute-start(f32[32,768]{1,0:T(8,128)S(1)} %collective-permute-done.29), channel_id=1, source_target_pairs={{4,8},{6,10},{8,12},{10,14},{5,9},{7,11},{9,13},{11,15},{20,24},{2... | collective-permute-start | bytes 294920 | tf_op jit(solution)/shard_map/ppermute | solution.py:1129
  278.4 4.7 %collective-permute-start.37 = (f32[32,768]{1,0:T(8,128)S(1)}, f32[32,768]{1,0:T(8,128)S(1)}, u32[]{:S(2)}, u32[]{:S(2)}) collective-permute-start(f32[32,768]{1,0:T(8,128)S(1)} %add_add_fusion.own_ref), channel_id=1, source_target_pairs={{0,1},{1,0},{2,3},{3,2},{4,5},{5,4},{6,7},{7,6},{8,9},{9,8},{10,11... | collective-permute-start | bytes 294920 | tf_op jit(solution)/shard_map/ppermute | solution.py:1069
  283.1 26.5 %collective-permute-start.38 = (bf16[512,768]{1,0:T(8,128)(2,1)}, bf16[512,768]{1,0:T(8,128)(2,1)S(1)}, u32[]{:S(2)}, u32[]{:S(2)}) collective-permute-start(bf16[512,768]{1,0:T(8,128)(2,1)} %get-tuple-element.315), channel_id=1, source_target_pairs={{0,1},{1,0},{2,3},{3,2},{4,5},{5,4},{6,7},{7,6},{8,9},{9,8},{10,11... | collective-permute-start | bytes 2359304 | tf_op jit(solution)/shard_map/ppermute | solution.py:1069
  286.3 5.8 %collective-permute-start.39 = (f32[16,384]{1,0:T(8,128)}, f32[16,384]{1,0:T(8,128)S(1)}, u32[]{:S(2)}, u32[]{:S(2)}) collective-permute-start(f32[16,384]{1,0:T(8,128)} %get-tuple-element.320), channel_id=1, source_target_pairs={{0,16},{16,0},{1,17},{17,1},{2,18},{18,2},{3,19},{19,3},{4,20},{20... | collective-permute-start | bytes 73736 | tf_op jit(solution)/shard_map/ppermute | solution.py:1069
  288.6 24.8 %collective-permute-start.41 = (bf16[96,1408]{1,0:T(8,128)(2,1)}, bf16[96,1408]{1,0:T(8,128)(2,1)S(1)}, u32[]{:S(2)}, u32[]{:S(2)}) collective-permute-start(bf16[96,1408]{1,0:T(8,128)(2,1)} %get-tuple-element.325), channel_id=1, source_target_pairs={{0,2},{2,0},{4,6},{6,4},{8,10},{10,8},{12,14},{14,12},{1,3},{3,1},... | collective-permute-start | bytes 811016 | tf_op jit(solution)/shard_map/ppermute | solution.py:1113
  290.0 23.5 %collective-permute-start.42 = (bf16[96,1408]{1,0:T(8,128)(2,1)}, bf16[96,1408]{1,0:T(8,128)(2,1)S(1)}, u32[]{:S(2)}, u32[]{:S(2)}) collective-permute-start(bf16[96,1408]{1,0:T(8,128)(2,1)} %get-tuple-element.326), channel_id=1, source_target_pairs={{0,1},{1,0},{2,3},{3,2},{4,5},{5,4},{6,7},{7,6},{8,9},{9,8},{10,11... | collective-permute-start | bytes 811016 | tf_op jit(solution)/shard_map/ppermute | solution.py:1069
  290.6 22.9 %collective-permute-start.43 = (bf16[96,1408]{1,0:T(8,128)(2,1)}, bf16[96,1408]{1,0:T(8,128)(2,1)S(1)}, u32[]{:S(2)}, u32[]{:S(2)}) collective-permute-start(bf16[96,1408]{1,0:T(8,128)(2,1)} %get-tuple-element.327), channel_id=1, source_target_pairs={{0,3},{1,2},{2,1},{3,0},{4,7},{5,6},{6,5},{7,4},{8,11},{9,10},{10,... | collective-permute-start | bytes 811016 | tf_op jit(solution)/shard_map/ppermute | solution.py:1161
  292.1 12.5 %collective-permute-start.40 = (f32[32,384]{1,0:T(8,128)S(1)}, f32[32,384]{1,0:T(8,128)S(1)}, u32[]{:S(2)}, u32[]{:S(2)}) collective-permute-start(f32[32,384]{1,0:T(8,128)S(1)} %constant_dynamic-update-slice_fusion), channel_id=1, source_target_pairs={{0,2},{2,0},{4,6},{6,4},{8,10},{10,8},{12,14},{14,12},{1,3},{3,1},... | collective-permute-start | bytes 147464 | tf_op jit(solution)/shard_map/ppermute | solution.py:1113
  313.7 6.2 %collective-permute-start.44 = (bf16[96,1408]{1,0:T(8,128)(2,1)S(1)}, bf16[96,1408]{1,0:T(8,128)(2,1)S(1)}, u32[]{:S(2)}, u32[]{:S(2)}) collective-permute-start(bf16[96,1408]{1,0:T(8,128)(2,1)S(1)} %get-tuple-element.335), channel_id=1, source_target_pairs={{0,16},{16,0},{1,17},{17,1},{2,18},{18,2},{3,19},{19,3},{4,20},{20... | collective-permute-start | bytes 811016 | tf_op jit(solution)/shard_map/ppermute | solution.py:1069
  316.0 3.8 %collective-permute-start.45 = (bf16[96,128]{1,0:T(8,128)(2,1)S(1)}, bf16[96,128]{1,0:T(8,128)(2,1)S(1)}, u32[]{:S(2)}, u32[]{:S(2)}) collective-permute-start(bf16[96,128]{1,0:T(8,128)(2,1)S(1)} %get-tuple-element.340), channel_id=1, source_target_pairs={{0,1},{1,0},{2,3},{3,2},{4,5},{5,4},{6,7},{7,6},{8,9},{9,8},{10,11... | collective-permute-start | bytes 73736 | tf_op jit(solution)/shard_map/ppermute | solution.py:1069
  (45 other events, 375.5 us)
Sparse Core Ops, SparseCore 0:
  34.3 29.2 all-gather.2
  65.2 49.9 all-gather.4
  187.0 78.3 reduce-scatter.2
  278.4 30.5 reduce-scatter.4

commit v5 on v4

--- a/solution.py
+++ b/solution.py
@@ -118,6 +118,22 @@
     first, last = columns
     mine = place_ref[0]
     size = refs[0].shape[1] // 4
+    if rows % 32:
+
+        def piece(index, step):
+            ref, offset = (refs[0], index * size) if len(refs) == 1 else (refs[index], 0)
+            if index == 3 and len(refs) == 5 and step >= ref.shape[0] // rows:
+                ref, step = refs[4], step - ref.shape[0] // rows
+            return ref[step * rows : (step + 1) * rows, offset + first : offset + last]
+
+        for turned in range(2):
+            target = start + turned * (last - first)
+            for step in range(weights.shape[0] // (2 * rows)):
+                own, moved = piece(2 * turned, step), piece(2 * turned + 1, step)
+                row = 2 * step * rows
+                weights[row : row + rows, target : target + last - first] = jnp.where(mine == 0, own, moved)
+                weights[row + rows : row + 2 * rows, target : target + last - first] = jnp.where(mine == 0, moved, own)
+        return
     base = 0
     for index in range(len(refs) if len(refs) > 1 else 4):
         moved, turned = PLANE[min(index, 3)]
@@ -134,6 +150,17 @@
     first, last = columns
     mine = place_ref[0]
     size = refs[0].shape[1] // 4
+    if rows % 32:
+        for index, (moved, turned) in enumerate(PLANE):
+            ref, offset = (refs[0], index * size + base) if len(refs) == 1 else (refs[index], 0)
+            source = start + (last - first if turned else 0)
+            for step in range(ref.shape[0] // rows):
+                row = 2 * step * rows
+                upper = acc[row : row + rows, source : source + last - first]
+                lower = acc[row + rows : row + 2 * rows, source : source + last - first]
+                block = jnp.where(mine == 0, lower, upper) if moved else jnp.where(mine == 0, upper, lower)
+                ref[step * rows : (step + 1) * rows, offset + first : offset + last] = block.astype(bf16)
+        return
     for index, (moved, turned) in enumerate(PLANE):
         ref, offset = (refs[0], index * size + base) if len(refs) == 1 else (refs[index], 0)
         place = 1 - mine if moved else mine
@@ -705,8 +732,9 @@
 
 
 def finish_kernel(
-    place_ref, own_ref, other_ref, h_ref, grad_out_ref, gain_ref, rows_ref, away_ref, grad_ref, low_ref, sums_ref, placed_ref, sums
+    place_ref, own_ref, other_ref, h_ref, grad_out_ref, gain_ref, rows_ref, away_ref, *refs
 ):
+    small_refs, (grad_ref, low_ref, smalls_ref, placed_ref, sums) = refs[:6], refs[6:]
     step = pl.program_id(0)
 
     @pl.when(step == 0)
@@ -718,7 +746,10 @@
     grad, gain_term = norm_backward(grad_normed, h_ref[...].astype(f32), next_grad.astype(bf16).astype(f32), gain_ref[0:1, :])
     rows = jnp.where(place_ref[3] == 0, grad, next_grad)
     sums[0:1, :] += jnp.sum(gain_term, axis=0, keepdims=True)
-    sums_ref[...] = sums[...]
+
+    @pl.when(step == pl.num_programs(0) - 1)
+    def _():
+        small_kernel(*small_refs, sums, smalls_ref)
 
     @pl.when(step < pl.num_programs(0) // 2)
     def _():
@@ -731,9 +762,10 @@
         placed_ref[0] = rows_ref[...]
 
 
-def finish(place, own, other, h, grad_out, gain, produced, produced_away):
+def finish(place, own, other, h, grad_out, gain, produced, produced_away, smalls):
     length, width = h.shape
     steps = length // SPAN
+    units = smalls[0].shape[1]
     part = steps // 2
 
     def rows(i, place):
@@ -761,11 +793,12 @@
                 whole,
                 pl.BlockSpec((SPAN, width), lambda i, place: (part * place[1] + late(i), 0)),
                 pl.BlockSpec((SPAN, width), lambda i, place: (early(i), 0)),
-            ],
+            ]
+            + [pl.BlockSpec(array.shape, lambda i, place: (0, 0)) for array in smalls],
             out_specs=[
                 pl.BlockSpec((1, SPAN, width), lambda i, place: (place[1], late(i), 0)),
                 pl.BlockSpec((SPAN, width), lambda i, place: (early(i), 0)),
-                whole,
+                pl.BlockSpec((32, units), lambda i, place: (0, 0)),
                 pl.BlockSpec((1, SPAN, width), placed),
             ],
             scratch_shapes=[pltpu.VMEM((8, width), f32)],
@@ -773,12 +806,12 @@
         out_shape=[
             jax.ShapeDtypeStruct((2, length // 2, width), f32),
             jax.ShapeDtypeStruct((length // 2, width), bf16),
-            jax.ShapeDtypeStruct((8, width), f32),
+            jax.ShapeDtypeStruct((32, units), f32),
             jax.ShapeDtypeStruct((2, length // 2, width), bf16),
         ],
         compiler_params=pltpu.CompilerParams(vmem_limit_bytes=VMEM_LIMIT, dimension_semantics=("arbitrary",)),
         cost_estimate=pl.CostEstimate(flops=0, bytes_accessed=500_000, transcendentals=0),
-    )(place, own, other, h, grad_out, gain, produced, produced_away)
+    )(place, own, other, h, grad_out, gain, produced, produced_away, *smalls)
 
 
 def placed_kernel(place_ref, away_ref, rows_ref, out_ref):
@@ -1209,8 +1242,9 @@
     gate_first = plane_end(*gate_half)
     results = gate_forward(place, block_rows, normed_first, saved_first[2], gate_first, params[0])
     (gated_first, part), scan_second = tied(results, plane_end(*next_half))
+    part, teacher = tied(part, teacher)
     parts_first = (part, swapped(part, "section"))
-    parts_first, teacher, gate_second = tied(parts_first, teacher, gate_second)
+    parts_first, gate_second = tied(parts_first, gate_second)
     results = second_forward(
         place, block_rows, x_rows, parts_first, scan_second, gate_second, marks, segment_row, params[1]
     )
@@ -1269,12 +1303,17 @@
     scan_reduce = over_plane(*results[:4])
     part, sums, states_sums = results[4:]
     sums_first = (gate_sums_first, sums, states_sums)
-    grad_rows, grad_low, gain_sums, layer_outputs = finish(
-        place, part, swapped(part, "section"), x_rows, grad_hidden, gain_first, produced, produced_away
-    )
-    smalls = plain_call(
-        lambda place_ref, *refs: small_kernel(*refs), place, sums_first + sums_second + (gain_sums,), [((32, units), f32)]
-    )[0]
+    grad_rows, grad_low, smalls, layer_outputs = finish(
+        place,
+        part,
+        swapped(part, "section"),
+        x_rows,
+        grad_hidden,
+        gain_first,
+        produced,
+        produced_away,
+        sums_first + sums_second,
+    )
     smalls, scan_reduce = line_total(smalls, scan_reduce)
     blocks = plain_call(
         join_kernel,

time: 335 us -> 332 us (level)
    pallas_call x11 -> x10, Pallas kernels: 24.7 us -> 23.2 us  [plain_call(): pl.pallas_call(body, in_specs=[pl.BlockSpec(memory_space=pltpu.SMEM)] + [...]
where the time goes in v5:
time: 332 us; the launch traced here: 327 us
  Pallas kernels  166 us (50%)
  waiting for transfers between devices  58.3 us (18%)
  starting transfers between devices  51.7 us (16%)
  blocking collectives  15.9 us (5%)
  local copies, waits for them, and re-layouts  15.4 us (5%)
  between operations  14.9 us (4%)
  other arithmetic  5.32 us (2%)
    pallas_call x6, Pallas kernels, call(): pl.pallas_call(kernel, grid=(chunks,), in_specs=[spec for _, spec in inpu...  130 us
    pallas_call x10, Pallas kernels, plain_call(): pl.pallas_call(body, in_specs=[pl.BlockSpec(memory_space=pltpu.SMEM)] + [...  23.2 us
    ppermute x27, starting transfers between devices, swapped(): return lax.ppermute(block, axis, [(0, 1), (1, 0)])  23.1 us
    ppermute x11, waiting for transfers between devices, x_swapped(): return lax.ppermute(block, 'dp', [(i, i ^ 1) for i in range(ranks)])  21.4 us
    ppermute x27, waiting for transfers between devices, swapped(): return lax.ppermute(block, axis, [(0, 1), (1, 0)])  19.5 us
    all_gather x1, blocking collectives, line_gather(): lax.all_gather(block, 'dp', axis_index_groups=line_groups, axis=0, tiled=...  15.9 us
    ppermute x11, starting transfers between devices, x_swapped(): return lax.ppermute(block, 'dp', [(i, i ^ 1) for i in range(ranks)])  14.5 us
    ppermute x5, waiting for transfers between devices, send(): lax.ppermute(rows, 'dp', [(2 * a + start, 2 * b + start) for a, b in move...  12.5 us
  transfers between devices with their start and end apart: 51, of which 19 were waited for; matrix products, arithmetic and copies ran while one was open for 3% of the time, Pallas kernels for 36%

profile of v5, /device:TPU:0, one launch (start us, length us, event | category | flops | bytes accessed | tf_op | source)
XLA Modules:
  0.0 327.4 jit_solution(13008668065649913314)
XLA Ops:
  7.9 2.9 shard_map.291
  11.4 2.6 collective-permute-start.1
  14.7 1.9 shard_map.292
  16.6 1.6 collective-permute-start.2
  18.3 15.9 %all_gather.9.refs_2_.refs_4_ = bf16[384,640]{1,0:T(8,128)(2,1)S(1)} all-gather(bf16[96,640]{1,0:T(8,128)(2,1)} %get-tuple-element.177), channel_id=1, replica_groups={{0,4,8,12},{2,6,10,14},{1,5,9,13},{3,7,11,15},{16,20,24,28},{18,22,26,3..., dimensions={0}, use_global_device_ids=true | all-gather | bytes 614400 | tf_op jit(solution)/shard_map/all_gather | solution.py:1152
  34.8 1.5 collective-permute-start.4
  37.4 1.9 shard_map.293
  39.4 1.6 collective-permute-start.9
  41.0 2.1 shard_map.294
  43.1 5.7 %collective-permute-done.8.refs_4_ = bf16[96,768]{1,0:T(8,128)(2,1)} collective-permute-done((bf16[96,768]{1,0:T(8,128)(2,1)}, bf16[96,768]{1,0:T(8,128)(2,1)}, u32[]{:S(2)}, u32[]{:S(2)}) %collective-permute-start.8) | collective-permute-done | bytes 147488 | tf_op jit(solution)/shard_map/ppermute | solution.py:1146
  48.8 1.5 collective-permute-start.10
  51.1 1.5 collective-permute-start.7
  52.6 1.7 slice.44
  56.0 1.9 maximum_select_fusion.refs_0_.refs_1_.h_ref
  58.6 2.0 shard_map.295
  60.7 2.9 all-gather.3.cloned.1.call-done.refs_1_
  63.8 2.3 shard_map.297
  66.1 1.5 collective-permute-start.12
  70.2 16.7 %shard_map.296 = (f32[8,768]{1,0:T(8,128)}, bf16[1024,768]{1,0:T(8,128)(2,1)}, f32[1024,768]{1,0:T(8,128)}, f32[1024,768]{1,0:T(8,128)}, f32[1024,768]{1,0:T(8,1...) custom-call(s32[4]{0:T(128)} %pad_add_fusion.place_ref.refs_0_.refs_1_, ...), custom_call_target="tpu_custom_call" | custom-call | flops 2000000000 | bytes 500000 | tf_op jit(solution)/shard_map/pallas_call | solution.py:561
  88.4 1.5 collective-permute-start.13
  89.9 3.2 collective-permute-done.16.refs_6_.refs_15_
  93.1 1.5 collective-permute-start.18
  94.7 1.5 collective-permute-start.17
  96.2 4.7 %collective-permute-done.14.refs_4_.refs_15_ = bf16[192,768]{1,0:T(8,128)(2,1)S(1)} collective-permute-done((bf16[192,768]{1,0:T(8,128)(2,1)S(1)}, bf16[192,768]{1,0:T(8,128)(2,1)S(1)}, u32[]{:S(2)}, u32[]{:S(2)}) %collective-permute-start.14) | collective-permute-done | bytes 294944 | tf_op jit(solution)/shard_map/ppermute | solution.py:1146
  102.4 6.7 %shard_map.298 = (f32[1024,768]{1,0:T(8,128)}, bf16[1024,896]{1,0:T(8,128)(2,1)}) custom-call(s32[4]{0:T(128)} %pad_add_fusion.place_ref.refs_0_.refs_1_, bf16[1024,768]{1,0:T(8,128)(2,1)} %get-tuple-element.209.normed_ref.refs_8_.refs_0_, f32[1024,768]{1,0:T(8,128)} %get-tuple-element.210.y_ref.refs_10_.refs_17_, ...), custom_call_target="tpu_custom_call" | custom-call | flops 1000000000 | bytes 500000 | tf_op jit(solution)/shard_map/pallas_call | solution.py:561
  111.7 2.2 collective-permute-done.19.refs_3_.refs_2_
  115.2 23.2 %shard_map.299 = (bf16[1024,768]{1,0:T(8,128)(2,1)}, f32[8,768]{1,0:T(8,128)}, bf16[1024,768]{1,0:T(8,128)(2,1)}, f32[1024,768]{1,0:T(8,128)}, f32[1024,768]{1,0...) custom-call(s32[4]{0:T(128)} %pad_add_fusion.place_ref.refs_0_.refs_, ...), custom_call_target="tpu_custom_call" | custom-call | flops 3000000000 | bytes 500000 | tf_op jit(solution)/shard_map/pallas_call | solution.py:561
  138.9 4.1 %collective-permute-done.22.refs_6_ = f32[256,768]{1,0:T(8,128)S(1)} collective-permute-done((f32[256,768]{1,0:T(8,128)S(1)}, f32[256,768]{1,0:T(8,128)S(1)}, u32[]{:S(2)}, u32[]{:S(2)}) %collective-permute-start.22) | collective-permute-done | bytes 786464 | tf_op jit(solution)/shard_map/ppermute | solution.py:1102
  145.2 39.0 %shard_map.300 = (bf16[1024,768]{1,0:T(8,128)(2,1)}, f32[1024,768]{1,0:T(8,128)}, bf16[384,5632]{1,0:T(8,128)(2,1)}, f32[8,768]{1,0:T(8,128)}, bf16[1024,768]{1,...) custom-call(s32[4]{0:T(128)} %pad_add_fusion.place_ref.refs_0_.refs_1_, ...), custom_call_target="tpu_custom_call" | custom-call | flops 4000000000 | bytes 500000 | tf_op jit(solution)/shard_map/pallas_call | solution.py:561
  189.1 17.5 %shard_map.301 = (f32[1024,768]{1,0:T(8,128)}, bf16[1024,768]{1,0:T(8,128)(2,1)}, f32[1024,768]{1,0:T(8,128)}, bf16[384,768]{1,0:T(8,128)(2,1)}, bf16[384,768]{1...) custom-call(s32[4]{0:T(128)} %pad_add_fusion.place_ref.refs_0_.refs_1_, ...), custom_call_target="tpu_custom_call" | custom-call | flops 2000000000 | bytes 500000 | tf_op jit(solution)/shard_map/pallas_call | solution.py:561
  210.5 27.0 %shard_map.302 = (bf16[384,640]{1,0:T(8,128)(2,1)}, bf16[384,640]{1,0:T(8,128)(2,1)}, bf16[384,640]{1,0:T(8,128)(2,1)}, bf16[384,640]{1,0:T(8,128)(2,1)}, bf16[1...) custom-call(bf16[1024,768]{1,0:T(8,128)(2,1)} %get-tuple-element.209.normed_ref.refs_8_.refs_0_, ...), custom_call_target="tpu_custom_call" | custom-call | flops 3000000000 | bytes 500000 | tf_op jit(solution)/shard_map/pallas_call | solution.py:561
  237.7 1.5 collective-permute-start.34
  242.4 7.8 %shard_map.303 = (f32[2,512,768]{2,1,0:T(8,128)}, bf16[512,768]{1,0:T(8,128)(2,1)}, f32[32,768]{1,0:T(8,128)}, bf16[2,512,768]{2,1,0:T(8,128)(2,1)}) custom-call(s32[4]{0:T(128)} %pad_add_fusion.place_ref.refs_0_.refs_1_, bf16[1024,768]{1,0:T(8,128)(2,1)} %get-tuple-element.288.own_ref, bf16[1024,768]{1,0:T(8,128)(2,1)} %copy-done.8, ...), custom_call_target="tpu_custom_call" | custom-call | bytes 500000 | tf_op jit(solution)/shard_map/pallas_call | solution.py:786
  251.5 4.6 %collective-permute-start.29 = (f32[32,768]{1,0:T(8,128)}, f32[32,768]{1,0:T(8,128)S(1)}, u32[]{:S(2)}, u32[]{:S(2)}) collective-permute-start(f32[32,768]{1,0:T(8,128)} %get-tuple-element.300), channel_id=1, source_target_pairs={{0,4},{2,6},{4,8},{6,10},{8,12},{10,14},{1,5},{3,7},{5,9},{7,11},{... | collective-permute-start | bytes 294920 | tf_op jit(solution)/shard_map/ppermute | solution.py:1162
  256.1 6.5 %collective-permute-done.31 = f32[32,768]{1,0:T(8,128)S(1)} collective-permute-done((f32[32,768]{1,0:T(8,128)}, f32[32,768]{1,0:T(8,128)S(1)}, u32[]{:S(2)}, u32[]{:S(2)}) %collective-permute-start.31) | collective-permute-done | bytes 98336 | tf_op jit(solution)/shard_map/ppermute | solution.py:1162
  266.4 5.9 %collective-permute-done.32 = f32[32,768]{1,0:T(8,128)S(1)} collective-permute-done((f32[32,768]{1,0:T(8,128)S(1)}, f32[32,768]{1,0:T(8,128)S(1)}, u32[]{:S(2)}, u32[]{:S(2)}) %collective-permute-start.32) | collective-permute-done | bytes 98336 | tf_op jit(solution)/shard_map/ppermute | solution.py:1162
  272.4 3.7 %shard_map.304.refs_0_ = bf16[384,1408]{1,0:T(8,128)(2,1)} custom-call(s32[4]{0:T(128)} %pad_add_fusion.place_ref.refs_0_.refs_1_, bf16[96,5632]{1,0:T(8,128)(2,1)} %reduce-scatter.3.cloned.1.call-done.refs_0_.refs_1_, bf16[384,640]{1,0:T(8,128)(2,1)} %get-tuple-element.305.refs_1_, bf16[384,640]{1,0:T(8,128)(2,1)} %collective-permute-done.34.refs_2_, ...), custom_call_target="tpu_custom_call" | custom-call | bytes 500000 | tf_op jit(solution)/shard_map/pallas_call | solution.py:933
  277.3 3.6 %collective-permute-done.37.away_ref = f32[32,768]{1,0:T(8,128)S(1)} collective-permute-done((f32[32,768]{1,0:T(8,128)S(1)}, f32[32,768]{1,0:T(8,128)S(1)}, u32[]{:S(2)}, u32[]{:S(2)}) %collective-permute-start.37) | collective-permute-done | bytes 98336 | tf_op jit(solution)/shard_map/ppermute | solution.py:1102
  281.9 1.7 shard_map.306
  283.6 2.4 shard_map.308
  289.5 1.5 collective-permute-start.40
  291.0 10.9 %collective-permute-done.40 = f32[32,384]{1,0:T(8,128)S(1)} collective-permute-done((f32[32,384]{1,0:T(8,128)S(1)}, f32[32,384]{1,0:T(8,128)S(1)}, u32[]{:S(2)}, u32[]{:S(2)}) %collective-permute-start.40) | collective-permute-done | bytes 49184 | tf_op jit(solution)/shard_map/ppermute | solution.py:1146
  302.5 1.9 shard_map.307
  304.4 2.4 collective-permute-done.38.away_ref
  307.7 3.0 shard_map.305.refs_0_
  311.8 1.6 collective-permute-start.46
  315.1 2.2 collective-permute-done.45.refs_6_
  318.0 2.3 shard_map.309
  (184 shorter events, 47.2 us)
Async XLA Ops:
  7.2 56.4 %all-gather.3.cloned.1.call-start = ((), (), s32[]{:S(2)}) async-start(), calls=%async_computation.2 | async-start | bytes 1351680 | tf_op jit(solution)/shard_map/all_gather | solution.py:1152
  11.4 22.8 %collective-permute-start.1 = (bf16[256,768]{1,0:T(8,128)(2,1)S(1)}, bf16[256,768]{1,0:T(8,128)(2,1)}, u32[]{:S(2)}, u32[]{:S(2)}) collective-permute-start(bf16[256,768]{1,0:T(8,128)(2,1)S(1)} %dynamic-slice_bitcast_fusion.2), channel_id=1, source_target_pairs={{0,1},{1,0},{2,3},{3,2},{4,5},{5,4},{6,7},{7,6},{8,9},{9,8},{10,11... | collective-permute-start | bytes 1179656 | tf_op jit(solution)/shard_map/ppermute | solution.py:1102
  16.6 17.5 %collective-permute-start.2 = (bf16[32,384]{1,0:T(8,128)(2,1)}, bf16[32,384]{1,0:T(8,128)(2,1)S(1)}, u32[]{:S(2)}, u32[]{:S(2)}) collective-permute-start(bf16[32,384]{1,0:T(8,128)(2,1)} %get-tuple-element.178), channel_id=1, source_target_pairs={{0,1},{1,0},{2,3},{3,2},{4,5},{5,4},{6,7},{7,6},{8,9},{9,8},{10,11... | collective-permute-start | bytes 73736 | tf_op jit(solution)/shard_map/ppermute | solution.py:1102
  34.2 81.0 %all-gather.5.cloned.1.call-start = ((), (), s32[]{:S(2)}) async-start(), calls=%async_computation.3 | async-start | bytes 2949120 | tf_op jit(solution)/shard_map/all_gather | solution.py:1152
  34.2 16.1 %collective-permute-start.5 = (bf16[384,640]{1,0:T(8,128)(2,1)S(1)}, bf16[384,640]{1,0:T(8,128)(2,1)S(1)}, u32[]{:S(2)}, u32[]{:S(2)}) collective-permute-start(bf16[384,640]{1,0:T(8,128)(2,1)S(1)} %all_gather.9.refs_2_.refs_4_), channel_id=1, source_target_pairs={{0,1},{1,0},{2,3},{3,2},{4,5},{5,4},{6,7},{7,6},{8,9},{9,8},{10,11... | collective-permute-start | bytes 1474568 | tf_op jit(solution)/shard_map/ppermute | solution.py:1102
  34.8 17.9 %collective-permute-start.4 = (bf16[384,640]{1,0:T(8,128)(2,1)S(1)}, bf16[384,640]{1,0:T(8,128)(2,1)}, u32[]{:S(2)}, u32[]{:S(2)}) collective-permute-start(bf16[384,640]{1,0:T(8,128)(2,1)S(1)} %all_gather.9.refs_2_.refs_4_), channel_id=1, source_target_pairs={{0,2},{2,0},{4,6},{6,4},{8,10},{10,8},{12,14},{14,12},{1,3},{3,1},... | collective-permute-start | bytes 1474568 | tf_op jit(solution)/shard_map/ppermute | solution.py:1146
  36.3 18.5 %collective-permute-start.3 = (bf16[256,768]{1,0:T(8,128)(2,1)}, bf16[256,768]{1,0:T(8,128)(2,1)}, u32[]{:S(2)}, u32[]{:S(2)}) collective-permute-start(bf16[256,768]{1,0:T(8,128)(2,1)} %collective-permute-done.1), channel_id=1, source_target_pairs={{0,16},{16,0},{1,17},{17,1},{2,18},{18,2},{3,19},{19,3},{4,20},{20... | collective-permute-start | bytes 1179656 | tf_op jit(solution)/shard_map/ppermute | solution.py:1102
  36.3 12.5 %collective-permute-start.8 = (bf16[96,768]{1,0:T(8,128)(2,1)}, bf16[96,768]{1,0:T(8,128)(2,1)}, u32[]{:S(2)}, u32[]{:S(2)}) collective-permute-start(bf16[96,768]{1,0:T(8,128)(2,1)} %get-tuple-element.187.refs_3_), channel_id=1, source_target_pairs={{0,2},{2,0},{4,6},{6,4},{8,10},{10,8},{12,14},{14,12},{1,3},{3,1},... | collective-permute-start | bytes 442376 | tf_op jit(solution)/shard_map/ppermute | solution.py:1146
  39.4 18.5 %collective-permute-start.9 = (bf16[96,768]{1,0:T(8,128)(2,1)S(1)}, bf16[96,768]{1,0:T(8,128)(2,1)S(1)}, u32[]{:S(2)}, u32[]{:S(2)}) collective-permute-start(bf16[96,768]{1,0:T(8,128)(2,1)S(1)} %copy-done.31), channel_id=1, source_target_pairs={{0,1},{1,0},{2,3},{3,2},{4,5},{5,4},{6,7},{7,6},{8,9},{9,8},{10,11... | collective-permute-start | bytes 442376 | tf_op jit(solution)/shard_map/ppermute | solution.py:1102
  48.8 9.1 %collective-permute-start.10 = (bf16[96,768]{1,0:T(8,128)(2,1)}, bf16[96,768]{1,0:T(8,128)(2,1)S(1)}, u32[]{:S(2)}, u32[]{:S(2)}) collective-permute-start(bf16[96,768]{1,0:T(8,128)(2,1)} %collective-permute-done.8.refs_4_), channel_id=1, source_target_pairs={{0,1},{1,0},{2,3},{3,2},{4,5},{5,4},{6,7},{7,6},{8,9},{9,8},{10,11... | collective-permute-start | bytes 442376 | tf_op jit(solution)/shard_map/ppermute | solution.py:1102
  51.1 9.5 %collective-permute-start.7 = (bf16[192,640]{1,0:T(8,128)(2,1)}, bf16[192,640]{1,0:T(8,128)(2,1)S(1)}, u32[]{:S(2)}, u32[]{:S(2)}) collective-permute-start(bf16[192,640]{1,0:T(8,128)(2,1)} %slice.45), channel_id=1, source_target_pairs={{0,2},{2,0},{4,6},{6,4},{8,10},{10,8},{12,14},{14,12},{1,3},{3,1},... | collective-permute-start | bytes 737288 | tf_op jit(solution)/shard_map/ppermute | solution.py:1146
  54.3 6.4 %collective-permute-start.6 = (bf16[192,640]{1,0:T(8,128)(2,1)}, bf16[192,640]{1,0:T(8,128)(2,1)S(1)}, u32[]{:S(2)}, u32[]{:S(2)}) collective-permute-start(bf16[192,640]{1,0:T(8,128)(2,1)} %slice.44), channel_id=1, source_target_pairs={{0,1},{1,0},{2,3},{3,2},{4,5},{5,4},{6,7},{7,6},{8,9},{9,8},{10,11... | collective-permute-start | bytes 737288 | tf_op jit(solution)/shard_map/ppermute | solution.py:1102
  63.6 208.7 %reduce-scatter.3.cloned.1.call-start = ((), (), s32[]{:S(2)}) async-start(), calls=%async_computation.4 | async-start | bytes 5406720 | tf_op jit(solution)/shard_map/reduce_scatter | solution.py:1155
  66.1 20.7 %collective-permute-start.12 = (bf16[384,768]{1,0:T(8,128)(2,1)}, bf16[384,768]{1,0:T(8,128)(2,1)S(1)}, u32[]{:S(2)}, u32[]{:S(2)}) collective-permute-start(bf16[384,768]{1,0:T(8,128)(2,1)} %get-tuple-element.211.refs_0_.refs_11_), channel_id=1, source_target_pairs={{0,1},{1,0},{2,3},{3,2},{4,5},{5,4},{6,7},{7,6},{8,9},{9,8},{10,11... | collective-permute-start | bytes 1769480 | tf_op jit(solution)/shard_map/ppermute | solution.py:1102
  67.6 19.3 %collective-permute-start.11 = (bf16[384,768]{1,0:T(8,128)(2,1)}, bf16[384,768]{1,0:T(8,128)(2,1)S(1)}, u32[]{:S(2)}, u32[]{:S(2)}) collective-permute-start(bf16[384,768]{1,0:T(8,128)(2,1)} %get-tuple-element.211.refs_0_.refs_11_), channel_id=1, source_target_pairs={{0,2},{2,0},{4,6},{6,4},{8,10},{10,8},{12,14},{14,12},{1,3},{3,1},... | collective-permute-start | bytes 1769480 | tf_op jit(solution)/shard_map/ppermute | solution.py:1146
  69.1 24.0 %collective-permute-start.16 = (bf16[384,640]{1,0:T(8,128)(2,1)}, bf16[384,640]{1,0:T(8,128)(2,1)S(1)}, u32[]{:S(2)}, u32[]{:S(2)}) collective-permute-start(bf16[384,640]{1,0:T(8,128)(2,1)} %get-tuple-element.222.refs_4_.refs_13_), channel_id=1, source_target_pairs={{0,1},{1,0},{2,3},{3,2},{4,5},{5,4},{6,7},{7,6},{8,9},{9,8},{10,11... | collective-permute-start | bytes 1474568 | tf_op jit(solution)/shard_map/ppermute | solution.py:1102
  69.6 25.1 %collective-permute-start.15 = (bf16[384,640]{1,0:T(8,128)(2,1)}, bf16[384,640]{1,0:T(8,128)(2,1)S(1)}, u32[]{:S(2)}, u32[]{:S(2)}) collective-permute-start(bf16[384,640]{1,0:T(8,128)(2,1)} %get-tuple-element.222.refs_4_.refs_13_), channel_id=1, source_target_pairs={{0,2},{2,0},{4,6},{6,4},{8,10},{10,8},{12,14},{14,12},{1,3},{3,1},... | collective-permute-start | bytes 1474568 | tf_op jit(solution)/shard_map/ppermute | solution.py:1146
  87.0 14.0 %collective-permute-start.14 = (bf16[192,768]{1,0:T(8,128)(2,1)S(1)}, bf16[192,768]{1,0:T(8,128)(2,1)S(1)}, u32[]{:S(2)}, u32[]{:S(2)}) collective-permute-start(bf16[192,768]{1,0:T(8,128)(2,1)S(1)} %slice.36), channel_id=1, source_target_pairs={{0,2},{2,0},{4,6},{6,4},{8,10},{10,8},{12,14},{14,12},{1,3},{3,1},... | collective-permute-start | bytes 884744 | tf_op jit(solution)/shard_map/ppermute | solution.py:1146
  88.4 12.5 %collective-permute-start.13 = (bf16[192,768]{1,0:T(8,128)(2,1)S(1)}, bf16[192,768]{1,0:T(8,128)(2,1)S(1)}, u32[]{:S(2)}, u32[]{:S(2)}) collective-permute-start(bf16[192,768]{1,0:T(8,128)(2,1)S(1)} %slice.35), channel_id=1, source_target_pairs={{0,1},{1,0},{2,3},{3,2},{4,5},{5,4},{6,7},{7,6},{8,9},{9,8},{10,11... | collective-permute-start | bytes 884744 | tf_op jit(solution)/shard_map/ppermute | solution.py:1102
  93.1 15.9 %collective-permute-start.18 = (bf16[192,640]{1,0:T(8,128)(2,1)S(1)}, bf16[192,640]{1,0:T(8,128)(2,1)S(1)}, u32[]{:S(2)}, u32[]{:S(2)}) collective-permute-start(bf16[192,640]{1,0:T(8,128)(2,1)S(1)} %slice.47), channel_id=1, source_target_pairs={{0,2},{2,0},{4,6},{6,4},{8,10},{10,8},{12,14},{14,12},{1,3},{3,1},... | collective-permute-start | bytes 737288 | tf_op jit(solution)/shard_map/ppermute | solution.py:1146
  94.7 14.4 %collective-permute-start.17 = (bf16[192,640]{1,0:T(8,128)(2,1)S(1)}, bf16[192,640]{1,0:T(8,128)(2,1)S(1)}, u32[]{:S(2)}, u32[]{:S(2)}) collective-permute-start(bf16[192,640]{1,0:T(8,128)(2,1)S(1)} %slice.46), channel_id=1, source_target_pairs={{0,1},{1,0},{2,3},{3,2},{4,5},{5,4},{6,7},{7,6},{8,9},{9,8},{10,11... | collective-permute-start | bytes 737288 | tf_op jit(solution)/shard_map/ppermute | solution.py:1102
  109.9 4.0 %collective-permute-start.19 = (bf16[1024,896]{1,0:T(8,128)(2,1)}, bf16[1024,896]{1,0:T(8,128)(2,1)S(1)}, u32[]{:S(2)}, u32[]{:S(2)}) collective-permute-start(bf16[1024,896]{1,0:T(8,128)(2,1)} %get-tuple-element.220.refs_2_.refs_1_), channel_id=1, source_target_pairs={{0,16},{16,0},{1,17},{17,1},{2,18},{18,2},{3,19},{19,3},{4,20},{20... | collective-permute-start | bytes 5505032 | tf_op jit(solution)/shard_map/ppermute | solution.py:1102
  111.1 27.3 %collective-permute-start.20 = (f32[256,768]{1,0:T(8,128)S(1)}, f32[256,768]{1,0:T(8,128)S(1)}, u32[]{:S(2)}, u32[]{:S(2)}) collective-permute-start(f32[256,768]{1,0:T(8,128)S(1)} %dynamic-slice_bitcast_fusion), channel_id=1, source_target_pairs={{0,1},{1,0},{2,3},{3,2},{4,5},{5,4},{6,7},{7,6},{8,9},{9,8},{10,11... | collective-permute-start | bytes 2359304 | tf_op jit(solution)/shard_map/ppermute | solution.py:1102
  138.4 5.2 %collective-permute-start.21 = (bf16[1024,896]{1,0:T(8,128)(2,1)}, bf16[1024,896]{1,0:T(8,128)(2,1)S(1)}, u32[]{:S(2)}, u32[]{:S(2)}) collective-permute-start(bf16[1024,896]{1,0:T(8,128)(2,1)} %get-tuple-element.245.refs_2_), channel_id=1, source_target_pairs={{0,16},{16,0},{1,17},{17,1},{2,18},{18,2},{3,19},{19,3},{4,20},{20... | collective-permute-start | bytes 5505032 | tf_op jit(solution)/shard_map/ppermute | solution.py:1102
  138.5 4.5 %collective-permute-start.22 = (f32[256,768]{1,0:T(8,128)S(1)}, f32[256,768]{1,0:T(8,128)S(1)}, u32[]{:S(2)}, u32[]{:S(2)}) collective-permute-start(f32[256,768]{1,0:T(8,128)S(1)} %collective-permute-done.20.refs_5_), channel_id=1, source_target_pairs={{0,16},{16,0},{1,17},{17,1},{2,18},{18,2},{3,19},{19,3},{4,20},{20... | collective-permute-start | bytes 2359304 | tf_op jit(solution)/shard_map/ppermute | solution.py:1102
  184.2 126.5 %reduce-scatter.5.cloned.1.call-start = ((), (), s32[]{:S(2)}) async-start(), calls=%async_computation.5 | async-start | bytes 1351680 | tf_op jit(solution)/shard_map/reduce_scatter | solution.py:1155
  187.0 20.0 %collective-permute-start.24 = (bf16[512,768]{1,0:T(8,128)(2,1)}, bf16[512,768]{1,0:T(8,128)(2,1)S(1)}, u32[]{:S(2)}, u32[]{:S(2)}) collective-permute-start(bf16[512,768]{1,0:T(8,128)(2,1)} %constant_dynamic-slice_fusion), channel_id=1, source_target_pairs={{0,1},{1,0},{2,3},{3,2},{4,5},{5,4},{6,7},{7,6},{8,9},{9,8},{10,11... | collective-permute-start | bytes 2359304 | tf_op jit(solution)/shard_map/ppermute | solution.py:1102
  207.0 30.5 %collective-permute-start.25 = (bf16[384,768]{1,0:T(8,128)(2,1)}, bf16[384,768]{1,0:T(8,128)(2,1)S(1)}, u32[]{:S(2)}, u32[]{:S(2)}) collective-permute-start(bf16[384,768]{1,0:T(8,128)(2,1)} %get-tuple-element.285), channel_id=1, source_target_pairs={{0,2},{2,0},{4,6},{6,4},{8,10},{10,8},{12,14},{14,12},{1,3},{3,1},... | collective-permute-start | bytes 1769480 | tf_op jit(solution)/shard_map/ppermute | solution.py:1146
  208.5 29.1 %collective-permute-start.26 = (bf16[384,768]{1,0:T(8,128)(2,1)}, bf16[384,768]{1,0:T(8,128)(2,1)S(1)}, u32[]{:S(2)}, u32[]{:S(2)}) collective-permute-start(bf16[384,768]{1,0:T(8,128)(2,1)} %get-tuple-element.286), channel_id=1, source_target_pairs={{0,1},{1,0},{2,3},{3,2},{4,5},{5,4},{6,7},{7,6},{8,9},{9,8},{10,11... | collective-permute-start | bytes 1769480 | tf_op jit(solution)/shard_map/ppermute | solution.py:1102
  209.9 27.7 %collective-permute-start.27 = (bf16[384,768]{1,0:T(8,128)(2,1)}, bf16[384,768]{1,0:T(8,128)(2,1)S(1)}, u32[]{:S(2)}, u32[]{:S(2)}) collective-permute-start(bf16[384,768]{1,0:T(8,128)(2,1)} %get-tuple-element.287), channel_id=1, source_target_pairs={{0,3},{1,2},{2,1},{3,0},{4,7},{5,6},{6,5},{7,4},{8,11},{9,10},{10,... | collective-permute-start | bytes 1769480 | tf_op jit(solution)/shard_map/ppermute | solution.py:1194
  237.6 3.7 %collective-permute-start.28 = (bf16[1024,768]{1,0:T(8,128)(2,1)}, bf16[1024,768]{1,0:T(8,128)(2,1)S(1)}, u32[]{:S(2)}, u32[]{:S(2)}) collective-permute-start(bf16[1024,768]{1,0:T(8,128)(2,1)} %get-tuple-element.288.own_ref), channel_id=1, source_target_pairs={{0,16},{16,0},{1,17},{17,1},{2,18},{18,2},{3,19},{19,3},{4,20},{20... | collective-permute-start | bytes 4718600 | tf_op jit(solution)/shard_map/ppermute | solution.py:1102
  237.7 27.8 %collective-permute-start.34 = (bf16[384,640]{1,0:T(8,128)(2,1)}, bf16[384,640]{1,0:T(8,128)(2,1)}, u32[]{:S(2)}, u32[]{:S(2)}) collective-permute-start(bf16[384,640]{1,0:T(8,128)(2,1)} %get-tuple-element.302), channel_id=1, source_target_pairs={{0,2},{2,0},{4,6},{6,4},{8,10},{10,8},{12,14},{14,12},{1,3},{3,1},... | collective-permute-start | bytes 1474568 | tf_op jit(solution)/shard_map/ppermute | solution.py:1146
  239.2 27.2 %collective-permute-start.35 = (bf16[384,640]{1,0:T(8,128)(2,1)}, bf16[384,640]{1,0:T(8,128)(2,1)}, u32[]{:S(2)}, u32[]{:S(2)}) collective-permute-start(bf16[384,640]{1,0:T(8,128)(2,1)} %get-tuple-element.303), channel_id=1, source_target_pairs={{0,1},{1,0},{2,3},{3,2},{4,5},{5,4},{6,7},{7,6},{8,9},{9,8},{10,11... | collective-permute-start | bytes 1474568 | tf_op jit(solution)/shard_map/ppermute | solution.py:1102
  240.6 25.8 %collective-permute-start.36 = (bf16[384,640]{1,0:T(8,128)(2,1)}, bf16[384,640]{1,0:T(8,128)(2,1)}, u32[]{:S(2)}, u32[]{:S(2)}) collective-permute-start(bf16[384,640]{1,0:T(8,128)(2,1)} %get-tuple-element.304), channel_id=1, source_target_pairs={{0,3},{1,2},{2,1},{3,0},{4,7},{5,6},{6,5},{7,4},{8,11},{9,10},{10,... | collective-permute-start | bytes 1474568 | tf_op jit(solution)/shard_map/ppermute | solution.py:1194
  250.2 12.4 %collective-permute-start.31 = (f32[32,768]{1,0:T(8,128)}, f32[32,768]{1,0:T(8,128)S(1)}, u32[]{:S(2)}, u32[]{:S(2)}) collective-permute-start(f32[32,768]{1,0:T(8,128)} %get-tuple-element.300), channel_id=1, source_target_pairs={{4,0},{6,2},{8,4},{10,6},{12,8},{14,10},{5,1},{7,3},{9,5},{11,7},{... | collective-permute-start | bytes 294920 | tf_op jit(solution)/shard_map/ppermute | solution.py:1162
  251.5 11.1 %collective-permute-start.29 = (f32[32,768]{1,0:T(8,128)}, f32[32,768]{1,0:T(8,128)S(1)}, u32[]{:S(2)}, u32[]{:S(2)}) collective-permute-start(f32[32,768]{1,0:T(8,128)} %get-tuple-element.300), channel_id=1, source_target_pairs={{0,4},{2,6},{4,8},{6,10},{8,12},{10,14},{1,5},{3,7},{5,9},{7,11},{... | collective-permute-start | bytes 294920 | tf_op jit(solution)/shard_map/ppermute | solution.py:1162
  262.7 9.7 %collective-permute-start.33 = (f32[32,768]{1,0:T(8,128)S(1)}, f32[32,768]{1,0:T(8,128)S(1)}, u32[]{:S(2)}, u32[]{:S(2)}) collective-permute-start(f32[32,768]{1,0:T(8,128)S(1)} %broadcast_select_fusion.3), channel_id=1, source_target_pairs={{4,12},{6,14},{8,0},{10,2},{5,13},{7,15},{9,1},{11,3},{20,28},{22,... | collective-permute-start | bytes 294920 | tf_op jit(solution)/shard_map/ppermute | solution.py:1162
  264.1 8.2 %collective-permute-start.32 = (f32[32,768]{1,0:T(8,128)S(1)}, f32[32,768]{1,0:T(8,128)S(1)}, u32[]{:S(2)}, u32[]{:S(2)}) collective-permute-start(f32[32,768]{1,0:T(8,128)S(1)} %collective-permute-done.31), channel_id=1, source_target_pairs={{8,4},{10,6},{4,0},{6,2},{9,5},{11,7},{5,1},{7,3},{24,20},{26,22},... | collective-permute-start | bytes 294920 | tf_op jit(solution)/shard_map/ppermute | solution.py:1162
  265.4 6.9 %collective-permute-start.30 = (f32[32,768]{1,0:T(8,128)S(1)}, f32[32,768]{1,0:T(8,128)S(1)}, u32[]{:S(2)}, u32[]{:S(2)}) collective-permute-start(f32[32,768]{1,0:T(8,128)S(1)} %collective-permute-done.29), channel_id=1, source_target_pairs={{4,8},{6,10},{8,12},{10,14},{5,9},{7,11},{9,13},{11,15},{20,24},{2... | collective-permute-start | bytes 294920 | tf_op jit(solution)/shard_map/ppermute | solution.py:1162
  276.2 4.7 %collective-permute-start.37 = (f32[32,768]{1,0:T(8,128)S(1)}, f32[32,768]{1,0:T(8,128)S(1)}, u32[]{:S(2)}, u32[]{:S(2)}) collective-permute-start(f32[32,768]{1,0:T(8,128)S(1)} %add_add_fusion.own_ref), channel_id=1, source_target_pairs={{0,1},{1,0},{2,3},{3,2},{4,5},{5,4},{6,7},{7,6},{8,9},{9,8},{10,11... | collective-permute-start | bytes 294920 | tf_op jit(solution)/shard_map/ppermute | solution.py:1102
  280.9 26.0 %collective-permute-start.38 = (bf16[512,768]{1,0:T(8,128)(2,1)}, bf16[512,768]{1,0:T(8,128)(2,1)S(1)}, u32[]{:S(2)}, u32[]{:S(2)}) collective-permute-start(bf16[512,768]{1,0:T(8,128)(2,1)} %get-tuple-element.317), channel_id=1, source_target_pairs={{0,1},{1,0},{2,3},{3,2},{4,5},{5,4},{6,7},{7,6},{8,9},{9,8},{10,11... | collective-permute-start | bytes 2359304 | tf_op jit(solution)/shard_map/ppermute | solution.py:1102
  283.6 5.9 %collective-permute-start.39 = (f32[16,384]{1,0:T(8,128)}, f32[16,384]{1,0:T(8,128)S(1)}, u32[]{:S(2)}, u32[]{:S(2)}) collective-permute-start(f32[16,384]{1,0:T(8,128)} %get-tuple-element.322), channel_id=1, source_target_pairs={{0,16},{16,0},{1,17},{17,1},{2,18},{18,2},{3,19},{19,3},{4,20},{20... | collective-permute-start | bytes 73736 | tf_op jit(solution)/shard_map/ppermute | solution.py:1102
  285.9 24.8 %collective-permute-start.41 = (bf16[96,1408]{1,0:T(8,128)(2,1)}, bf16[96,1408]{1,0:T(8,128)(2,1)S(1)}, u32[]{:S(2)}, u32[]{:S(2)}) collective-permute-start(bf16[96,1408]{1,0:T(8,128)(2,1)} %get-tuple-element.327), channel_id=1, source_target_pairs={{0,2},{2,0},{4,6},{6,4},{8,10},{10,8},{12,14},{14,12},{1,3},{3,1},... | collective-permute-start | bytes 811016 | tf_op jit(solution)/shard_map/ppermute | solution.py:1146
  287.4 23.4 %collective-permute-start.42 = (bf16[96,1408]{1,0:T(8,128)(2,1)}, bf16[96,1408]{1,0:T(8,128)(2,1)S(1)}, u32[]{:S(2)}, u32[]{:S(2)}) collective-permute-start(bf16[96,1408]{1,0:T(8,128)(2,1)} %get-tuple-element.328), channel_id=1, source_target_pairs={{0,1},{1,0},{2,3},{3,2},{4,5},{5,4},{6,7},{7,6},{8,9},{9,8},{10,11... | collective-permute-start | bytes 811016 | tf_op jit(solution)/shard_map/ppermute | solution.py:1102
  288.1 22.7 %collective-permute-start.43 = (bf16[96,1408]{1,0:T(8,128)(2,1)}, bf16[96,1408]{1,0:T(8,128)(2,1)S(1)}, u32[]{:S(2)}, u32[]{:S(2)}) collective-permute-start(bf16[96,1408]{1,0:T(8,128)(2,1)} %get-tuple-element.329), channel_id=1, source_target_pairs={{0,3},{1,2},{2,1},{3,0},{4,7},{5,6},{6,5},{7,4},{8,11},{9,10},{10,... | collective-permute-start | bytes 811016 | tf_op jit(solution)/shard_map/ppermute | solution.py:1194
  289.5 12.4 %collective-permute-start.40 = (f32[32,384]{1,0:T(8,128)S(1)}, f32[32,384]{1,0:T(8,128)S(1)}, u32[]{:S(2)}, u32[]{:S(2)}) collective-permute-start(f32[32,384]{1,0:T(8,128)S(1)} %constant_dynamic-update-slice_fusion), channel_id=1, source_target_pairs={{0,2},{2,0},{4,6},{6,4},{8,10},{10,8},{12,14},{14,12},{1,3},{3,1},... | collective-permute-start | bytes 147464 | tf_op jit(solution)/shard_map/ppermute | solution.py:1146
  311.0 6.3 %collective-permute-start.44 = (bf16[96,1408]{1,0:T(8,128)(2,1)S(1)}, bf16[96,1408]{1,0:T(8,128)(2,1)S(1)}, u32[]{:S(2)}, u32[]{:S(2)}) collective-permute-start(bf16[96,1408]{1,0:T(8,128)(2,1)S(1)} %get-tuple-element.337), channel_id=1, source_target_pairs={{0,16},{16,0},{1,17},{17,1},{2,18},{18,2},{3,19},{19,3},{4,20},{20... | collective-permute-start | bytes 811016 | tf_op jit(solution)/shard_map/ppermute | solution.py:1102
  313.5 3.8 %collective-permute-start.45 = (bf16[96,128]{1,0:T(8,128)(2,1)S(1)}, bf16[96,128]{1,0:T(8,128)(2,1)S(1)}, u32[]{:S(2)}, u32[]{:S(2)}) collective-permute-start(bf16[96,128]{1,0:T(8,128)(2,1)S(1)} %get-tuple-element.342), channel_id=1, source_target_pairs={{0,1},{1,0},{2,3},{3,2},{4,5},{5,4},{6,7},{7,6},{8,9},{9,8},{10,11... | collective-permute-start | bytes 73736 | tf_op jit(solution)/shard_map/ppermute | solution.py:1102
  (45 other events, 373.1 us)
Sparse Core Ops, SparseCore 0:
  34.3 29.2 all-gather.2
  65.2 49.9 all-gather.4
  184.3 79.7 reduce-scatter.2
  276.2 29.6 reduce-scatter.4
